TPU v7x, 32 devices: a whole 2x2x4 slice. The times are simulated.
32 devices in a mesh: ctx: 16 (over z, y, x), tp: 2 (over core).
Axes of the slice: x: 2, y: 2, z: 4, core: 2. Of those that a mesh axis runs over, the one named last changes fastest.
Arguments:
- queries: bfloat16 [4096, 4096], P('ctx', 'tp'), may hold values from -6 to 6
- keys: bfloat16 [4096, 2048], P('ctx', 'tp'), may hold values from -6 to 6
- values: bfloat16 [4096, 2048], P('ctx', 'tp'), may hold values from -6 to 6
- out_weight: bfloat16 [4096, 2688], P('tp'), may hold values from -0.09375 to 0.09375
- out_grad: bfloat16 [4096, 2688], P('ctx'), may hold values from -6 to 6
- block_doc: int32 [16], replicated, may hold values from 0 to 3, never falling along the last dimension, each value on 1 to 8 neighbouring positions
Outputs:
- attn_output: bfloat16 [4096, 2688], P('ctx', 'tp')
- query_grad: bfloat16 [4096, 4096], P('ctx', 'tp')
- key_grad: bfloat16 [4096, 2048], P('ctx', 'tp')
- value_grad: bfloat16 [4096, 2048], P('ctx', 'tp')
- out_weight_grad: float32 [4096, 2688], P('tp', 'ctx')
Inputs may be any that keep to these rules, and one draw needn't show every extreme that they name: block_doc never falls; each document covers 1 to 8 whole blocks, one exactly 8.
All inputs are finite; a program needn't handle non-finite values.
Results may differ from a plain program's by a relative error of at most 0.017.
Values may be sent and summed in bfloat16 or wider, within the bound.
No kernel may reach another device: no remote copies, remote signals or barrier semaphores. Data moves between devices by JAX's collectives and lax.ppermute only.
A program may use at most 128 MiB of HBM per device.

v0:
```python
import jax
import jax.numpy as jnp
from jax import lax
from jax.sharding import PartitionSpec as P

HEAD = 128
WINDOW = 1024


query_scale = 168.0 ** (-0.5)


def shifted(shard, axis, by):
    size = lax.axis_size(axis)
    pairs = [(i, i + by) for i in range(size) if 0 <= i + by < size]
    return lax.ppermute(shard, axis, pairs)


def local(queries, keys, values, out_weight, out_grad, block_doc):
    tok_rows = queries.shape[0]
    head_size = HEAD
    kv_count = keys.shape[1] // head_size
    group_size = queries.shape[1] // keys.shape[1]
    key_width = keys.shape[1]
    span_blocks = WINDOW // tok_rows
    reach_blocks = min(span_blocks, lax.axis_size("ctx") - 1)
    own_block = lax.axis_index("ctx")
    paired = jnp.stack([keys, values])
    by_distance = jnp.stack(
        [paired] + [shifted(paired, "ctx", distance) for distance in range(1, reach_blocks + 1)]
    )
    ordered = by_distance[::-1]
    missing = span_blocks - reach_blocks
    window_rows = (span_blocks + 1) * tok_rows
    key_window = ordered[:, 0].reshape(window_rows, kv_count, head_size)
    value_window = ordered[:, 1].reshape(window_rows, kv_count, head_size)
    doc_padded = jnp.concatenate([jnp.full((span_blocks,), -1, jnp.int32), block_doc])
    window_docs = lax.dynamic_slice_in_dim(doc_padded, own_block, span_blocks + 1, 0)
    key_docs = jnp.repeat(window_docs, tok_rows)
    own_doc = lax.dynamic_slice_in_dim(block_doc, own_block, 1, 0)
    rel_key = jnp.arange(window_rows, dtype=jnp.int32)
    rel_query = jnp.arange(tok_rows, dtype=jnp.int32) + span_blocks * tok_rows
    visible = (rel_key[None, :] <= rel_query[:, None]) & (
        rel_key[None, :] > rel_query[:, None] - WINDOW
    )
    visible = visible & (key_docs[None, :] == own_doc[0])
    query_heads = queries.reshape(tok_rows, kv_count, group_size, head_size)
    scores = (
        jnp.einsum("tkgd,skd->kgts", query_heads, key_window, preferred_element_type=jnp.float32)
        * query_scale
    )
    scores = jnp.where(visible[None, None], scores, -jnp.inf)
    top = jnp.max(scores, axis=-1, keepdims=True)
    expo = jnp.exp(scores - top)
    probs = expo / jnp.sum(expo, axis=-1, keepdims=True)
    probs_low = probs.astype(jnp.bfloat16)
    attn_heads = jnp.einsum(
        "kgts,skd->tkgd", probs_low, value_window, preferred_element_type=jnp.float32
    ).astype(jnp.bfloat16)
    attn = attn_heads.reshape(tok_rows, queries.shape[1])
    output_terms = jnp.dot(attn, out_weight, preferred_element_type=jnp.float32)
    attn_output = lax.psum_scatter(output_terms, "tp", scatter_dimension=1, tiled=True).astype(
        jnp.bfloat16
    )
    weight_terms = jnp.einsum("tr,tc->rc", attn, out_grad, preferred_element_type=jnp.float32)
    out_weight_grad = lax.psum_scatter(weight_terms, "ctx", scatter_dimension=1, tiled=True)
    d_attn = jnp.einsum(
        "te,re->tr", out_grad, out_weight, preferred_element_type=jnp.float32
    ).astype(jnp.bfloat16)
    d_attn_heads = d_attn.reshape(tok_rows, kv_count, group_size, head_size)
    d_probs = jnp.einsum(
        "tkgd,skd->kgts", d_attn_heads, value_window, preferred_element_type=jnp.float32
    )
    delta = jnp.einsum(
        "tkgd,tkgd->kgt", attn_heads, d_attn_heads, preferred_element_type=jnp.float32
    )
    d_scores = (probs * (d_probs - delta[..., None])).astype(jnp.bfloat16)
    query_grad = (
        jnp.einsum("kgts,skd->tkgd", d_scores, key_window, preferred_element_type=jnp.float32)
        * query_scale
    ).astype(jnp.bfloat16)
    query_grad = query_grad.reshape(tok_rows, queries.shape[1])
    key_part = (
        jnp.einsum("kgts,tkgd->skd", d_scores, query_heads, preferred_element_type=jnp.float32)
        * query_scale
    )
    value_part = jnp.einsum(
        "kgts,tkgd->skd", probs_low, d_attn_heads, preferred_element_type=jnp.float32
    )
    by_position = jnp.stack(
        [
            key_part.reshape(span_blocks + 1, tok_rows, key_width),
            value_part.reshape(span_blocks + 1, tok_rows, key_width),
        ],
        axis=1,
    )
    terms_near = by_position[::-1]
    total = terms_near[0] + sum(
        [shifted(terms_near[distance], "ctx", -distance) for distance in range(1, reach_blocks + 1)]
    )
    key_grad = total[0].astype(jnp.bfloat16)
    value_grad = total[1].astype(jnp.bfloat16)
    return (attn_output, query_grad, key_grad, value_grad, out_weight_grad)


def solution(mesh):
    placed = (P("ctx", "tp"), P("ctx", "tp"), P("ctx", "tp"), P("tp", None), P("ctx", None), P())
    return jax.shard_map(
        local,
        mesh=mesh,
        in_specs=placed,
        out_specs=(P("ctx", "tp"), P("ctx", "tp"), P("ctx", "tp"), P("ctx", "tp"), P("tp", "ctx")),
        check_vma=False,
    )
```

profile of v0, /device:TPU:0, one launch (start us, length us, event | category | flops | bytes accessed | tf_op | source)
XLA Modules:
  0.0 665.5 jit_solution(11684412894010935408)
XLA Ops:
  8.6 5.8 collective-permute-start
  14.5 4.4 collective-permute-start.2
  18.8 4.4 collective-permute-start.1
  33.0 4.0 collective-permute-done
  38.3 21.0 %collective-permute-done.1 = bf16[2,256,1024]{2,1,0:T(8,128)(2,1)} collective-permute-done((bf16[2,256,1024]{2,1,0:T(8,128)(2,1)S(1)}, bf16[2,256,1024]{2,1,0:T(8,128)(2,1)}, u32[]{:S(2)}, u32[]{:S(2)}) %collective-permute-start.1) | collective-permute-done | bytes 1048608 | tf_op jit(solution)/shard_map/ppermute | solution.py:16
  66.1 3.6 slice.41
  69.7 3.8 copy.70
  73.5 3.7 slice.43
  77.2 3.9 copy.71
  81.2 4.7 copy.53
  85.9 12.4 %exponential_reduce_fusion = (f32[8,2,256]{2,1,0:T(2,128)S(1)}, f32[8,2,256,1280]{2,3,1,0:T(8,128)}) fusion(bf16[1280,8,128,1]{0,2,3,1:T(8,128)(2,1)} %copy.53, pred[256,1280]{0,1:T(8,128)(4,1)S(1)} %copy-done.9, bf16[256,8,2,128]{3,2,1,0:T(2,128)(2,1)S(1)} %reshape.99), kind=kOutput, calls=%fused_computation.7 | convolution fusion | flops 1363150080 | bytes 24985600 | tf_op jit(solution)/shard_map/sub | solution.py:54
  98.3 11.6 %fusion.4 = bf16[8,2,256,1280]{2,3,1,0:T(8,128)(2,1)S(1)} fusion(f32[8,2,256]{2,1,0:T(2,128)S(1)} %get-tuple-element.23, f32[8,2,256,1280]{2,3,1,0:T(8,128)} %get-tuple-element.24), kind=kLoop, calls=%fused_computation.8 | loop fusion | flops 10485760 | bytes 31473664 | tf_op jit(solution)/shard_map/convert_element_type | solution.py:56
  115.0 6.1 fusion.28
  121.2 9.3 %fusion.29 = f32[2048,2688]{0,1:T(8,128)} fusion(bf16[256,2048]{0,1:T(8,128)(2,1)S(1)} %bitcast.112, bf16[256,2688]{1,0:T(8,128)(2,1)S(1)} %copy-done), kind=kOutput, calls=%fused_computation.51 | convolution fusion | flops 2818572288 | bytes 24444928 | tf_op jit(solution)/shard_map/tr,tc->rc/dot_general | solution.py:65
  130.5 7.3 %convolution_convert_fusion = bf16[256,2048]{1,0:T(8,128)(2,1)S(1)} fusion(bf16[256,2688]{1,0:T(8,128)(2,1)S(1)} %copy-done, bf16[2048,2688]{1,0:T(8,128)(2,1)} %param.9), kind=kOutput, calls=%fused_computation.12 | convolution fusion | flops 2819096576 | bytes 13434880 | tf_op jit(solution)/shard_map/te,re->tr/dot_general | solution.py:67
  139.7 10.1 %convolution_bitcast_fusion = f32[1280,8,128]{0,2,1:T(8,128)} fusion(bf16[256,8,2,128]{0,3,2,1:T(8,128)(2,1)S(1)} %copy.34, bf16[8,2,256,1280]{2,3,1,0:T(8,128)(2,1)} %copy-done.2), kind=kOutput, calls=%fused_computation.11 | convolution fusion | flops 1342177280 | bytes 16777216 | tf_op jit(solution)/shard_map/kgts,tkgd->skd/dot_general | solution.py:87
  149.8 6.2 copy.36
  156.1 6.8 %stack_reshape.7 = f32[5,1,256,1024]{3,2,0,1:T(8,128)} reshape(f32[1280,8,128]{2,1,0:T(8,128)} %copy.36) | data formatting | bytes 10485760 | tf_op jit(solution)/shard_map/stack;reshape | solution.py:90
  162.9 3.2 copy.51
  166.1 3.2 multiply_reduce_fusion
  170.8 14.1 %fusion.3 = bf16[8,2,256,1280]{2,3,1,0:T(8,128)(2,1)} fusion(bf16[256,8,2,128]{0,3,2,1:T(8,128)(2,1)} %copy-done.6, f32[8,2,256]{2,1,0:T(2,128)S(1)} %copy.52, f32[8,2,256]{2,1,0:T(2,128)S(1)} %get-tuple-element.23, f32[8,2,256,1280]{2,3,1,0:T(8,128)} %get-tuple-element.24, bf16[1280,8,128,1]{2,1,0,3:T(8,128)(2,1)} %bitcast.106), kind=kOutput, calls=%fused_computation.4 | convolution fusion | flops 1363148800 | bytes 35160064 | tf_op jit(solution)/shard_map/tkgd,skd->kgts/dot_general | solution.py:71
  184.9 6.9 %fusion.5 = f32[1280,8,128]{2,0,1:T(8,128)S(1)} fusion(bf16[8,2,256,1280]{2,3,1,0:T(8,128)(2,1)} %fusion.3, bf16[256,8,2,128]{3,2,1,0:T(2,128)(2,1)S(1)} %copy-done.8), kind=kOutput, calls=%fused_computation.10 | convolution fusion | flops 1343488000 | bytes 16777216 | tf_op jit(solution)/shard_map/kgts,tkgd->skd/dot_general | solution.py:84
  191.8 8.4 %copy.33 = f32[1280,8,128]{2,1,0:T(8,128)} copy(f32[1280,8,128]{2,0,1:T(8,128)S(1)} %fusion.5) | data formatting | bytes 10485760 | tf_op jit(solution)/shard_map/mul | solution.py:84
  200.2 6.8 %stack_reshape.6 = f32[5,1,256,1024]{3,2,0,1:T(8,128)} reshape(f32[1280,8,128]{2,1,0:T(8,128)} %copy.33) | data formatting | bytes 10485760 | tf_op jit(solution)/shard_map/stack;reshape | solution.py:90
  207.0 3.2 constant_dynamic-update-slice_fusion.1
  211.6 3.7 slice_bitcast_fusion.2
  215.2 3.7 copy-done.3
  224.4 5.9 multiply_convert_fusion
  231.7 78.4 %collective-permute-done.5 = f32[2,256,1024]{2,1,0:T(8,128)} collective-permute-done((f32[2,256,1024]{2,1,0:T(8,128)}, f32[2,256,1024]{2,1,0:T(8,128)}, u32[]{:S(2)}, u32[]{:S(2)}) %collective-permute-start.5) | collective-permute-done | bytes 2097184 | tf_op jit(solution)/shard_map/ppermute | solution.py:16
  310.1 136.8 %collective-permute-done.7 = f32[2,256,1024]{2,1,0:T(8,128)} collective-permute-done((f32[2,256,1024]{2,1,0:T(8,128)}, f32[2,256,1024]{2,1,0:T(8,128)}, u32[]{:S(2)}, u32[]{:S(2)}) %collective-permute-start.7) | collective-permute-done | bytes 2097184 | tf_op jit(solution)/shard_map/ppermute | solution.py:16
  446.9 5.1 fusion.10
  455.2 203.0 %reduce-scatter.5.cloned.1.call-done = f32[2048,168]{0,1:T(8,128)} async-done(((f32[2048,2688]{0,1:T(8,128)}), f32[2048,168]{0,1:T(8,128)}) %reduce-scatter.5.cloned.1.call-update) | async-done | bytes 1376272 | tf_op jit(solution)/shard_map/reduce_scatter | solution.py:66
  (67 shorter events, 39.2 us)
Async XLA Ops:
  7.2 114.0 %copy-start = (bf16[256,2688]{1,0:T(8,128)(2,1)S(1)}, bf16[256,2688]{1,0:T(8,128)(2,1)}, u32[]{:S(2)}) copy-start(bf16[256,2688]{1,0:T(8,128)(2,1)} %param.10) | copy-start | bytes 4128772
  7.2 445.8 %reduce-scatter.3.cloned.1.call-start = ((), (), s32[]{:S(2)}) async-start(), calls=%async_computation.2 | async-start | bytes 4128768 | tf_op jit(solution)/shard_map/reduce_scatter | solution.py:62
  8.6 28.4 %collective-permute-start = (bf16[2,256,1024]{2,1,0:T(8,128)(2,1)S(1)}, bf16[2,256,1024]{2,1,0:T(8,128)(2,1)}, u32[]{:S(2)}, u32[]{:S(2)}) collective-permute-start(bf16[2,256,1024]{2,1,0:T(8,128)(2,1)S(1)} %pad_maximum_fusion), channel_id=1, source_target_pairs={{0,2},{2,4},{4,6},{6,8},{8,10},{10,12},{12,14},{14,16},{16,18},{18... | collective-permute-start | bytes 3145736 | tf_op jit(solution)/shard_map/ppermute | solution.py:16
  14.5 46.1 %collective-permute-start.2 = (bf16[2,256,1024]{2,1,0:T(8,128)(2,1)S(1)}, bf16[2,256,1024]{2,1,0:T(8,128)(2,1)}, u32[]{:S(2)}, u32[]{:S(2)}) collective-permute-start(bf16[2,256,1024]{2,1,0:T(8,128)(2,1)S(1)} %pad_maximum_fusion), channel_id=1, source_target_pairs={{0,6},{2,8},{4,10},{6,12},{8,14},{10,16},{12,18},{14,20},{16,22},{... | collective-permute-start | bytes 3145736 | tf_op jit(solution)/shard_map/ppermute | solution.py:16
  18.8 40.4 %collective-permute-start.1 = (bf16[2,256,1024]{2,1,0:T(8,128)(2,1)S(1)}, bf16[2,256,1024]{2,1,0:T(8,128)(2,1)}, u32[]{:S(2)}, u32[]{:S(2)}) collective-permute-start(bf16[2,256,1024]{2,1,0:T(8,128)(2,1)S(1)} %pad_maximum_fusion), channel_id=1, source_target_pairs={{0,4},{2,6},{4,8},{6,10},{8,12},{10,14},{12,16},{14,18},{16,20},{1... | collective-permute-start | bytes 3145736 | tf_op jit(solution)/shard_map/ppermute | solution.py:16
  23.2 38.7 %collective-permute-start.3 = (bf16[2,256,1024]{2,1,0:T(8,128)(2,1)S(1)}, bf16[2,256,1024]{2,1,0:T(8,128)(2,1)}, u32[]{:S(2)}, u32[]{:S(2)}) collective-permute-start(bf16[2,256,1024]{2,1,0:T(8,128)(2,1)S(1)} %pad_maximum_fusion), channel_id=1, source_target_pairs={{0,8},{2,10},{4,12},{6,14},{8,16},{10,18},{12,20},{14,22},{16,24},... | collective-permute-start | bytes 3145736 | tf_op jit(solution)/shard_map/ppermute | solution.py:16
  31.3 54.6 %copy-start.7 = (bf16[256,8,2,128]{3,2,1,0:T(2,128)(2,1)}, bf16[256,8,2,128]{3,2,1,0:T(2,128)(2,1)S(1)}, u32[]{:S(2)}) copy-start(bf16[256,8,2,128]{3,2,1,0:T(2,128)(2,1)S(1)} %reshape.99) | copy-start | bytes 3145732
  77.2 8.7 %copy-start.9 = (pred[256,1280]{0,1:T(8,128)(4,1)S(1)}, pred[256,1280]{0,1:T(8,128)(4,1)}, u32[]{:S(2)}) copy-start(pred[256,1280]{0,1:T(8,128)(4,1)} %fusion.15) | copy-start | bytes 983044
  98.3 11.6 %copy-start.5 = (bf16[160,8,8,128]{3,2,1,0:T(8,128)(2,1)S(1)}, bf16[160,8,8,128]{3,2,1,0:T(8,128)(2,1)}, u32[]{:S(2)}) copy-start(bf16[160,8,8,128]{3,2,1,0:T(8,128)(2,1)} %copy.70) | copy-start | bytes 7864324
  98.3 16.7 %slice-start.2 = ((s8[11010048]{0:T(1024)(128)(4,1)}), s8[4194304]{0:T(1024)(128)(4,1)S(1)}, s32[]{:S(2)}) async-start(s8[11010048]{0:T(1024)(128)(4,1)} %bitcast.118), calls=%async_computation.6 | async-start | bytes 8388608
  98.3 16.7 %slice-start.3 = ((s8[11010048]{0:T(1024)(128)(4,1)}), s8[4194304]{0:T(1024)(128)(4,1)S(1)}, s32[]{:S(2)}) async-start(s8[11010048]{0:T(1024)(128)(4,1)} %bitcast.118), calls=%async_computation.7 | async-start | bytes 8388608
  109.9 5.1 copy-start.2
  109.9 5.1 slice-start.4
  121.1 537.1 %reduce-scatter.5.cloned.1.call-start = ((), (), s32[]{:S(2)}) async-start(), calls=%async_computation.3 | async-start | bytes 23396352 | tf_op jit(solution)/shard_map/reduce_scatter | solution.py:66
  139.7 10.2 %copy-start.6 = (bf16[256,8,2,128]{0,3,2,1:T(8,128)(2,1)}, bf16[256,8,2,128]{0,3,2,1:T(8,128)(2,1)S(1)}, u32[]{:S(2)}) copy-start(bf16[256,8,2,128]{0,3,2,1:T(8,128)(2,1)S(1)} %copy.34) | copy-start | bytes 3145732
  170.8 14.1 %copy-start.8 = (bf16[256,8,2,128]{3,2,1,0:T(2,128)(2,1)S(1)}, bf16[256,8,2,128]{3,2,1,0:T(2,128)(2,1)}, u32[]{:S(2)}) copy-start(bf16[256,8,2,128]{3,2,1,0:T(2,128)(2,1)} %copy-done.7) | copy-start | bytes 3145732
  200.2 10.1 %slice-start = ((s8[5242880]{0:T(1024)(128)(4,1)}), s8[1048576]{0:T(1024)(128)(4,1)S(1)}, s32[]{:S(2)}) async-start(s8[5242880]{0:T(1024)(128)(4,1)} %bitcast.104), calls=%async_computation.4 | async-start | bytes 2097152
  207.0 3.9 slice-start.1
  211.5 7.3 %copy-start.3 = (f32[5,2,256,1024]{3,2,0,1:T(8,128)}, f32[5,2,256,1024]{3,2,0,1:T(8,128)S(1)}, u32[]{:S(2)}) copy-start(f32[5,2,256,1024]{3,2,0,1:T(8,128)S(1)} %constant_dynamic-update-slice_fusion) | copy-start | bytes 31457284
  211.6 12.8 %copy-start.4 = (bf16[1280,8,128,1]{0,2,3,1:T(8,128)(2,1)S(1)}, bf16[1280,8,128,1]{0,2,3,1:T(8,128)(2,1)}, u32[]{:S(2)}) copy-start(bf16[1280,8,128,1]{0,2,3,1:T(8,128)(2,1)} %copy.53) | copy-start | bytes 7864324
  218.9 91.2 %collective-permute-start.5 = (f32[2,256,1024]{2,1,0:T(8,128)}, f32[2,256,1024]{2,1,0:T(8,128)}, u32[]{:S(2)}, u32[]{:S(2)}) collective-permute-start(f32[2,256,1024]{2,1,0:T(8,128)} %get-tuple-element.15), channel_id=1, source_target_pairs={{4,0},{6,2},{8,4},{10,6},{12,8},{14,10},{16,12},{18,14},{20,16},{2... | collective-permute-start | bytes 6291464 | tf_op jit(solution)/shard_map/ppermute | solution.py:16
  220.2 90.0 %collective-permute-start.4 = (f32[2,256,1024]{2,1,0:T(8,128)}, f32[2,256,1024]{2,1,0:T(8,128)}, u32[]{:S(2)}, u32[]{:S(2)}) collective-permute-start(f32[2,256,1024]{2,1,0:T(8,128)} %get-tuple-element.16), channel_id=1, source_target_pairs={{2,0},{4,2},{6,4},{8,6},{10,8},{12,10},{14,12},{16,14},{18,16},{20... | collective-permute-start | bytes 6291464 | tf_op jit(solution)/shard_map/ppermute | solution.py:16
  221.5 225.4 %collective-permute-start.7 = (f32[2,256,1024]{2,1,0:T(8,128)}, f32[2,256,1024]{2,1,0:T(8,128)}, u32[]{:S(2)}, u32[]{:S(2)}) collective-permute-start(f32[2,256,1024]{2,1,0:T(8,128)} %get-tuple-element.17), channel_id=1, source_target_pairs={{8,0},{10,2},{12,4},{14,6},{16,8},{18,10},{20,12},{22,14},{24,16},... | collective-permute-start | bytes 6291464 | tf_op jit(solution)/shard_map/ppermute | solution.py:16
  222.8 224.1 %collective-permute-start.6 = (f32[2,256,1024]{2,1,0:T(8,128)}, f32[2,256,1024]{2,1,0:T(8,128)}, u32[]{:S(2)}, u32[]{:S(2)}) collective-permute-start(f32[2,256,1024]{2,1,0:T(8,128)} %get-tuple-element.18), channel_id=1, source_target_pairs={{6,0},{8,2},{10,4},{12,6},{14,8},{16,10},{18,12},{20,14},{22,16},{... | collective-permute-start | bytes 6291464 | tf_op jit(solution)/shard_map/ppermute | solution.py:16
  230.2 428.0 %copy-start.1 = (bf16[256,2688]{1,0:T(8,128)(2,1)S(1)}, bf16[256,2688]{1,0:T(8,128)(2,1)}, u32[]{:S(2)}) copy-start(bf16[256,2688]{1,0:T(8,128)(2,1)} %param.10) | copy-start | bytes 4128772
Sparse Core Ops, SparseCore 0:
  121.2 53.9 reduce-scatter.2
  182.6 475.5 reduce-scatter.4
where the time goes:
time: 674 us; the launch traced here: 666 us
  waiting for transfers between devices  443 us (66%)
  local copies, waits for them, and re-layouts  82.1 us (12%)
  matrix products  75.1 us (11%)
  other arithmetic  27.6 us (4%)
  starting transfers between devices  22.7 us (3%)
  between operations  14.8 us (2%)
    ppermute x8, waiting for transfers between devices, shifted(): return lax.ppermute(shard, axis, pairs)  240 us
    reduce_scatter x1, waiting for transfers between devices, local(): lax.psum_scatter(weight_terms, 'ctx', scatter_dimension=1, tiled=True)  203 us
    unnamed x38, local copies, waits for them, and re-layouts  25.8 us
    ppermute x8, starting transfers between devices, shifted(): return lax.ppermute(shard, axis, pairs)  22.6 us
    another operation x3, local copies, waits for them, and re-layouts, local(): jnp.stack([key_part.reshape(span_blocks + 1, tok_rows, key_width), value_...  14.3 us
    dot_general x1, matrix products, local(): jnp.einsum('tkgd,skd->kgts', d_attn_heads, value_window, preferred_elemen...  14.1 us
  transfers between devices with their start and end apart: 10, of which 5 were waited for; matrix products, arithmetic and copies ran while one was open for 18% of the time, Pallas kernels for 0%

commit v1 on v0

--- a/solution.py
+++ b/solution.py
@@ -1,13 +1,20 @@
+import functools
+
 import jax
 import jax.numpy as jnp
 from jax import lax
+from jax.experimental import pallas as pl
+from jax.experimental.pallas import tpu as pltpu
 from jax.sharding import PartitionSpec as P
 
 HEAD = 128
 WINDOW = 1024
+GROUP = 4
 
 
 query_scale = 168.0 ** (-0.5)
+LOG2E = 1.4426950408889634
+HIDDEN = -1e30
 
 
 def shifted(shard, axis, by):
@@ -16,7 +23,222 @@
     return lax.ppermute(shard, axis, pairs)
 
 
-def local(queries, keys, values, out_weight, out_grad, block_doc):
+def swapped(shard, axis, by):
+    return lax.ppermute(shard, axis, [(i, i ^ by) for i in range(lax.axis_size(axis))])
+
+
+def attention_kernel(rows, info, *refs):
+    q_refs, g_refs = refs[:GROUP], refs[GROUP : 2 * GROUP]
+    k_own, v_own, k_far, v_far = refs[2 * GROUP : 2 * GROUP + 4]
+    outs = refs[2 * GROUP + 4 :]
+    back_refs = outs[:GROUP]
+    attn_cat, kv_own, kv_far = outs[GROUP : GROUP + 3]
+    q_all, g_all, k_all, v_all, k_tr, v_tr, k_acc, v_acc, back = outs[GROUP + 3 :]
+    r, tp = info[0], info[1]
+    heads = q_refs[0].shape[1] // HEAD
+    half = rows // 2
+    for m in range(GROUP):
+        q_all[m] = q_refs[m][...]
+        g_all[m] = g_refs[m][...]
+        spot = r ^ m
+        for place, k, v in ((spot, k_far, v_far), (spot + GROUP, k_own, v_own)):
+            k_all[place] = k[m]
+            v_all[place] = v[m]
+            k_tr[place] = k[m].T
+            v_tr[place] = v[m].T
+    k_acc[...] = jnp.zeros_like(k_acc)
+    v_acc[...] = jnp.zeros_like(v_acc)
+    key_at = lax.broadcasted_iota(jnp.int32, (rows, rows), 0)
+    query_at = lax.broadcasted_iota(jnp.int32, (rows, rows), 1)
+    nt = (((1,), (1,)), ((), ()))
+
+    def dot(a, b):
+        return jnp.dot(a, b, preferred_element_type=jnp.float32)
+
+    def block(m, carry):
+        first = r ^ m
+        own_doc = info[2 + first + GROUP]
+        for h in range(heads):
+            cols = slice(h * HEAD, (h + 1) * HEAD)
+            q = q_all[m, :, cols]
+            g = g_all[m, :, cols]
+            scores = []
+            for j in range(GROUP + 1):
+                s = lax.dot_general(k_all[first + j], q, nt, preferred_element_type=jnp.float32)
+                if j == 0:
+                    s = jnp.where(key_at > query_at, s, HIDDEN)
+                if j == GROUP:
+                    s = jnp.where(key_at <= query_at, s, HIDDEN)
+                else:
+                    s = s + jnp.where(info[2 + first + j] == own_doc, 0.0, HIDDEN)
+                scores.append(s)
+            top = functools.reduce(jnp.maximum, [jnp.max(s, axis=0, keepdims=True) for s in scores])
+            top = top * (query_scale * LOG2E)
+            expo = [jnp.exp2(s * (query_scale * LOG2E) - top) for s in scores]
+            whole = functools.reduce(jnp.add, [jnp.sum(e, axis=0, keepdims=True) for e in expo])
+            inverse = 1.0 / whole
+            probs = [e * inverse for e in expo]
+            low = [p.astype(jnp.bfloat16) for p in probs]
+            attn_tr = functools.reduce(
+                jnp.add, [dot(v_tr[first + j], low[j]) for j in range(GROUP + 1)]
+            )
+            attn_tr = attn_tr.astype(jnp.bfloat16).astype(jnp.float32)
+            g_tr = g.astype(jnp.float32).T
+            delta = jnp.sum(attn_tr * g_tr, axis=0, keepdims=True)
+            dq_tr = None
+            for j in range(GROUP + 1):
+                d_p = lax.dot_general(v_all[first + j], g, nt, preferred_element_type=jnp.float32)
+                d_s = (probs[j] * (d_p - delta)).astype(jnp.bfloat16)
+                term = dot(k_tr[first + j], d_s)
+                dq_tr = term if dq_tr is None else dq_tr + term
+                k_acc[first + j] += dot(d_s, q)
+                v_acc[first + j] += dot(low[j], g)
+            back[m, 0, :, cols] = attn_tr.T.astype(jnp.bfloat16)
+            back[m, 1, :, cols] = (dq_tr * query_scale).T.astype(jnp.bfloat16)
+        return carry
+
+    lax.fori_loop(0, GROUP, block, 0)
+    for m in range(GROUP):
+        back_refs[m][...] = back[m]
+        spot = r ^ m
+        kv_far[0, m] = (k_acc[spot] * query_scale).astype(kv_far.dtype)
+        kv_far[1, m] = v_acc[spot].astype(kv_far.dtype)
+        kv_own[0, m] = k_acc[spot + GROUP] * query_scale
+        kv_own[1, m] = v_acc[spot + GROUP]
+    attn_cat[0:rows] = back[0, 0]
+    near = pl.multiple_of(tp * half, half)
+    away = pl.multiple_of((1 - tp) * half, half)
+    for m in range(1, GROUP):
+        at = rows + (m - 1) * half
+        attn_cat[at : at + half] = back[m, 0, pl.ds(near, half), :]
+        at += (GROUP - 1) * half
+        attn_cat[at : at + half] = back[m, 0, pl.ds(away, half), :]
+
+
+def attention(info, queries, d_attn, kv_own, kv_far):
+    rows, q_width = queries[0].shape
+    kv_heads = kv_own.shape[2] // HEAD // 2
+    q_block = q_width // kv_heads
+    q_spec = pl.BlockSpec((rows, q_block), lambda g: (0, g))
+    k_spec = pl.BlockSpec((GROUP, rows, HEAD), lambda g: (0, 0, g))
+    v_spec = pl.BlockSpec((GROUP, rows, HEAD), lambda g: (0, 0, g + kv_heads))
+    back_spec = pl.BlockSpec((2, rows, q_block), lambda g: (0, 0, g))
+    kv_spec = pl.BlockSpec((2, GROUP, rows, HEAD), lambda g: (0, 0, 0, g))
+    kv_shape = (2, GROUP, rows, kv_heads * HEAD)
+    bf16 = jnp.bfloat16
+    blocks = 2 * GROUP
+    return pl.pallas_call(
+        functools.partial(attention_kernel, rows),
+        grid=(kv_heads,),
+        in_specs=[pl.BlockSpec(memory_space=pltpu.SMEM)]
+        + [q_spec] * (2 * GROUP)
+        + [k_spec, v_spec, k_spec, v_spec],
+        out_specs=[back_spec] * GROUP
+        + [pl.BlockSpec((GROUP * rows, q_block), lambda g: (0, g)), kv_spec, kv_spec],
+        out_shape=[jax.ShapeDtypeStruct((2, rows, q_width), bf16)] * GROUP
+        + [
+            jax.ShapeDtypeStruct((GROUP * rows, q_width), bf16),
+            jax.ShapeDtypeStruct(kv_shape, jnp.float32),
+            jax.ShapeDtypeStruct(kv_shape, bf16),
+        ],
+        scratch_shapes=[
+            pltpu.VMEM((GROUP, rows, q_block), bf16),
+            pltpu.VMEM((GROUP, rows, q_block), bf16),
+            pltpu.VMEM((blocks, rows, HEAD), bf16),
+            pltpu.VMEM((blocks, rows, HEAD), bf16),
+            pltpu.VMEM((blocks, HEAD, rows), bf16),
+            pltpu.VMEM((blocks, HEAD, rows), bf16),
+            pltpu.VMEM((blocks, rows, HEAD), jnp.float32),
+            pltpu.VMEM((blocks, rows, HEAD), jnp.float32),
+            pltpu.VMEM((GROUP, 2, rows, q_block), bf16),
+        ],
+        compiler_params=pltpu.CompilerParams(vmem_limit_bytes=40 * 1024 * 1024),
+        cost_estimate=pl.CostEstimate(
+            flops=12 * q_width * GROUP * rows * (GROUP + 1) * rows,
+            bytes_accessed=10 * 1024 * 1024,
+            transcendentals=0,
+        ),
+    )(info, *queries, *d_attn, kv_own, kv_own, kv_far, kv_far)
+
+
+def grouped(queries, keys, values, out_weight, out_grad, block_doc):
+    f32, bf16 = jnp.float32, jnp.bfloat16
+    rows = queries.shape[0]
+    me, tp = lax.axis_index("ctx"), lax.axis_index("tp")
+    r, layer = me % GROUP, me // GROUP
+    members = range(GROUP)
+    q_width, kv_width = queries.shape[1] // GROUP, keys.shape[1] // GROUP
+    d_out = out_grad.shape[1]
+
+    def part(array, m, width, dim):
+        return lax.dynamic_slice_in_dim(array, (r ^ m) * width, width, dim)
+
+    def traded(blocks):
+        return [blocks[0]] + [swapped(blocks[m], "ctx", m) for m in members[1:]]
+
+    def in_order(blocks, dim):
+        width = blocks[0].shape[dim]
+        shape = list(blocks[0].shape)
+        shape[dim] = width * GROUP
+        whole = jnp.zeros(shape, blocks[0].dtype)
+        for m in members:
+            whole = lax.dynamic_update_slice_in_dim(whole, blocks[m], (r ^ m) * width, dim)
+        return whole
+
+    kv = traded(
+        [
+            jnp.concatenate([part(keys, m, kv_width, 1), part(values, m, kv_width, 1)], axis=1)
+            for m in members
+        ]
+    )
+    kv_own = jnp.stack(kv)
+    kv_far = shifted(kv_own, "ctx", GROUP)
+    q = traded([part(queries, m, q_width, 1) for m in members])
+    d_attn = traded(
+        [
+            jnp.einsum(
+                "te,re->tr", out_grad, part(out_weight, m, q_width, 0), preferred_element_type=f32
+            ).astype(bf16)
+            for m in members
+        ]
+    )
+    half = lax.dynamic_slice_in_dim(out_grad, tp * (rows // 2), rows // 2, 0)
+    near = jnp.concatenate([swapped(half, "ctx", m) for m in members[1:]], axis=0)
+    away = swapped(near, "tp", 1)
+    grad_cat = jnp.concatenate([out_grad, near, away], axis=0)
+
+    doc_padded = jnp.concatenate([jnp.full((GROUP,), -1, jnp.int32), block_doc])
+    docs = lax.dynamic_slice_in_dim(doc_padded, layer * GROUP, 2 * GROUP, 0)
+    info = jnp.concatenate([jnp.stack([r, tp]).astype(jnp.int32), docs])
+    *back, attn_cat, own_grad, far_grad = attention(info, q, d_attn, kv_own, kv_far)
+
+    weight_terms = jnp.einsum("te,th->eh", grad_cat, attn_cat, preferred_element_type=f32)
+    layers = lax.axis_size("ctx") // GROUP
+    columns = [[i * GROUP + j for i in range(layers)] for j in members]
+    weight_sums = lax.psum_scatter(
+        weight_terms.astype(bf16),
+        "ctx",
+        scatter_dimension=0,
+        axis_index_groups=columns,
+        tiled=True,
+    )
+    cut = weight_sums.shape[0] // GROUP
+    weight_blocks = traded([part(weight_sums, m, cut, 0) for m in members])
+    out_weight_grad = in_order([b.astype(f32) for b in weight_blocks], 1).T
+
+    back = in_order(traded(back), 2)
+    attn, query_grad = back[0], back[1]
+    terms = jnp.einsum("re,tr->et", out_weight, attn, preferred_element_type=f32)
+    mine = lax.dynamic_slice_in_dim(terms, tp * (d_out // 2), d_out // 2, 0)
+    theirs = lax.dynamic_slice_in_dim(terms, (1 - tp) * (d_out // 2), d_out // 2, 0)
+    attn_output = (mine + swapped(theirs.astype(bf16), "tp", 1).astype(f32)).astype(bf16).T
+
+    total = (own_grad + shifted(far_grad, "ctx", -GROUP).astype(f32)).astype(bf16)
+    total = in_order(traded([total[:, m] for m in members]), 2)
+    return (attn_output, query_grad, total[0], total[1], out_weight_grad)
+
+
+def single(queries, keys, values, out_weight, out_grad, block_doc):
     tok_rows = queries.shape[0]
     head_size = HEAD
     kv_count = keys.shape[1] // head_size
@@ -103,6 +325,17 @@
     return (attn_output, query_grad, key_grad, value_grad, out_weight_grad)
 
 
+def local(queries, keys, values, out_weight, out_grad, block_doc):
+    fits = (
+        lax.axis_size("ctx") % GROUP == 0
+        and queries.shape[0] * GROUP == WINDOW
+        and keys.shape[1] % (GROUP * HEAD) == 0
+        and lax.axis_size("tp") == 2
+    )
+    step = grouped if fits else single
+    return step(queries, keys, values, out_weight, out_grad, block_doc)
+
+
 def solution(mesh):
     placed = (P("ctx", "tp"), P("ctx", "tp"), P("ctx", "tp"), P("tp", None), P("ctx", None), P())
     return jax.shard_map(

time: 674 us -> 236 us (0.35)
  waiting for transfers between devices: 443 us -> 91.1 us
  local copies, waits for them, and re-layouts: 82.1 us -> 28.3 us
  matrix products: 75.1 us -> 24.6 us
  Pallas kernels: 0 us -> 33.7 us
  other arithmetic: 27.6 us -> 9.55 us
  starting transfers between devices: 22.7 us -> 31.8 us
    reduce_scatter x2 -> x1, waiting for transfers between devices: 203 us -> 0.02 us  [grouped(): lax.psum_scatter(weight_terms.astype(bf16), 'ctx', scatter_dimension=0, a...]
    ppermute x8 -> x2, waiting for transfers between devices: 240 us -> 37.9 us  [shifted(): return lax.ppermute(shard, axis, pairs)]
    ppermute x0 -> x23, waiting for transfers between devices: none -> 53.1 us  [swapped(): lax.ppermute(shard, axis, [(i, i ^ by) for i in range(lax.axis_size(axis))])]
    dot_general x8 -> x6, matrix products: 62.7 us -> 24.6 us  [the longest x4 13 us: grouped(): jnp.einsum('te,re->tr', out_grad, part(out_weight, m, q_width, 0), prefer...]
    pallas_call x0 -> x1, Pallas kernels: none -> 33.7 us  [attention(): pl.pallas_call(functools.partial(attention_kernel, rows), grid=(kv_heads,...]
    ppermute x0 -> x23, starting transfers between devices: none -> 25.8 us  [swapped(): lax.ppermute(shard, axis, [(i, i ^ by) for i in range(lax.axis_size(axis))])]
    another operation x5 -> x0, local copies, waits for them, and re-layouts: 20.3 us -> none  [the longest x3 14.3 us: local(): jnp.stack([key_part.reshape(span_blocks + 1, tok_rows, key_width), value_...]
    unnamed x38 -> x35, local copies, waits for them, and re-layouts: 25.8 us -> 8.7 us
  transfers between devices with their start and end apart: 10 -> 26, of which waited for: 5 -> 13; matrix products, arithmetic and copies ran while one was open for 18% -> 21% of each run, Pallas kernels for 0% -> 14%
where the time goes in v1:
time: 236 us; the launch traced here: 233 us
  waiting for transfers between devices  91.1 us (39%)
  Pallas kernels  33.7 us (14%)
  starting transfers between devices  31.8 us (13%)
  local copies, waits for them, and re-layouts  28.3 us (12%)
  matrix products  24.6 us (10%)
  between operations  14.5 us (6%)
  other arithmetic  9.55 us (4%)
    ppermute x23, waiting for transfers between devices, swapped(): lax.ppermute(shard, axis, [(i, i ^ by) for i in range(lax.axis_size(axis))])  53.1 us
    ppermute x2, waiting for transfers between devices, shifted(): return lax.ppermute(shard, axis, pairs)  37.9 us
    pallas_call x1, Pallas kernels, attention(): pl.pallas_call(functools.partial(attention_kernel, rows), grid=(kv_heads,...  33.7 us
    ppermute x23, starting transfers between devices, swapped(): lax.ppermute(shard, axis, [(i, i ^ by) for i in range(lax.axis_size(axis))])  25.8 us
    dot_general x4, matrix products, grouped(): jnp.einsum('te,re->tr', out_grad, part(out_weight, m, q_width, 0), prefer...  13 us
    unnamed x35, local copies, waits for them, and re-layouts  8.7 us
    dot_general x1, matrix products, grouped(): jnp.einsum('re,tr->et', out_weight, attn, preferred_element_type=f32)  7.03 us
    ppermute x2, starting transfers between devices, shifted(): return lax.ppermute(shard, axis, pairs)  5.93 us
  transfers between devices with their start and end apart: 26, of which 13 were waited for; matrix products, arithmetic and copies ran while one was open for 21% of the time, Pallas kernels for 14%

profile of v1, /device:TPU:0, one launch (start us, length us, event | category | flops | bytes accessed | tf_op | source)
XLA Modules:
  0.0 233.5 jit_solution(4633814677722520854)
XLA Ops:
  7.2 2.0 constant_dynamic-slice_fusion.3
  9.2 2.9 %collective-permute-start.18 = (bf16[128,2688]{1,0:T(8,128)(2,1)}, bf16[128,2688]{1,0:T(8,128)(2,1)S(1)}, u32[]{:S(2)}, u32[]{:S(2)}) collective-permute-start(bf16[128,2688]{1,0:T(8,128)(2,1)} %constant_dynamic-slice_fusion.3), channel_id=1, source_target_pairs={{0,2},{2,0},{4,6},{6,4},{8,10},{10,8},{12,14},{14,12},{16,18},{18,... | collective-permute-start | bytes 2064392 | tf_op jit(solution)/shard_map/ppermute | solution.py:27
  12.2 1.5 collective-permute-start.19
  13.7 2.2 constant_dynamic-slice_fusion.12
  15.9 2.0 collective-permute-start
  17.8 2.1 constant_dynamic-slice_fusion.10
  22.2 3.4 %fusion.30.refs_4_ = bf16[256,512]{1,0:T(8,128)(2,1)} fusion(bf16[256,2688]{1,0:T(8,128)(2,1)S(1)} %copy-done.7, bf16[2048,2688]{1,0:T(8,128)(2,1)} %param.9, s32[]{:T(128)S(6)} %select_n.82), kind=kOutput, calls=%fused_computation.21 | convolution fusion | flops 704774144 | bytes 4390916 | tf_op jit(solution)/shard_map/te,re->tr/dot_general | solution.py:199
  25.6 3.4 %fusion.27 = bf16[256,512]{1,0:T(8,128)(2,1)} fusion(bf16[256,2688]{1,0:T(8,128)(2,1)S(1)} %copy-done.7, bf16[2048,2688]{1,0:T(8,128)(2,1)} %param.9, s32[]{:T(128)S(6)} %select_n.83), kind=kOutput, calls=%fused_computation.20 | convolution fusion | flops 704774144 | bytes 4390916 | tf_op jit(solution)/shard_map/te,re->tr/dot_general | solution.py:199
  29.0 3.4 %fusion.24 = bf16[256,512]{1,0:T(8,128)(2,1)} fusion(bf16[256,2688]{1,0:T(8,128)(2,1)S(1)} %copy-done.7, bf16[2048,2688]{1,0:T(8,128)(2,1)} %param.9, s32[]{:T(128)S(6)} %select_n.84), kind=kOutput, calls=%fused_computation.19 | convolution fusion | flops 704774144 | bytes 4390916 | tf_op jit(solution)/shard_map/te,re->tr/dot_general | solution.py:199
  34.5 2.7 %fusion.21 = bf16[256,512]{1,0:T(8,128)(2,1)S(1)} fusion(bf16[256,2688]{1,0:T(8,128)(2,1)S(1)} %copy-done.7, bf16[2048,2688]{1,0:T(8,128)(2,1)} %param.9, s32[]{:T(128)S(6)} %select_n.85), kind=kOutput, calls=%fused_computation.18 | convolution fusion | flops 704774144 | bytes 4390916 | tf_op jit(solution)/shard_map/te,re->tr/dot_general | solution.py:199
  37.5 7.0 %collective-permute-done.19 = bf16[128,2688]{1,0:T(8,128)(2,1)} collective-permute-done((bf16[128,2688]{1,0:T(8,128)(2,1)}, bf16[128,2688]{1,0:T(8,128)(2,1)}, u32[]{:S(2)}, u32[]{:S(2)}) %collective-permute-start.19) | collective-permute-done | bytes 688160 | tf_op jit(solution)/shard_map/ppermute | solution.py:27
  46.3 10.0 %collective-permute-done.8 = bf16[256,512]{1,0:T(8,128)(2,1)} collective-permute-done((bf16[256,512]{1,0:T(8,128)(2,1)}, bf16[256,512]{1,0:T(8,128)(2,1)}, u32[]{:S(2)}, u32[]{:S(2)}) %collective-permute-start.8) | collective-permute-done | bytes 262176 | tf_op jit(solution)/shard_map/ppermute | solution.py:27
  56.4 2.9 %collective-permute-start.2 = (bf16[256,512]{1,0:T(8,128)(2,1)S(1)}, bf16[256,512]{1,0:T(8,128)(2,1)S(1)}, u32[]{:S(2)}, u32[]{:S(2)}) collective-permute-start(bf16[256,512]{1,0:T(8,128)(2,1)S(1)} %copy-done.10), channel_id=1, source_target_pairs={{0,6},{2,4},{4,2},{6,0},{8,14},{10,12},{12,10},{14,8},{16,22},{18,... | collective-permute-start | bytes 786440 | tf_op jit(solution)/shard_map/ppermute | solution.py:27
  61.5 4.4 %collective-permute-start.9 = (bf16[4,256,512]{2,1,0:T(8,128)(2,1)S(1)}, bf16[4,256,512]{2,1,0:T(8,128)(2,1)S(1)}, u32[]{:S(2)}, u32[]{:S(2)}) collective-permute-start(bf16[4,256,512]{2,1,0:T(8,128)(2,1)S(1)} %pad_maximum_fusion.1.refs_8_.refs_9_), channel_id=1, source_target_pairs={{0,8},{2,10},{4,12},{6,14},{8,16},{10,18},{12,20},{14,22},{16,24},... | collective-permute-start | bytes 3145736 | tf_op jit(solution)/shard_map/ppermute | solution.py:23
  67.2 1.6 collective-permute-start.3
  71.5 4.3 %collective-permute-done.3.refs_5_ = bf16[256,512]{1,0:T(8,128)(2,1)S(1)} collective-permute-done((bf16[256,512]{1,0:T(8,128)(2,1)S(1)}, bf16[256,512]{1,0:T(8,128)(2,1)S(1)}, u32[]{:S(2)}, u32[]{:S(2)}) %collective-permute-start.3) | collective-permute-done | bytes 262176 | tf_op jit(solution)/shard_map/ppermute | solution.py:27
  75.8 4.0 %collective-permute-done.4.refs_6_ = bf16[256,512]{1,0:T(8,128)(2,1)S(1)} collective-permute-done((bf16[256,512]{1,0:T(8,128)(2,1)S(1)}, bf16[256,512]{1,0:T(8,128)(2,1)S(1)}, u32[]{:S(2)}, u32[]{:S(2)}) %collective-permute-start.4) | collective-permute-done | bytes 262176 | tf_op jit(solution)/shard_map/ppermute | solution.py:27
  79.9 6.2 %collective-permute-done.9.refs_10_.refs_11_ = bf16[4,256,512]{2,1,0:T(8,128)(2,1)S(1)} collective-permute-done((bf16[4,256,512]{2,1,0:T(8,128)(2,1)S(1)}, bf16[4,256,512]{2,1,0:T(8,128)(2,1)S(1)}, u32[]{:S(2)}, u32[]{:S(2)}) %collective-permute-start.9) | collective-permute-done | bytes 1048608 | tf_op jit(solution)/shard_map/ppermute | solution.py:23
  87.0 33.7 %shard_map.101 = (bf16[2,256,512]{2,1,0:T(8,128)(2,1)S(1)}, bf16[2,256,512]{2,1,0:T(8,128)(2,1)S(1)}, bf16[2,256,512]{2,1,0:T(8,128)(2,1)S(1)}, bf16[2,256,512]{...) custom-call(s32[10]{0:T(128)S(1)} %pad_add_fusion.info, ...), custom_call_target="tpu_custom_call" | custom-call | flops 8053063680 | bytes 10485760 | tf_op jit(solution)/shard_map/pallas_call | solution.py:130
  123.6 4.6 %convolution_convert_fusion = bf16[2688,512]{1,0:T(8,128)(2,1)} fusion(bf16[1024,2688]{1,0:T(8,128)(2,1)S(1)} %constant_dynamic-update-slice_fusion, bf16[1024,512]{1,0:T(8,128)(2,1)S(1)} %get-tuple-element.18), kind=kOutput, calls=%fused_computation | convolution fusion | flops 2819948544 | bytes 9306112 | tf_op jit(solution)/shard_map/te,th->eh/dot_general | solution.py:215
  128.2 1.6 collective-permute-start.10
  133.6 9.9 %collective-permute-done.10 = bf16[2,256,512]{2,1,0:T(8,128)(2,1)} collective-permute-done((bf16[2,256,512]{2,1,0:T(8,128)(2,1)}, bf16[2,256,512]{2,1,0:T(8,128)(2,1)}, u32[]{:S(2)}, u32[]{:S(2)}) %collective-permute-start.10) | collective-permute-done | bytes 524320 | tf_op jit(solution)/shard_map/ppermute | solution.py:27
  144.5 7.2 %collective-permute-done.11 = bf16[2,256,512]{2,1,0:T(8,128)(2,1)} collective-permute-done((bf16[2,256,512]{2,1,0:T(8,128)(2,1)}, bf16[2,256,512]{2,1,0:T(8,128)(2,1)}, u32[]{:S(2)}, u32[]{:S(2)}) %collective-permute-start.11) | collective-permute-done | bytes 524320 | tf_op jit(solution)/shard_map/ppermute | solution.py:27
  154.0 7.0 %fusion.33 = f32[256,2688]{1,0:T(8,128)S(1)} fusion(bf16[2048,2688]{1,0:T(8,128)(2,1)} %param.9, bf16[2,256,2048]{2,1,0:T(8,128)(2,1)S(1)} %constant_dynamic-update-slice_fusion.8), kind=kOutput, calls=%fused_computation.24 | convolution fusion | flops 2818572288 | bytes 14811136 | tf_op jit(solution)/shard_map/re,tr->et/dot_general | solution.py:231
  161.1 1.5 copy-done.8
  164.0 2.3 slice_bitcast_fusion
  166.3 31.8 %collective-permute-done.14 = bf16[2,4,256,256]{3,2,1,0:T(8,128)(2,1)} collective-permute-done((bf16[2,4,256,256]{3,2,1,0:T(8,128)(2,1)}, bf16[2,4,256,256]{3,2,1,0:T(8,128)(2,1)}, u32[]{:S(2)}, u32[]{:S(2)}) %collective-permute-start.14) | collective-permute-done | bytes 1048608 | tf_op jit(solution)/shard_map/ppermute | solution.py:23
  200.4 1.5 collective-permute-start.15
  204.4 1.9 fusion.35
  210.5 4.1 %collective-permute-done.17 = bf16[2,256,256]{2,1,0:T(8,128)(2,1)S(1)} collective-permute-done((bf16[2,256,256]{2,1,0:T(8,128)(2,1)}, bf16[2,256,256]{2,1,0:T(8,128)(2,1)S(1)}, u32[]{:S(2)}, u32[]{:S(2)}) %collective-permute-start.17) | collective-permute-done | bytes 262176 | tf_op jit(solution)/shard_map/ppermute | solution.py:27
  218.9 1.5 collective-permute-start.24
  221.6 3.9 %collective-permute-done.23 = bf16[168,512]{1,0:T(8,128)(2,1)S(1)} collective-permute-done((bf16[168,512]{1,0:T(8,128)(2,1)S(1)}, bf16[168,512]{1,0:T(8,128)(2,1)S(1)}, u32[]{:S(2)}, u32[]{:S(2)}) %collective-permute-start.23) | collective-permute-done | bytes 172064 | tf_op jit(solution)/shard_map/ppermute | solution.py:27
  (99 shorter events, 40.4 us)
Async XLA Ops:
  7.2 207.5 %reduce-scatter.2.cloned.1.call-start = ((), (), s32[]{:S(2)}) async-start(), calls=%async_computation.1 | async-start | bytes 3440640 | tf_op jit(solution)/shard_map/reduce_scatter | solution.py:218
  9.2 28.2 %collective-permute-start.18 = (bf16[128,2688]{1,0:T(8,128)(2,1)}, bf16[128,2688]{1,0:T(8,128)(2,1)S(1)}, u32[]{:S(2)}, u32[]{:S(2)}) collective-permute-start(bf16[128,2688]{1,0:T(8,128)(2,1)} %constant_dynamic-slice_fusion.3), channel_id=1, source_target_pairs={{0,2},{2,0},{4,6},{6,4},{8,10},{10,8},{12,14},{14,12},{16,18},{18,... | collective-permute-start | bytes 2064392 | tf_op jit(solution)/shard_map/ppermute | solution.py:27
  12.2 32.4 %collective-permute-start.19 = (bf16[128,2688]{1,0:T(8,128)(2,1)}, bf16[128,2688]{1,0:T(8,128)(2,1)}, u32[]{:S(2)}, u32[]{:S(2)}) collective-permute-start(bf16[128,2688]{1,0:T(8,128)(2,1)} %constant_dynamic-slice_fusion.3), channel_id=1, source_target_pairs={{0,4},{2,6},{4,0},{6,2},{8,12},{10,14},{12,8},{14,10},{16,20},{18,... | collective-permute-start | bytes 2064392 | tf_op jit(solution)/shard_map/ppermute | solution.py:27
  13.7 31.3 %collective-permute-start.20 = (bf16[128,2688]{1,0:T(8,128)(2,1)}, bf16[128,2688]{1,0:T(8,128)(2,1)S(1)}, u32[]{:S(2)}, u32[]{:S(2)}) collective-permute-start(bf16[128,2688]{1,0:T(8,128)(2,1)} %constant_dynamic-slice_fusion.3), channel_id=1, source_target_pairs={{0,6},{2,4},{4,2},{6,0},{8,14},{10,12},{12,10},{14,8},{16,22},{18,... | collective-permute-start | bytes 2064392 | tf_op jit(solution)/shard_map/ppermute | solution.py:27
  13.7 8.5 %copy-start.7 = (bf16[256,2688]{1,0:T(8,128)(2,1)S(1)}, bf16[256,2688]{1,0:T(8,128)(2,1)}, u32[]{:S(2)}) copy-start(bf16[256,2688]{1,0:T(8,128)(2,1)} %param.10) | copy-start | bytes 4128772
  15.9 51.3 %collective-permute-start = (bf16[256,512]{1,0:T(8,128)(2,1)}, bf16[256,512]{1,0:T(8,128)(2,1)S(1)}, u32[]{:S(2)}, u32[]{:S(2)}) collective-permute-start(bf16[256,512]{1,0:T(8,128)(2,1)} %get-tuple-element.35), channel_id=1, source_target_pairs={{0,2},{2,0},{4,6},{6,4},{8,10},{10,8},{12,14},{14,12},{16,18},{18,... | collective-permute-start | bytes 786440 | tf_op jit(solution)/shard_map/ppermute | solution.py:27
  20.7 35.6 %collective-permute-start.8 = (bf16[256,512]{1,0:T(8,128)(2,1)}, bf16[256,512]{1,0:T(8,128)(2,1)}, u32[]{:S(2)}, u32[]{:S(2)}) collective-permute-start(bf16[256,512]{1,0:T(8,128)(2,1)} %pad_maximum_fusion.4), channel_id=1, source_target_pairs={{0,6},{2,4},{4,2},{6,0},{8,14},{10,12},{12,10},{14,8},{16,22},{18,... | collective-permute-start | bytes 786440 | tf_op jit(solution)/shard_map/ppermute | solution.py:27
  37.4 19.0 %copy-start.11 = (bf16[256,512]{1,0:T(8,128)(2,1)S(1)}, bf16[256,512]{1,0:T(8,128)(2,1)}, u32[]{:S(2)}) copy-start(bf16[256,512]{1,0:T(8,128)(2,1)} %get-tuple-element.37) | copy-start | bytes 786436
  37.4 19.0 %copy-start.10 = (bf16[256,512]{1,0:T(8,128)(2,1)S(1)}, bf16[256,512]{1,0:T(8,128)(2,1)}, u32[]{:S(2)}) copy-start(bf16[256,512]{1,0:T(8,128)(2,1)} %get-tuple-element.34) | copy-start | bytes 786436
  37.4 18.9 %collective-permute-start.7 = (bf16[256,512]{1,0:T(8,128)(2,1)S(1)}, bf16[256,512]{1,0:T(8,128)(2,1)S(1)}, u32[]{:S(2)}, u32[]{:S(2)}) collective-permute-start(bf16[256,512]{1,0:T(8,128)(2,1)S(1)} %pad_maximum_fusion.3), channel_id=1, source_target_pairs={{0,4},{2,6},{4,0},{6,2},{8,12},{10,14},{12,8},{14,10},{16,20},{18,... | collective-permute-start | bytes 786440 | tf_op jit(solution)/shard_map/ppermute | solution.py:27
  44.5 15.8 %collective-permute-start.6 = (bf16[256,512]{1,0:T(8,128)(2,1)S(1)}, bf16[256,512]{1,0:T(8,128)(2,1)S(1)}, u32[]{:S(2)}, u32[]{:S(2)}) collective-permute-start(bf16[256,512]{1,0:T(8,128)(2,1)S(1)} %pad_maximum_fusion.2), channel_id=1, source_target_pairs={{0,2},{2,0},{4,6},{6,4},{8,10},{10,8},{12,14},{14,12},{16,18},{18,... | collective-permute-start | bytes 786440 | tf_op jit(solution)/shard_map/ppermute | solution.py:27
  46.2 77.1 %collective-permute-start.21 = (bf16[384,2688]{1,0:T(8,128)(2,1)S(1)}, bf16[384,2688]{1,0:T(8,128)(2,1)S(1)}, u32[]{:S(2)}, u32[]{:S(2)}) collective-permute-start(bf16[384,2688]{1,0:T(8,128)(2,1)S(1)} %pad_maximum_fusion), channel_id=1, source_target_pairs={{0,1},{1,0},{2,3},{3,2},{4,5},{5,4},{6,7},{7,6},{8,9},{9,8},{10,11... | collective-permute-start | bytes 6193160 | tf_op jit(solution)/shard_map/ppermute | solution.py:27
  56.3 12.4 %collective-permute-start.1 = (bf16[256,512]{1,0:T(8,128)(2,1)S(1)}, bf16[256,512]{1,0:T(8,128)(2,1)S(1)}, u32[]{:S(2)}, u32[]{:S(2)}) collective-permute-start(bf16[256,512]{1,0:T(8,128)(2,1)S(1)} %copy-done.11), channel_id=1, source_target_pairs={{0,4},{2,6},{4,0},{6,2},{8,12},{10,14},{12,8},{14,10},{16,20},{18,... | collective-permute-start | bytes 786440 | tf_op jit(solution)/shard_map/ppermute | solution.py:27
  56.4 13.9 %collective-permute-start.2 = (bf16[256,512]{1,0:T(8,128)(2,1)S(1)}, bf16[256,512]{1,0:T(8,128)(2,1)S(1)}, u32[]{:S(2)}, u32[]{:S(2)}) collective-permute-start(bf16[256,512]{1,0:T(8,128)(2,1)S(1)} %copy-done.10), channel_id=1, source_target_pairs={{0,6},{2,4},{4,2},{6,0},{8,14},{10,12},{12,10},{14,8},{16,22},{18,... | collective-permute-start | bytes 786440 | tf_op jit(solution)/shard_map/ppermute | solution.py:27
  60.3 8.5 %copy-start.12 = (bf16[256,512]{1,0:T(8,128)(2,1)S(1)}, bf16[256,512]{1,0:T(8,128)(2,1)}, u32[]{:S(2)}) copy-start(bf16[256,512]{1,0:T(8,128)(2,1)} %fusion.24) | copy-start | bytes 786436
  61.5 24.6 %copy-start.5 = (bf16[256,512]{1,0:T(8,128)(2,1)S(1)}, bf16[256,512]{1,0:T(8,128)(2,1)}, u32[]{:S(2)}) copy-start(bf16[256,512]{1,0:T(8,128)(2,1)} %fusion.30.refs_4_) | copy-start | bytes 786436
  61.5 24.6 %collective-permute-start.9 = (bf16[4,256,512]{2,1,0:T(8,128)(2,1)S(1)}, bf16[4,256,512]{2,1,0:T(8,128)(2,1)S(1)}, u32[]{:S(2)}, u32[]{:S(2)}) collective-permute-start(bf16[4,256,512]{2,1,0:T(8,128)(2,1)S(1)} %pad_maximum_fusion.1.refs_8_.refs_9_), channel_id=1, source_target_pairs={{0,8},{2,10},{4,12},{6,14},{8,16},{10,18},{12,20},{14,22},{16,24},... | collective-permute-start | bytes 3145736 | tf_op jit(solution)/shard_map/ppermute | solution.py:23
  67.2 18.9 %copy-start.3 = (bf16[256,512]{1,0:T(8,128)(2,1)}, bf16[256,512]{1,0:T(8,128)(2,1)S(1)}, u32[]{:S(2)}) copy-start(bf16[256,512]{1,0:T(8,128)(2,1)S(1)} %collective-permute-done.refs_1_) | copy-start | bytes 786436
  67.2 8.6 %collective-permute-start.3 = (bf16[256,512]{1,0:T(8,128)(2,1)S(1)}, bf16[256,512]{1,0:T(8,128)(2,1)S(1)}, u32[]{:S(2)}, u32[]{:S(2)}) collective-permute-start(bf16[256,512]{1,0:T(8,128)(2,1)S(1)} %copy-done.13), channel_id=1, source_target_pairs={{0,2},{2,0},{4,6},{6,4},{8,10},{10,8},{12,14},{14,12},{16,18},{18,... | collective-permute-start | bytes 786440 | tf_op jit(solution)/shard_map/ppermute | solution.py:27
  68.8 11.1 %collective-permute-start.4 = (bf16[256,512]{1,0:T(8,128)(2,1)S(1)}, bf16[256,512]{1,0:T(8,128)(2,1)S(1)}, u32[]{:S(2)}, u32[]{:S(2)}) collective-permute-start(bf16[256,512]{1,0:T(8,128)(2,1)S(1)} %copy-done.12), channel_id=1, source_target_pairs={{0,4},{2,6},{4,0},{6,2},{8,12},{10,14},{12,8},{14,10},{16,20},{18,... | collective-permute-start | bytes 786440 | tf_op jit(solution)/shard_map/ppermute | solution.py:27
  70.2 9.6 %collective-permute-start.5 = (bf16[256,512]{1,0:T(8,128)(2,1)S(1)}, bf16[256,512]{1,0:T(8,128)(2,1)S(1)}, u32[]{:S(2)}, u32[]{:S(2)}) collective-permute-start(bf16[256,512]{1,0:T(8,128)(2,1)S(1)} %fusion.21), channel_id=1, source_target_pairs={{0,6},{2,4},{4,2},{6,0},{8,14},{10,12},{12,10},{14,8},{16,22},{18,... | collective-permute-start | bytes 786440 | tf_op jit(solution)/shard_map/ppermute | solution.py:27
  128.2 15.2 %collective-permute-start.10 = (bf16[2,256,512]{2,1,0:T(8,128)(2,1)}, bf16[2,256,512]{2,1,0:T(8,128)(2,1)}, u32[]{:S(2)}, u32[]{:S(2)}) collective-permute-start(bf16[2,256,512]{2,1,0:T(8,128)(2,1)} %copy-done.2), channel_id=1, source_target_pairs={{0,2},{2,0},{4,6},{6,4},{8,10},{10,8},{12,14},{14,12},{16,18},{18,... | collective-permute-start | bytes 1572872 | tf_op jit(solution)/shard_map/ppermute | solution.py:27
  129.7 22.0 %collective-permute-start.11 = (bf16[2,256,512]{2,1,0:T(8,128)(2,1)}, bf16[2,256,512]{2,1,0:T(8,128)(2,1)}, u32[]{:S(2)}, u32[]{:S(2)}) collective-permute-start(bf16[2,256,512]{2,1,0:T(8,128)(2,1)} %copy-done.1), channel_id=1, source_target_pairs={{0,4},{2,6},{4,0},{6,2},{8,12},{10,14},{12,8},{14,10},{16,20},{18,... | collective-permute-start | bytes 1572872 | tf_op jit(solution)/shard_map/ppermute | solution.py:27
  131.2 21.6 %collective-permute-start.12 = (bf16[2,256,512]{2,1,0:T(8,128)(2,1)S(1)}, bf16[2,256,512]{2,1,0:T(8,128)(2,1)}, u32[]{:S(2)}, u32[]{:S(2)}) collective-permute-start(bf16[2,256,512]{2,1,0:T(8,128)(2,1)S(1)} %get-tuple-element.15), channel_id=1, source_target_pairs={{0,6},{2,4},{4,2},{6,0},{8,14},{10,12},{12,10},{14,8},{16,22},{18,... | collective-permute-start | bytes 1572872 | tf_op jit(solution)/shard_map/ppermute | solution.py:27
  131.7 66.3 %collective-permute-start.14 = (bf16[2,4,256,256]{3,2,1,0:T(8,128)(2,1)}, bf16[2,4,256,256]{3,2,1,0:T(8,128)(2,1)}, u32[]{:S(2)}, u32[]{:S(2)}) collective-permute-start(bf16[2,4,256,256]{3,2,1,0:T(8,128)(2,1)} %copy-done), channel_id=1, source_target_pairs={{8,0},{10,2},{12,4},{14,6},{16,8},{18,10},{20,12},{22,14},{24,16},... | collective-permute-start | bytes 3145736 | tf_op jit(solution)/shard_map/ppermute | solution.py:23
  164.0 40.1 %collective-permute-start.13 = (bf16[1344,256]{1,0:T(8,128)(2,1)}, bf16[1344,256]{1,0:T(8,128)(2,1)S(1)}, u32[]{:S(2)}, u32[]{:S(2)}) collective-permute-start(bf16[1344,256]{1,0:T(8,128)(2,1)} %copy.20), channel_id=1, source_target_pairs={{0,1},{1,0},{2,3},{3,2},{4,5},{5,4},{6,7},{7,6},{8,9},{9,8},{10,11... | collective-permute-start | bytes 2064392 | tf_op jit(solution)/shard_map/ppermute | solution.py:27
  200.4 8.1 %collective-permute-start.15 = (bf16[2,256,256]{2,1,0:T(8,128)(2,1)}, bf16[2,256,256]{2,1,0:T(8,128)(2,1)}, u32[]{:S(2)}, u32[]{:S(2)}) collective-permute-start(bf16[2,256,256]{2,1,0:T(8,128)(2,1)} %get-tuple-element.33), channel_id=1, source_target_pairs={{0,2},{2,0},{4,6},{6,4},{8,10},{10,8},{12,14},{14,12},{16,18},{18,... | collective-permute-start | bytes 786440 | tf_op jit(solution)/shard_map/ppermute | solution.py:27
  201.9 7.5 %collective-permute-start.16 = (bf16[2,256,256]{2,1,0:T(8,128)(2,1)}, bf16[2,256,256]{2,1,0:T(8,128)(2,1)}, u32[]{:S(2)}, u32[]{:S(2)}) collective-permute-start(bf16[2,256,256]{2,1,0:T(8,128)(2,1)} %get-tuple-element.32), channel_id=1, source_target_pairs={{0,4},{2,6},{4,0},{6,2},{8,12},{10,14},{12,8},{14,10},{16,20},{18,... | collective-permute-start | bytes 786440 | tf_op jit(solution)/shard_map/ppermute | solution.py:27
  203.4 11.2 %collective-permute-start.17 = (bf16[2,256,256]{2,1,0:T(8,128)(2,1)}, bf16[2,256,256]{2,1,0:T(8,128)(2,1)S(1)}, u32[]{:S(2)}, u32[]{:S(2)}) collective-permute-start(bf16[2,256,256]{2,1,0:T(8,128)(2,1)} %get-tuple-element.31), channel_id=1, source_target_pairs={{0,6},{2,4},{4,2},{6,0},{8,14},{10,12},{12,10},{14,8},{16,22},{18,... | collective-permute-start | bytes 786440 | tf_op jit(solution)/shard_map/ppermute | solution.py:27
  215.8 5.7 %collective-permute-start.22 = (bf16[168,512]{1,0:T(8,128)(2,1)S(1)}, bf16[168,512]{1,0:T(8,128)(2,1)S(1)}, u32[]{:S(2)}, u32[]{:S(2)}) collective-permute-start(bf16[168,512]{1,0:T(8,128)(2,1)S(1)} %get-tuple-element.40), channel_id=1, source_target_pairs={{0,2},{2,0},{4,6},{6,4},{8,10},{10,8},{12,14},{14,12},{16,18},{18,... | collective-permute-start | bytes 516104 | tf_op jit(solution)/shard_map/ppermute | solution.py:27
  218.2 7.2 %collective-permute-start.23 = (bf16[168,512]{1,0:T(8,128)(2,1)S(1)}, bf16[168,512]{1,0:T(8,128)(2,1)S(1)}, u32[]{:S(2)}, u32[]{:S(2)}) collective-permute-start(bf16[168,512]{1,0:T(8,128)(2,1)S(1)} %get-tuple-element.39), channel_id=1, source_target_pairs={{0,4},{2,6},{4,0},{6,2},{8,12},{10,14},{12,8},{14,10},{16,20},{18,... | collective-permute-start | bytes 516104 | tf_op jit(solution)/shard_map/ppermute | solution.py:27
  218.9 6.6 %collective-permute-start.24 = (bf16[168,512]{1,0:T(8,128)(2,1)S(1)}, bf16[168,512]{1,0:T(8,128)(2,1)S(1)}, u32[]{:S(2)}, u32[]{:S(2)}) collective-permute-start(bf16[168,512]{1,0:T(8,128)(2,1)S(1)} %get-tuple-element.38), channel_id=1, source_target_pairs={{0,6},{2,4},{4,2},{6,0},{8,14},{10,12},{12,10},{14,8},{16,22},{18,... | collective-permute-start | bytes 516104 | tf_op jit(solution)/shard_map/ppermute | solution.py:27
  (9 other events, 25.5 us)
Sparse Core Ops, SparseCore 0:
  128.3 73.3 reduce-scatter.1

commit v2 on v1

--- a/solution.py
+++ b/solution.py
@@ -27,19 +27,24 @@
     return lax.ppermute(shard, axis, [(i, i ^ by) for i in range(lax.axis_size(axis))])
 
 
-def attention_kernel(rows, info, *refs):
-    q_refs, g_refs = refs[:GROUP], refs[GROUP : 2 * GROUP]
-    k_own, v_own, k_far, v_far = refs[2 * GROUP : 2 * GROUP + 4]
-    outs = refs[2 * GROUP + 4 :]
+SMEM = pl.BlockSpec(memory_space=pltpu.SMEM)
+ANY = pl.BlockSpec(memory_space=pl.ANY)
+
+
+def attention_kernel(rows, skip, info, *refs):
+    q_refs = refs[:GROUP]
+    k_own, v_own, k_far, v_far = refs[GROUP : GROUP + 4]
+    outs = refs[GROUP + 4 + skip :]
     back_refs = outs[:GROUP]
     attn_cat, kv_own, kv_far = outs[GROUP : GROUP + 3]
     q_all, g_all, k_all, v_all, k_tr, v_tr, k_acc, v_acc, back = outs[GROUP + 3 :]
     r, tp = info[0], info[1]
-    heads = q_refs[0].shape[1] // HEAD
+    width = q_refs[0].shape[1] // 2
+    heads = width // HEAD
     half = rows // 2
     for m in range(GROUP):
-        q_all[m] = q_refs[m][...]
-        g_all[m] = g_refs[m][...]
+        q_all[m] = q_refs[m][:, :width]
+        g_all[m] = q_refs[m][:, width:]
         spot = r ^ m
         for place, k, v in ((spot, k_far, v_far), (spot + GROUP, k_own, v_own)):
             k_all[place] = k[m]
@@ -57,7 +62,7 @@
 
     def block(m, carry):
         first = r ^ m
-        own_doc = info[2 + first + GROUP]
+        own_doc = info[3 + first + GROUP]
         for h in range(heads):
             cols = slice(h * HEAD, (h + 1) * HEAD)
             q = q_all[m, :, cols]
@@ -70,7 +75,7 @@
                 if j == GROUP:
                     s = jnp.where(key_at <= query_at, s, HIDDEN)
                 else:
-                    s = s + jnp.where(info[2 + first + j] == own_doc, 0.0, HIDDEN)
+                    s = s + jnp.where(info[3 + first + j] == own_doc, 0.0, HIDDEN)
                 scores.append(s)
             top = functools.reduce(jnp.maximum, [jnp.max(s, axis=0, keepdims=True) for s in scores])
             top = top * (query_scale * LOG2E)
@@ -115,32 +120,31 @@
         attn_cat[at : at + half] = back[m, 0, pl.ds(away, half), :]
 
 
-def attention(info, queries, d_attn, kv_own, kv_far):
-    rows, q_width = queries[0].shape
-    kv_heads = kv_own.shape[2] // HEAD // 2
-    q_block = q_width // kv_heads
-    q_spec = pl.BlockSpec((rows, q_block), lambda g: (0, g))
-    k_spec = pl.BlockSpec((GROUP, rows, HEAD), lambda g: (0, 0, g))
-    v_spec = pl.BlockSpec((GROUP, rows, HEAD), lambda g: (0, 0, g + kv_heads))
-    back_spec = pl.BlockSpec((2, rows, q_block), lambda g: (0, 0, g))
-    kv_spec = pl.BlockSpec((2, GROUP, rows, HEAD), lambda g: (0, 0, 0, g))
-    kv_shape = (2, GROUP, rows, kv_heads * HEAD)
+def entire(array):
+    return pl.BlockSpec(array.shape, lambda i: (0,) * len(array.shape))
+
+
+def attention(info, q_and_d, kv_own, kv_far, after=()):
+    rows, q_block = q_and_d[0].shape[0], q_and_d[0].shape[1] // 2
+    k_spec = pl.BlockSpec((GROUP, rows, HEAD), lambda i: (0, 0, 0))
+    v_spec = pl.BlockSpec((GROUP, rows, HEAD), lambda i: (0, 0, 1))
+    kv_shape = (2, GROUP, rows, HEAD)
     bf16 = jnp.bfloat16
     blocks = 2 * GROUP
+    out = [jax.ShapeDtypeStruct((2, rows, q_block), bf16)] * GROUP + [
+        jax.ShapeDtypeStruct((GROUP * rows, q_block), bf16),
+        jax.ShapeDtypeStruct(kv_shape, jnp.float32),
+        jax.ShapeDtypeStruct(kv_shape, bf16),
+    ]
     return pl.pallas_call(
-        functools.partial(attention_kernel, rows),
-        grid=(kv_heads,),
-        in_specs=[pl.BlockSpec(memory_space=pltpu.SMEM)]
-        + [q_spec] * (2 * GROUP)
-        + [k_spec, v_spec, k_spec, v_spec],
-        out_specs=[back_spec] * GROUP
-        + [pl.BlockSpec((GROUP * rows, q_block), lambda g: (0, g)), kv_spec, kv_spec],
-        out_shape=[jax.ShapeDtypeStruct((2, rows, q_width), bf16)] * GROUP
-        + [
-            jax.ShapeDtypeStruct((GROUP * rows, q_width), bf16),
-            jax.ShapeDtypeStruct(kv_shape, jnp.float32),
-            jax.ShapeDtypeStruct(kv_shape, bf16),
-        ],
+        functools.partial(attention_kernel, rows, len(after)),
+        grid=(1,),
+        in_specs=[SMEM]
+        + [entire(a) for a in q_and_d]
+        + [k_spec, v_spec, k_spec, v_spec]
+        + [ANY] * len(after),
+        out_specs=[entire(a) for a in out],
+        out_shape=out,
         scratch_shapes=[
             pltpu.VMEM((GROUP, rows, q_block), bf16),
             pltpu.VMEM((GROUP, rows, q_block), bf16),
@@ -152,13 +156,182 @@
             pltpu.VMEM((blocks, rows, HEAD), jnp.float32),
             pltpu.VMEM((GROUP, 2, rows, q_block), bf16),
         ],
-        compiler_params=pltpu.CompilerParams(vmem_limit_bytes=40 * 1024 * 1024),
+        compiler_params=pltpu.CompilerParams(vmem_limit_bytes=32 * 1024 * 1024),
         cost_estimate=pl.CostEstimate(
-            flops=12 * q_width * GROUP * rows * (GROUP + 1) * rows,
-            bytes_accessed=10 * 1024 * 1024,
+            flops=12 * q_block * GROUP * rows * (GROUP + 1) * rows,
+            bytes_accessed=5 * 1024 * 1024,
             transcendentals=0,
         ),
-    )(info, *queries, *d_attn, kv_own, kv_own, kv_far, kv_far)
+    )(info, *q_and_d, kv_own, kv_own, kv_far, kv_far, *after)
+
+
+def moved(body, info, arrays, out, after=()):
+    n = len(arrays)
+
+    def kernel(info_ref, *refs):
+        body(info_ref, refs[:n], refs[n + len(after) :])
+
+    size = sum(a.size * a.dtype.itemsize for a in list(arrays) + list(out))
+    return pl.pallas_call(
+        kernel,
+        grid=(1,),
+        in_specs=[SMEM] + [entire(a) for a in arrays] + [ANY] * len(after),
+        out_specs=[entire(a) for a in out],
+        out_shape=list(out),
+        compiler_params=pltpu.CompilerParams(vmem_limit_bytes=32 * 1024 * 1024),
+        cost_estimate=pl.CostEstimate(flops=0, bytes_accessed=size, transcendentals=0),
+    )(info, *arrays, *after)
+
+
+def columns(ref, start, width):
+    return ref[:, pl.ds(pl.multiple_of(start, HEAD), width)]
+
+
+def project_back(info, out_grad, out_weight):
+    rows, d_out = out_grad.shape
+    per = 2
+    steps = GROUP * per
+    block = out_weight.shape[0] // steps
+
+    def kernel(info_ref, grad, weight, *outs):
+        step = pl.program_id(0)
+        part = lax.dot_general(
+            grad[...], weight[...], (((1,), (1,)), ((), ())), preferred_element_type=jnp.float32
+        ).astype(jnp.bfloat16)
+        for at in range(steps):
+
+            @pl.when(step == at)
+            def _():
+                outs[at][...] = part
+
+    def weight_block(step, info_ref):
+        return ((info_ref[0] ^ (step % GROUP)) * per + step // GROUP, 0)
+
+    outs = pl.pallas_call(
+        kernel,
+        grid_spec=pltpu.PrefetchScalarGridSpec(
+            num_scalar_prefetch=1,
+            grid=(steps,),
+            in_specs=[
+                pl.BlockSpec((rows, d_out), lambda i, info_ref: (0, 0)),
+                pl.BlockSpec((block, d_out), weight_block),
+            ],
+            out_specs=[pl.BlockSpec((rows, block), lambda i, info_ref: (0, 0))] * steps,
+        ),
+        out_shape=[jax.ShapeDtypeStruct((rows, block), jnp.bfloat16)] * steps,
+        compiler_params=pltpu.CompilerParams(vmem_limit_bytes=32 * 1024 * 1024),
+        cost_estimate=pl.CostEstimate(
+            flops=2 * rows * out_weight.size, bytes_accessed=2 * out_weight.size, transcendentals=0
+        ),
+    )(info, out_grad, out_weight)
+    return [outs[g * GROUP : (g + 1) * GROUP] for g in range(per)]
+
+
+def weight_terms(info, pieces, attn_cat):
+    d_out, width = pieces[0].shape[1], attn_cat.shape[1]
+    block = 3 * HEAD if d_out % (3 * HEAD) == 0 else d_out
+    steps, cut = d_out // block, d_out // GROUP
+
+    def kernel(info_ref, *refs):
+        inputs, attn = refs[: len(pieces)], refs[len(pieces)]
+        own, other, away, whole = refs[len(pieces) + 1 :]
+        total, at = None, 0
+        for piece in inputs:
+            rows = piece.shape[0]
+            term = lax.dot_general(
+                piece[...],
+                attn[at : at + rows],
+                (((0,), (0,)), ((), ())),
+                preferred_element_type=jnp.float32,
+            )
+            total, at = term if total is None else total + term, at + rows
+        step = pl.program_id(0)
+        whole[pl.ds(pl.multiple_of(step * block, block), block)] = total.astype(whole.dtype)
+
+        @pl.when(step == steps - 1)
+        def _():
+            def chunk(m):
+                return whole[pl.ds(pl.multiple_of((info_ref[2] ^ m) * cut, 16), cut)]
+
+            own[...] = chunk(0)
+            other[...] = chunk(2)
+            away[0] = chunk(1)
+            away[1] = chunk(3)
+
+    shapes = [(cut, width), (cut, width), (2, cut, width)]
+    out = [jax.ShapeDtypeStruct(s, jnp.bfloat16) for s in shapes]
+    return pl.pallas_call(
+        kernel,
+        grid=(steps,),
+        in_specs=[SMEM]
+        + [pl.BlockSpec((p.shape[0], block), lambda i: (0, i)) for p in pieces]
+        + [entire(attn_cat)],
+        out_specs=[entire(a) for a in out],
+        out_shape=out,
+        scratch_shapes=[pltpu.VMEM((d_out, width), jnp.bfloat16)],
+        compiler_params=pltpu.CompilerParams(vmem_limit_bytes=32 * 1024 * 1024),
+        cost_estimate=pl.CostEstimate(
+            flops=2 * attn_cat.size * d_out,
+            bytes_accessed=2 * (attn_cat.shape[0] + width) * d_out,
+            transcendentals=0,
+        ),
+    )(info, *pieces, attn_cat)
+
+
+def split_sum(info, own, met):
+    rows, width = own.shape
+    cut = rows // GROUP
+
+    def kernel(info_ref, own_ref, met_ref, *refs):
+        outs, total = refs[:GROUP], refs[GROUP]
+        total[...] = own_ref[...].astype(jnp.float32) + met_ref[...].astype(jnp.float32)
+        for m in range(GROUP):
+            start = pl.multiple_of((info_ref[0] ^ m) * cut, 8)
+            outs[m][...] = total[pl.ds(start, cut)].astype(outs[m].dtype)
+
+    out = [jax.ShapeDtypeStruct((cut, width), jnp.bfloat16)] * GROUP
+    return pl.pallas_call(
+        kernel,
+        grid=(1,),
+        in_specs=[SMEM, entire(own), entire(met)],
+        out_specs=[entire(a) for a in out],
+        out_shape=out,
+        scratch_shapes=[pltpu.VMEM((rows, width), jnp.float32)],
+        compiler_params=pltpu.CompilerParams(vmem_limit_bytes=32 * 1024 * 1024),
+    )(info, own, met)
+
+
+def project(info, attn, out_weight):
+    rows, depth = attn.shape
+    d_out = out_weight.shape[1]
+    block = 3 * HEAD if d_out % (3 * HEAD) == 0 else d_out
+    steps, half = d_out // block, d_out // 2
+
+    def kernel(info_ref, attn_ref, weight, mine, theirs, whole):
+        step = pl.program_id(0)
+        part = jnp.dot(attn_ref[...], weight[...], preferred_element_type=jnp.float32)
+        whole[pl.ds(pl.multiple_of(step * block, block), block)] = part.T
+
+        @pl.when(step == steps - 1)
+        def _():
+            tp = info_ref[1]
+            mine[...] = whole[pl.ds(pl.multiple_of(tp * half, 8), half)]
+            other = whole[pl.ds(pl.multiple_of((1 - tp) * half, 8), half)]
+            theirs[...] = other.astype(theirs.dtype)
+
+    out = [jax.ShapeDtypeStruct((half, rows), d) for d in (jnp.float32, jnp.bfloat16)]
+    return pl.pallas_call(
+        kernel,
+        grid=(steps,),
+        in_specs=[SMEM, entire(attn), pl.BlockSpec((depth, block), lambda i: (0, i))],
+        out_specs=[entire(a) for a in out],
+        out_shape=out,
+        scratch_shapes=[pltpu.VMEM((d_out, rows), jnp.float32)],
+        compiler_params=pltpu.CompilerParams(vmem_limit_bytes=32 * 1024 * 1024),
+        cost_estimate=pl.CostEstimate(
+            flops=2 * attn.size * d_out, bytes_accessed=2 * out_weight.size, transcendentals=0
+        ),
+    )(info, attn, out_weight)
 
 
 def grouped(queries, keys, values, out_weight, out_grad, block_doc):
@@ -168,74 +341,128 @@
     r, layer = me % GROUP, me // GROUP
     members = range(GROUP)
     q_width, kv_width = queries.shape[1] // GROUP, keys.shape[1] // GROUP
+    kv_heads = kv_width // HEAD
+    head_width = q_width // kv_heads
     d_out = out_grad.shape[1]
-
-    def part(array, m, width, dim):
-        return lax.dynamic_slice_in_dim(array, (r ^ m) * width, width, dim)
+    doc_padded = jnp.concatenate([jnp.full((GROUP,), -1, jnp.int32), block_doc])
+    docs = lax.dynamic_slice_in_dim(doc_padded, layer * GROUP, 2 * GROUP, 0)
+    info = jnp.concatenate([jnp.stack([r, tp, layer]).astype(jnp.int32), docs])
+
+    def shape(*dims, dtype=bf16):
+        return jax.ShapeDtypeStruct(dims, dtype)
 
     def traded(blocks):
         return [blocks[0]] + [swapped(blocks[m], "ctx", m) for m in members[1:]]
 
-    def in_order(blocks, dim):
-        width = blocks[0].shape[dim]
-        shape = list(blocks[0].shape)
-        shape[dim] = width * GROUP
-        whole = jnp.zeros(shape, blocks[0].dtype)
+    def pack_kv(info_ref, ins, outs):
         for m in members:
-            whole = lax.dynamic_update_slice_in_dim(whole, blocks[m], (r ^ m) * width, dim)
-        return whole
-
-    kv = traded(
-        [
-            jnp.concatenate([part(keys, m, kv_width, 1), part(values, m, kv_width, 1)], axis=1)
-            for m in members
-        ]
-    )
-    kv_own = jnp.stack(kv)
-    kv_far = shifted(kv_own, "ctx", GROUP)
-    q = traded([part(queries, m, q_width, 1) for m in members])
-    d_attn = traded(
-        [
-            jnp.einsum(
-                "te,re->tr", out_grad, part(out_weight, m, q_width, 0), preferred_element_type=f32
-            ).astype(bf16)
-            for m in members
-        ]
-    )
-    half = lax.dynamic_slice_in_dim(out_grad, tp * (rows // 2), rows // 2, 0)
-    near = jnp.concatenate([swapped(half, "ctx", m) for m in members[1:]], axis=0)
-    away = swapped(near, "tp", 1)
-    grad_cat = jnp.concatenate([out_grad, near, away], axis=0)
-
-    doc_padded = jnp.concatenate([jnp.full((GROUP,), -1, jnp.int32), block_doc])
-    docs = lax.dynamic_slice_in_dim(doc_padded, layer * GROUP, 2 * GROUP, 0)
-    info = jnp.concatenate([jnp.stack([r, tp]).astype(jnp.int32), docs])
-    *back, attn_cat, own_grad, far_grad = attention(info, q, d_attn, kv_own, kv_far)
-
-    weight_terms = jnp.einsum("te,th->eh", grad_cat, attn_cat, preferred_element_type=f32)
-    layers = lax.axis_size("ctx") // GROUP
-    columns = [[i * GROUP + j for i in range(layers)] for j in members]
-    weight_sums = lax.psum_scatter(
-        weight_terms.astype(bf16),
-        "ctx",
-        scatter_dimension=0,
-        axis_index_groups=columns,
-        tiled=True,
-    )
-    cut = weight_sums.shape[0] // GROUP
-    weight_blocks = traded([part(weight_sums, m, cut, 0) for m in members])
-    out_weight_grad = in_order([b.astype(f32) for b in weight_blocks], 1).T
-
-    back = in_order(traded(back), 2)
-    attn, query_grad = back[0], back[1]
-    terms = jnp.einsum("re,tr->et", out_weight, attn, preferred_element_type=f32)
-    mine = lax.dynamic_slice_in_dim(terms, tp * (d_out // 2), d_out // 2, 0)
-    theirs = lax.dynamic_slice_in_dim(terms, (1 - tp) * (d_out // 2), d_out // 2, 0)
-    attn_output = (mine + swapped(theirs.astype(bf16), "tp", 1).astype(f32)).astype(bf16).T
-
-    total = (own_grad + shifted(far_grad, "ctx", -GROUP).astype(f32)).astype(bf16)
-    total = in_order(traded([total[:, m] for m in members]), 2)
-    return (attn_output, query_grad, total[0], total[1], out_weight_grad)
+            start = (info_ref[0] ^ m) * kv_width
+            for i in range(2):
+                outs[m][:, i * kv_width : (i + 1) * kv_width] = columns(ins[i], start, kv_width)
+
+    kv = traded(moved(pack_kv, info, [keys, values], [shape(rows, 2 * kv_width)] * GROUP))
+
+    def pack_heads(info_ref, ins, outs):
+        for m in members:
+            for g in range(kv_heads):
+                for i in range(2):
+                    at = (i * kv_heads + g) * HEAD
+                    outs[g][m, :, i * HEAD : (i + 1) * HEAD] = ins[m][:, at : at + HEAD]
+
+    d_attn = project_back(info, out_grad, out_weight)
+    heads_shape = [shape(GROUP, rows, 2 * HEAD)] * kv_heads
+    kv_own = moved(pack_heads, info, kv, heads_shape, d_attn[0])
+    kv_far = [shifted(a, "ctx", GROUP) for a in kv_own]
+
+    def pack_queries(g, after):
+        def body(info_ref, ins, outs):
+            for m in members:
+                start = (info_ref[0] ^ m) * q_width + g * head_width
+                outs[m][:, :head_width] = columns(ins[0], start, head_width)
+                outs[m][:, head_width:] = ins[1 + m][...]
+
+        return traded(
+            moved(body, info, [queries, *d_attn[g]], [shape(rows, 2 * head_width)] * GROUP, after)
+        )
+
+    def pack_half(info_ref, ins, outs):
+        outs[0][...] = ins[0][pl.ds(pl.multiple_of(info_ref[1] * (rows // 2), 16), rows // 2), :]
+
+    q_and_d = [pack_queries(0, kv[1:])]
+    half = moved(pack_half, info, [out_grad], [shape(rows // 2, d_out)], [*q_and_d[0][1:], kv_far[0]])[0]
+    near = traded([half] * GROUP)[1:]
+    q_and_d += [pack_queries(g, near) for g in range(1, kv_heads)]
+
+    def pack_near(info_ref, ins, outs):
+        for i in range(GROUP - 1):
+            outs[0][i * (rows // 2) : (i + 1) * (rows // 2)] = ins[i][...]
+
+    back, own_grads, far_grads, all_terms = [], [], [], []
+    pieces, after = None, kv_far[1:]
+    for g in range(kv_heads):
+        *blocks, attn_cat, own_grad, far_grad = attention(
+            info, q_and_d[g], kv_own[g], kv_far[g], after
+        )
+        far_grads.append(shifted(far_grad, "ctx", -GROUP))
+        if pieces is None:
+            near_shape = shape((GROUP - 1) * (rows // 2), d_out)
+            near = moved(pack_near, info, near, [near_shape], [attn_cat])[0]
+            pieces = [out_grad, near, swapped(near, "tp", 1)]
+        terms = weight_terms(info, pieces, attn_cat)
+        after = [*terms, *far_grads]
+        all_terms.append(terms)
+        back += traded(blocks)
+        own_grads.append(own_grad)
+
+    def add_pair(info_ref, ins, outs):
+        for i in range(2):
+            outs[i][...] = (ins[i][...].astype(f32) + ins[2][i].astype(f32)).astype(outs[i].dtype)
+
+    weight_blocks = []
+    for own, other, away in all_terms:
+        met = swapped(away, "ctx", GROUP)
+        pair_shape = [shape(*own.shape, dtype=f32), shape(*own.shape)]
+        own, other = moved(add_pair, info, [own, other, met], pair_shape, all_terms[-1][:1])
+        weight_blocks += traded(split_sum(info, own, swapped(other, "ctx", 2 * GROUP)))
+
+    def lay_out(info_ref, ins, outs):
+        for g in range(kv_heads):
+            for m in members:
+                start = pl.multiple_of((info_ref[0] ^ m) * q_width + g * head_width, HEAD)
+                block = ins[g * GROUP + m]
+                for i, out in enumerate(outs):
+                    piece = block[...] if len(block.shape) == 2 else block[i]
+                    out[:, pl.ds(start, head_width)] = piece.astype(out.dtype)
+
+    attn, query_grad = moved(lay_out, info, back, [shape(rows, GROUP * q_width)] * 2, [other])
+    mine, theirs = project(info, attn, out_weight)
+
+    def add_shares(info_ref, ins, outs):
+        outs[0][...] = (ins[0][...] + ins[1][...].astype(f32)).astype(bf16)
+
+    theirs = swapped(theirs, "tp", 1)
+    attn_output = moved(add_shares, info, [mine, theirs], [shape(d_out // 2, rows)])[0]
+
+    def add_up(info_ref, ins, outs):
+        for g in range(kv_heads):
+            for m in members:
+                for i in range(2):
+                    at = (i * kv_heads + g) * HEAD
+                    total = ins[g][i, m] + ins[kv_heads + g][i, m].astype(f32)
+                    outs[m][:, at : at + HEAD] = total.astype(bf16)
+
+    def lay_out_kv(info_ref, ins, outs):
+        for m in members:
+            start = pl.multiple_of((info_ref[0] ^ m) * kv_width, HEAD)
+            for i in range(2):
+                outs[i][:, pl.ds(start, kv_width)] = ins[m][:, i * kv_width : (i + 1) * kv_width]
+
+    totals = moved(add_up, info, own_grads + far_grads, [shape(rows, 2 * kv_width)] * GROUP)
+    key_grad, value_grad = moved(lay_out_kv, info, traded(totals), [shape(rows, GROUP * kv_width)] * 2)
+    out_weight_grad = moved(
+        lay_out, info, weight_blocks, [shape(d_out // GROUP // GROUP, GROUP * q_width, dtype=f32)]
+    )[0].T
+    return (attn_output.T, query_grad, key_grad, value_grad, out_weight_grad)
 
 
 def single(queries, keys, values, out_weight, out_grad, block_doc):
@@ -327,9 +554,9 @@
 
 def local(queries, keys, values, out_weight, out_grad, block_doc):
     fits = (
-        lax.axis_size("ctx") % GROUP == 0
+        lax.axis_size("ctx") == GROUP * GROUP
         and queries.shape[0] * GROUP == WINDOW
-        and keys.shape[1] % (GROUP * HEAD) == 0
+        and keys.shape[1] == 2 * GROUP * HEAD
         and lax.axis_size("tp") == 2
     )
     step = grouped if fits else single

time: 236 us -> 191 us (0.81)
  Pallas kernels: 33.7 us -> 69.5 us
  waiting for transfers between devices: 91.1 us -> 59.4 us
  matrix products: 24.6 us -> 0 us
  starting transfers between devices: 31.8 us -> 52.4 us
  local copies, waits for them, and re-layouts: 28.3 us -> 8.31 us
  between operations: 14.5 us -> 0.94 us
  other arithmetic: 9.55 us -> 0.08 us
    pallas_call x1 -> x21, Pallas kernels: 33.7 us -> 69.5 us  [the longest x2 33.3 us: attention(): pl.pallas_call(functools.partial(attention_kernel, rows, len(after)), gri...]
    dot_general x6 -> x0, matrix products: 24.6 us -> none  [the longest x4 13 us: grouped(): jnp.einsum('te,re->tr', out_grad, part(out_weight, m, q_width, 0), prefer...]
    ppermute x2 -> x4, waiting for transfers between devices: 37.9 us -> 14.7 us  [shifted(): return lax.ppermute(shard, axis, pairs)]
    ppermute x23 -> x33, starting transfers between devices: 25.8 us -> 42.6 us  [swapped(): lax.ppermute(shard, axis, [(i, i ^ by) for i in range(lax.axis_size(axis))])]
    ppermute x23 -> x33, waiting for transfers between devices: 53.1 us -> 44.7 us  [swapped(): lax.ppermute(shard, axis, [(i, i ^ by) for i in range(lax.axis_size(axis))])]
    dynamic_slice x4 -> x0, local copies, waits for them, and re-layouts: 7.44 us -> none  [the longest x3 5.44 us: part(): return lax.dynamic_slice_in_dim(array, (r ^ m) * width, width, dim)]
    dynamic_update_slice x8 -> x0, local copies, waits for them, and re-layouts: 5.38 us -> none  [in_order(): lax.dynamic_update_slice_in_dim(whole, blocks[m], (r ^ m) * width, dim)]
    squeeze x3 -> x0, local copies, waits for them, and re-layouts: 4.23 us -> none  [the longest x1 2.3 us: grouped(): attn, query_grad = (back[0], back[1])]
  transfers between devices with their start and end apart: 26 -> 37, of which waited for: 13 -> 16; matrix products, arithmetic and copies ran while one was open for 21% -> 0% of each run, Pallas kernels for 14% -> 23%
where the time goes in v2:
time: 191 us
  Pallas kernels  69.5 us (36%)
  waiting for transfers between devices  59.4 us (31%)
  starting transfers between devices  52.4 us (27%)
  local copies, waits for them, and re-layouts  8.31 us (4%)
    ppermute x33, waiting for transfers between devices, swapped(): lax.ppermute(shard, axis, [(i, i ^ by) for i in range(lax.axis_size(axis))])  44.7 us
    ppermute x33, starting transfers between devices, swapped(): lax.ppermute(shard, axis, [(i, i ^ by) for i in range(lax.axis_size(axis))])  42.6 us
    pallas_call x2, Pallas kernels, attention(): pl.pallas_call(functools.partial(attention_kernel, rows, len(after)), gri...  33.3 us
    ppermute x4, waiting for transfers between devices, shifted(): return lax.ppermute(shard, axis, pairs)  14.7 us
    pallas_call x13, Pallas kernels, moved(): pl.pallas_call(kernel, grid=(1,), in_specs=[SMEM] + [entire(a) for a in a...  12.7 us
    ppermute x4, starting transfers between devices, shifted(): return lax.ppermute(shard, axis, pairs)  9.74 us
    pallas_call x2, Pallas kernels, weight_terms(): pl.pallas_call(kernel, grid=(steps,), in_specs=[SMEM] + [pl.BlockSpec((p....  9.06 us
    unnamed x18, local copies, waits for them, and re-layouts  7.57 us
  transfers between devices with their start and end apart: 37, of which 16 were waited for; matrix products, arithmetic and copies ran while one was open for 0% of the time, Pallas kernels for 23%

profile of v2, /device:TPU:0, one launch (start us, length us, event | category | flops | bytes accessed | tf_op | source)
XLA Modules:
  0.0 190.6 jit_solution(1601273632578900027)
XLA Ops:
  4.2 3.0 %collective-permute-start = (bf16[256,512]{1,0:T(8,128)(2,1)S(1)}, bf16[256,512]{1,0:T(8,128)(2,1)S(1)}, u32[]{:S(2)}, u32[]{:S(2)}) collective-permute-start(bf16[256,512]{1,0:T(8,128)(2,1)S(1)} %get-tuple-element.73), channel_id=1, source_target_pairs={{0,2},{2,0},{4,6},{6,4},{8,10},{10,8},{12,14},{14,12},{16,18},{18,... | collective-permute-start | bytes 786440 | tf_op jit(solution)/shard_map/ppermute | solution.py:27
  8.8 4.1 %copy-done = bf16[2048,2688]{1,0:T(8,128)(2,1)S(1)} copy-done((bf16[2048,2688]{1,0:T(8,128)(2,1)S(1)}, bf16[2048,2688]{1,0:T(8,128)(2,1)}, u32[]{:S(2)}) %copy-start) | copy-done | bytes 11010072
  14.3 5.6 %shard_map.101 = (bf16[256,256]{1,0:T(8,128)(2,1)S(1)}, bf16[256,256]{1,0:T(8,128)(2,1)S(1)}, bf16[256,256]{1,0:T(8,128)(2,1)S(1)}, bf16[256,256]{1,0:T(8,128)(2...) custom-call(s32[11]{0:T(128)S(1)} %pad_add_fusion.info_ref.info, ...), custom_call_target="tpu_custom_call" | custom-call | flops 2818572288 | bytes 11010048 | tf_op jit(solution)/shard_map/pallas_call | solution.py:210
  21.4 3.5 %collective-permute-start.6 = (bf16[4,256,256]{2,1,0:T(8,128)(2,1)S(1)}, bf16[4,256,256]{2,1,0:T(8,128)(2,1)S(1)}, u32[]{:S(2)}, u32[]{:S(2)}) collective-permute-start(bf16[4,256,256]{2,1,0:T(8,128)(2,1)S(1)} %get-tuple-element.81.refs_4_.refs_5_), channel_id=1, source_target_pairs={{0,8},{2,10},{4,12},{6,14},{8,16},{10,18},{12,20},{14,22},{16,24},... | collective-permute-start | bytes 1572872 | tf_op jit(solution)/shard_map/ppermute | solution.py:23
  29.1 3.5 %collective-permute-start.7 = (bf16[4,256,256]{2,1,0:T(8,128)(2,1)S(1)}, bf16[4,256,256]{2,1,0:T(8,128)(2,1)S(1)}, u32[]{:S(2)}, u32[]{:S(2)}) collective-permute-start(bf16[4,256,256]{2,1,0:T(8,128)(2,1)S(1)} %get-tuple-element.82.refs_4_.refs_5_), channel_id=1, source_target_pairs={{0,8},{2,10},{4,12},{6,14},{8,16},{10,18},{12,20},{14,22},{16,24},... | collective-permute-start | bytes 1572872 | tf_op jit(solution)/shard_map/ppermute | solution.py:23
  32.6 2.3 %collective-permute-done.3.refs_1_ = bf16[256,512]{1,0:T(8,128)(2,1)S(1)} collective-permute-done((bf16[256,512]{1,0:T(8,128)(2,1)S(1)}, bf16[256,512]{1,0:T(8,128)(2,1)S(1)}, u32[]{:S(2)}, u32[]{:S(2)}) %collective-permute-start.3) | collective-permute-done | bytes 262176 | tf_op jit(solution)/shard_map/ppermute | solution.py:27
  34.9 4.2 %collective-permute-done.4.refs_2_ = bf16[256,512]{1,0:T(8,128)(2,1)S(1)} collective-permute-done((bf16[256,512]{1,0:T(8,128)(2,1)S(1)}, bf16[256,512]{1,0:T(8,128)(2,1)S(1)}, u32[]{:S(2)}, u32[]{:S(2)}) %collective-permute-start.4) | collective-permute-done | bytes 262176 | tf_op jit(solution)/shard_map/ppermute | solution.py:27
  43.2 2.9 %collective-permute-done.7.refs_8_.refs_6_.refs_7_ = bf16[4,256,256]{2,1,0:T(8,128)(2,1)S(1)} collective-permute-done((bf16[4,256,256]{2,1,0:T(8,128)(2,1)S(1)}, bf16[4,256,256]{2,1,0:T(8,128)(2,1)S(1)}, u32[]{:S(2)}, u32[]{:S(2)}) %collective-permute-start.7) | collective-permute-done | bytes 524320 | tf_op jit(solution)/shard_map/ppermute | solution.py:23
  46.2 16.6 %shard_map.105 = (bf16[2,256,256]{2,1,0:T(8,128)(2,1)S(1)}, bf16[2,256,256]{2,1,0:T(8,128)(2,1)S(1)}, bf16[2,256,256]{2,1,0:T(8,128)(2,1)S(1)}, bf16[2,256,256]{...) custom-call(s32[11]{0:T(128)S(1)} %pad_add_fusion.info_ref.info, ...), custom_call_target="tpu_custom_call" | custom-call | flops 4026531840 | bytes 5242880 | tf_op jit(solution)/shard_map/pallas_call | solution.py:139
  62.8 7.7 %collective-permute-done.12.refs_6_.refs_1_ = bf16[128,2688]{1,0:T(8,128)(2,1)S(1)} collective-permute-done((bf16[128,2688]{1,0:T(8,128)(2,1)S(1)}, bf16[128,2688]{1,0:T(8,128)(2,1)S(1)}, u32[]{:S(2)}, u32[]{:S(2)}) %collective-permute-start.12) | collective-permute-done | bytes 688160 | tf_op jit(solution)/shard_map/ppermute | solution.py:27
  75.3 1.7 collective-permute-start.16
  77.0 4.5 %shard_map.109 = (bf16[672,256]{1,0:T(8,128)(2,1)S(1)}, bf16[672,256]{1,0:T(8,128)(2,1)S(1)}, bf16[2,672,256]{2,1,0:T(8,128)(2,1)S(1)}) custom-call(s32[11]{0:T(128)S(1)} %pad_add_fusion.info_ref.info, bf16[256,2688]{1,0:T(8,128)(2,1)S(1)} %copy-done.2, bf16[384,2688]{1,0:T(8,128)(2,1)S(1)} %shard_map.108.refs_1_, ...), custom_call_target="tpu_custom_call" | custom-call | flops 1409286144 | bytes 6881280 | tf_op jit(solution)/shard_map/pallas_call | solution.py:263
  81.5 6.0 %collective-permute-done.18.refs_11_.refs_2_ = bf16[2,4,256,128]{3,2,1,0:T(8,128)(2,1)S(1)} collective-permute-done((bf16[2,4,256,128]{3,2,1,0:T(8,128)(2,1)S(1)}, bf16[2,4,256,128]{3,2,1,0:T(8,128)(2,1)S(1)}, u32[]{:S(2)}, u32[]{:S(2)}) %collective-permute-start.18) | collective-permute-done | bytes 524320 | tf_op jit(solution)/shard_map/ppermute | solution.py:23
  87.9 16.7 %shard_map.110 = (bf16[2,256,256]{2,1,0:T(8,128)(2,1)S(1)}, bf16[2,256,256]{2,1,0:T(8,128)(2,1)S(1)}, bf16[2,256,256]{2,1,0:T(8,128)(2,1)S(1)}, bf16[2,256,256]{...) custom-call(s32[11]{0:T(128)S(1)} %pad_add_fusion.info_ref.info, ...), custom_call_target="tpu_custom_call" | custom-call | flops 4026531840 | bytes 5242880 | tf_op jit(solution)/shard_map/pallas_call | solution.py:139
  104.6 4.5 %shard_map.111 = (bf16[672,256]{1,0:T(8,128)(2,1)S(1)}, bf16[672,256]{1,0:T(8,128)(2,1)S(1)}, bf16[2,672,256]{2,1,0:T(8,128)(2,1)S(1)}) custom-call(s32[11]{0:T(128)S(1)} %pad_add_fusion.info_ref.info, bf16[256,2688]{1,0:T(8,128)(2,1)S(1)} %copy-done.2, bf16[384,2688]{1,0:T(8,128)(2,1)S(1)} %shard_map.108.refs_1_, ...), custom_call_target="tpu_custom_call" | custom-call | flops 1409286144 | bytes 6881280 | tf_op jit(solution)/shard_map/pallas_call | solution.py:263
  109.1 2.4 %collective-permute-start.22 = (bf16[2,672,256]{2,1,0:T(8,128)(2,1)S(1)}, bf16[2,672,256]{2,1,0:T(8,128)(2,1)S(1)}, u32[]{:S(2)}, u32[]{:S(2)}) collective-permute-start(bf16[2,672,256]{2,1,0:T(8,128)(2,1)S(1)} %get-tuple-element.107), channel_id=1, source_target_pairs={{0,8},{2,10},{4,12},{6,14},{8,0},{10,2},{12,4},{14,6},{16,24},{18,... | collective-permute-start | bytes 2064392 | tf_op jit(solution)/shard_map/ppermute | solution.py:27
  115.0 1.7 collective-permute-start.19
  116.7 5.0 %collective-permute-done.10.refs_3_ = bf16[2,256,256]{2,1,0:T(8,128)(2,1)S(1)} collective-permute-done((bf16[2,256,256]{2,1,0:T(8,128)(2,1)S(1)}, bf16[2,256,256]{2,1,0:T(8,128)(2,1)S(1)}, u32[]{:S(2)}, u32[]{:S(2)}) %collective-permute-start.10) | collective-permute-done | bytes 262176 | tf_op jit(solution)/shard_map/ppermute | solution.py:27
  123.1 4.2 %collective-permute-done.8.refs_1_ = bf16[2,256,256]{2,1,0:T(8,128)(2,1)S(1)} collective-permute-done((bf16[2,256,256]{2,1,0:T(8,128)(2,1)S(1)}, bf16[2,256,256]{2,1,0:T(8,128)(2,1)S(1)}, u32[]{:S(2)}, u32[]{:S(2)}) %collective-permute-start.8) | collective-permute-done | bytes 262176 | tf_op jit(solution)/shard_map/ppermute | solution.py:27
  127.3 1.7 collective-permute-start.21
  131.1 1.8 collective-permute-done.19.refs_5_
  132.9 2.6 %collective-permute-start.33 = (bf16[672,256]{1,0:T(8,128)(2,1)S(1)}, bf16[672,256]{1,0:T(8,128)(2,1)S(1)}, u32[]{:S(2)}, u32[]{:S(2)}) collective-permute-start(bf16[672,256]{1,0:T(8,128)(2,1)S(1)} %get-tuple-element.108.refs_8_), channel_id=1, source_target_pairs={{0,16},{2,18},{4,20},{6,22},{8,24},{10,26},{12,28},{14,30},{16,0},... | collective-permute-start | bytes 1032200 | tf_op jit(solution)/shard_map/ppermute | solution.py:27
  136.6 1.8 shard_map.113
  138.4 7.5 %shard_map.114 = (f32[1344,256]{1,0:T(8,128)S(1)}, bf16[1344,256]{1,0:T(8,128)(2,1)S(1)}) custom-call(s32[11]{0:T(128)S(1)} %pad_add_fusion.info_ref.info, bf16[256,2048]{1,0:T(8,128)(2,1)S(1)} %get-tuple-element.109.attn_ref, bf16[2048,2688]{1,0:T(8,128)(2,1)S(1)} %bitcast.6), custom_call_target="tpu_custom_call" | custom-call | flops 2818572288 | bytes 11010048 | tf_op jit(solution)/shard_map/pallas_call | solution.py:323
  146.0 12.4 %collective-permute-done.28.refs_2_ = bf16[2,672,256]{2,1,0:T(8,128)(2,1)S(1)} collective-permute-done((bf16[2,672,256]{2,1,0:T(8,128)(2,1)S(1)}, bf16[2,672,256]{2,1,0:T(8,128)(2,1)S(1)}, u32[]{:S(2)}, u32[]{:S(2)}) %collective-permute-start.28) | collective-permute-done | bytes 688160 | tf_op jit(solution)/shard_map/ppermute | solution.py:27
  159.2 5.8 %collective-permute-done.24.refs_3_ = bf16[2,4,256,128]{3,2,1,0:T(8,128)(2,1)S(1)} collective-permute-done((bf16[2,4,256,128]{3,2,1,0:T(8,128)(2,1)S(1)}, bf16[2,4,256,128]{3,2,1,0:T(8,128)(2,1)S(1)}, u32[]{:S(2)}, u32[]{:S(2)}) %collective-permute-start.24) | collective-permute-done | bytes 524320 | tf_op jit(solution)/shard_map/ppermute | solution.py:23
  167.4 1.9 collective-permute-start.27
  170.0 3.3 %collective-permute-done.25.refs_1_ = bf16[256,512]{1,0:T(8,128)(2,1)S(1)} collective-permute-done((bf16[256,512]{1,0:T(8,128)(2,1)S(1)}, bf16[256,512]{1,0:T(8,128)(2,1)S(1)}, u32[]{:S(2)}, u32[]{:S(2)}) %collective-permute-start.25) | collective-permute-done | bytes 262176 | tf_op jit(solution)/shard_map/ppermute | solution.py:27
  173.3 1.7 collective-permute-start.34
  177.4 3.9 %collective-permute-start.36 = (bf16[168,256]{1,0:T(8,128)(2,1)S(1)}, bf16[168,256]{1,0:T(8,128)(2,1)S(1)}, u32[]{:S(2)}, u32[]{:S(2)}) collective-permute-start(bf16[168,256]{1,0:T(8,128)(2,1)S(1)} %get-tuple-element.132), channel_id=1, source_target_pairs={{0,6},{2,4},{4,2},{6,0},{8,14},{10,12},{12,10},{14,8},{16,22},{18,... | collective-permute-start | bytes 258056 | tf_op jit(solution)/shard_map/ppermute | solution.py:27
  182.0 2.8 %collective-permute-start.32 = (bf16[168,256]{1,0:T(8,128)(2,1)S(1)}, bf16[168,256]{1,0:T(8,128)(2,1)S(1)}, u32[]{:S(2)}, u32[]{:S(2)}) collective-permute-start(bf16[168,256]{1,0:T(8,128)(2,1)S(1)} %get-tuple-element.127), channel_id=1, source_target_pairs={{0,6},{2,4},{4,2},{6,0},{8,14},{10,12},{12,10},{14,8},{16,22},{18,... | collective-permute-start | bytes 258056 | tf_op jit(solution)/shard_map/ppermute | solution.py:27
  187.4 1.7 shard_map.121
  (84 shorter events, 40.4 us)
Async XLA Ops:
  4.2 15.6 %collective-permute-start = (bf16[256,512]{1,0:T(8,128)(2,1)S(1)}, bf16[256,512]{1,0:T(8,128)(2,1)S(1)}, u32[]{:S(2)}, u32[]{:S(2)}) collective-permute-start(bf16[256,512]{1,0:T(8,128)(2,1)S(1)} %get-tuple-element.73), channel_id=1, source_target_pairs={{0,2},{2,0},{4,6},{6,4},{8,10},{10,8},{12,14},{14,12},{16,18},{18,... | collective-permute-start | bytes 786440 | tf_op jit(solution)/shard_map/ppermute | solution.py:27
  7.3 13.4 %collective-permute-start.1 = (bf16[256,512]{1,0:T(8,128)(2,1)S(1)}, bf16[256,512]{1,0:T(8,128)(2,1)S(1)}, u32[]{:S(2)}, u32[]{:S(2)}) collective-permute-start(bf16[256,512]{1,0:T(8,128)(2,1)S(1)} %get-tuple-element.74), channel_id=1, source_target_pairs={{0,4},{2,6},{4,0},{6,2},{8,12},{10,14},{12,8},{14,10},{16,20},{18,... | collective-permute-start | bytes 786440 | tf_op jit(solution)/shard_map/ppermute | solution.py:27
  8.8 11.9 %collective-permute-start.2 = (bf16[256,512]{1,0:T(8,128)(2,1)S(1)}, bf16[256,512]{1,0:T(8,128)(2,1)S(1)}, u32[]{:S(2)}, u32[]{:S(2)}) collective-permute-start(bf16[256,512]{1,0:T(8,128)(2,1)S(1)} %get-tuple-element.75), channel_id=1, source_target_pairs={{0,6},{2,4},{4,2},{6,0},{8,14},{10,12},{12,10},{14,8},{16,22},{18,... | collective-permute-start | bytes 786440 | tf_op jit(solution)/shard_map/ppermute | solution.py:27
  21.4 17.7 %collective-permute-start.6 = (bf16[4,256,256]{2,1,0:T(8,128)(2,1)S(1)}, bf16[4,256,256]{2,1,0:T(8,128)(2,1)S(1)}, u32[]{:S(2)}, u32[]{:S(2)}) collective-permute-start(bf16[4,256,256]{2,1,0:T(8,128)(2,1)S(1)} %get-tuple-element.81.refs_4_.refs_5_), channel_id=1, source_target_pairs={{0,8},{2,10},{4,12},{6,14},{8,16},{10,18},{12,20},{14,22},{16,24},... | collective-permute-start | bytes 1572872 | tf_op jit(solution)/shard_map/ppermute | solution.py:23
  25.6 9.3 %collective-permute-start.3 = (bf16[256,512]{1,0:T(8,128)(2,1)S(1)}, bf16[256,512]{1,0:T(8,128)(2,1)S(1)}, u32[]{:S(2)}, u32[]{:S(2)}) collective-permute-start(bf16[256,512]{1,0:T(8,128)(2,1)S(1)} %get-tuple-element.77), channel_id=1, source_target_pairs={{0,2},{2,0},{4,6},{6,4},{8,10},{10,8},{12,14},{14,12},{16,18},{18,... | collective-permute-start | bytes 786440 | tf_op jit(solution)/shard_map/ppermute | solution.py:27
  26.8 12.2 %collective-permute-start.4 = (bf16[256,512]{1,0:T(8,128)(2,1)S(1)}, bf16[256,512]{1,0:T(8,128)(2,1)S(1)}, u32[]{:S(2)}, u32[]{:S(2)}) collective-permute-start(bf16[256,512]{1,0:T(8,128)(2,1)S(1)} %get-tuple-element.78), channel_id=1, source_target_pairs={{0,4},{2,6},{4,0},{6,2},{8,12},{10,14},{12,8},{14,10},{16,20},{18,... | collective-permute-start | bytes 786440 | tf_op jit(solution)/shard_map/ppermute | solution.py:27
  28.3 10.8 %collective-permute-start.5 = (bf16[256,512]{1,0:T(8,128)(2,1)S(1)}, bf16[256,512]{1,0:T(8,128)(2,1)S(1)}, u32[]{:S(2)}, u32[]{:S(2)}) collective-permute-start(bf16[256,512]{1,0:T(8,128)(2,1)S(1)} %get-tuple-element.79), channel_id=1, source_target_pairs={{0,6},{2,4},{4,2},{6,0},{8,14},{10,12},{12,10},{14,8},{16,22},{18,... | collective-permute-start | bytes 786440 | tf_op jit(solution)/shard_map/ppermute | solution.py:27
  29.1 17.1 %collective-permute-start.7 = (bf16[4,256,256]{2,1,0:T(8,128)(2,1)S(1)}, bf16[4,256,256]{2,1,0:T(8,128)(2,1)S(1)}, u32[]{:S(2)}, u32[]{:S(2)}) collective-permute-start(bf16[4,256,256]{2,1,0:T(8,128)(2,1)S(1)} %get-tuple-element.82.refs_4_.refs_5_), channel_id=1, source_target_pairs={{0,8},{2,10},{4,12},{6,14},{8,16},{10,18},{12,20},{14,22},{16,24},... | collective-permute-start | bytes 1572872 | tf_op jit(solution)/shard_map/ppermute | solution.py:23
  39.7 23.1 %collective-permute-start.11 = (bf16[128,2688]{1,0:T(8,128)(2,1)S(1)}, bf16[128,2688]{1,0:T(8,128)(2,1)S(1)}, u32[]{:S(2)}, u32[]{:S(2)}) collective-permute-start(bf16[128,2688]{1,0:T(8,128)(2,1)S(1)} %shard_map.106), channel_id=1, source_target_pairs={{0,2},{2,0},{4,6},{6,4},{8,10},{10,8},{12,14},{14,12},{16,18},{18,... | collective-permute-start | bytes 2064392 | tf_op jit(solution)/shard_map/ppermute | solution.py:27
  41.0 29.6 %collective-permute-start.12 = (bf16[128,2688]{1,0:T(8,128)(2,1)S(1)}, bf16[128,2688]{1,0:T(8,128)(2,1)S(1)}, u32[]{:S(2)}, u32[]{:S(2)}) collective-permute-start(bf16[128,2688]{1,0:T(8,128)(2,1)S(1)} %shard_map.106), channel_id=1, source_target_pairs={{0,4},{2,6},{4,0},{6,2},{8,12},{10,14},{12,8},{14,10},{16,20},{18,... | collective-permute-start | bytes 2064392 | tf_op jit(solution)/shard_map/ppermute | solution.py:27
  41.8 28.7 %collective-permute-start.13 = (bf16[128,2688]{1,0:T(8,128)(2,1)S(1)}, bf16[128,2688]{1,0:T(8,128)(2,1)S(1)}, u32[]{:S(2)}, u32[]{:S(2)}) collective-permute-start(bf16[128,2688]{1,0:T(8,128)(2,1)S(1)} %shard_map.106), channel_id=1, source_target_pairs={{0,6},{2,4},{4,2},{6,0},{8,14},{10,12},{12,10},{14,8},{16,22},{18,... | collective-permute-start | bytes 2064392 | tf_op jit(solution)/shard_map/ppermute | solution.py:27
  71.3 16.2 %collective-permute-start.18 = (bf16[2,4,256,128]{3,2,1,0:T(8,128)(2,1)S(1)}, bf16[2,4,256,128]{3,2,1,0:T(8,128)(2,1)S(1)}, u32[]{:S(2)}, u32[]{:S(2)}) collective-permute-start(bf16[2,4,256,128]{3,2,1,0:T(8,128)(2,1)S(1)} %get-tuple-element.99), channel_id=1, source_target_pairs={{8,0},{10,2},{12,4},{14,6},{16,8},{18,10},{20,12},{22,14},{24,16},... | collective-permute-start | bytes 1572872 | tf_op jit(solution)/shard_map/ppermute | solution.py:23
  73.4 14.1 %collective-permute-start.14 = (bf16[256,512]{1,0:T(8,128)(2,1)S(1)}, bf16[256,512]{1,0:T(8,128)(2,1)S(1)}, u32[]{:S(2)}, u32[]{:S(2)}) collective-permute-start(bf16[256,512]{1,0:T(8,128)(2,1)S(1)} %get-tuple-element.92), channel_id=1, source_target_pairs={{0,2},{2,0},{4,6},{6,4},{8,10},{10,8},{12,14},{14,12},{16,18},{18,... | collective-permute-start | bytes 786440 | tf_op jit(solution)/shard_map/ppermute | solution.py:27
  73.9 14.0 %collective-permute-start.15 = (bf16[256,512]{1,0:T(8,128)(2,1)S(1)}, bf16[256,512]{1,0:T(8,128)(2,1)S(1)}, u32[]{:S(2)}, u32[]{:S(2)}) collective-permute-start(bf16[256,512]{1,0:T(8,128)(2,1)S(1)} %get-tuple-element.93), channel_id=1, source_target_pairs={{0,4},{2,6},{4,0},{6,2},{8,12},{10,14},{12,8},{14,10},{16,20},{18,... | collective-permute-start | bytes 786440 | tf_op jit(solution)/shard_map/ppermute | solution.py:27
  75.3 12.7 %collective-permute-start.16 = (bf16[256,512]{1,0:T(8,128)(2,1)S(1)}, bf16[256,512]{1,0:T(8,128)(2,1)S(1)}, u32[]{:S(2)}, u32[]{:S(2)}) collective-permute-start(bf16[256,512]{1,0:T(8,128)(2,1)S(1)} %get-tuple-element.94), channel_id=1, source_target_pairs={{0,6},{2,4},{4,2},{6,0},{8,14},{10,12},{12,10},{14,8},{16,22},{18,... | collective-permute-start | bytes 786440 | tf_op jit(solution)/shard_map/ppermute | solution.py:27
  109.1 20.0 %collective-permute-start.22 = (bf16[2,672,256]{2,1,0:T(8,128)(2,1)S(1)}, bf16[2,672,256]{2,1,0:T(8,128)(2,1)S(1)}, u32[]{:S(2)}, u32[]{:S(2)}) collective-permute-start(bf16[2,672,256]{2,1,0:T(8,128)(2,1)S(1)} %get-tuple-element.107), channel_id=1, source_target_pairs={{0,8},{2,10},{4,12},{6,14},{8,0},{10,2},{12,4},{14,6},{16,24},{18,... | collective-permute-start | bytes 2064392 | tf_op jit(solution)/shard_map/ppermute | solution.py:27
  111.6 10.2 %collective-permute-start.10 = (bf16[2,256,256]{2,1,0:T(8,128)(2,1)S(1)}, bf16[2,256,256]{2,1,0:T(8,128)(2,1)S(1)}, u32[]{:S(2)}, u32[]{:S(2)}) collective-permute-start(bf16[2,256,256]{2,1,0:T(8,128)(2,1)S(1)} %get-tuple-element.86), channel_id=1, source_target_pairs={{0,6},{2,4},{4,2},{6,0},{8,14},{10,12},{12,10},{14,8},{16,22},{18,... | collective-permute-start | bytes 786440 | tf_op jit(solution)/shard_map/ppermute | solution.py:27
  113.2 14.1 %collective-permute-start.8 = (bf16[2,256,256]{2,1,0:T(8,128)(2,1)S(1)}, bf16[2,256,256]{2,1,0:T(8,128)(2,1)S(1)}, u32[]{:S(2)}, u32[]{:S(2)}) collective-permute-start(bf16[2,256,256]{2,1,0:T(8,128)(2,1)S(1)} %get-tuple-element.84), channel_id=1, source_target_pairs={{0,2},{2,0},{4,6},{6,4},{8,10},{10,8},{12,14},{14,12},{16,18},{18,... | collective-permute-start | bytes 786440 | tf_op jit(solution)/shard_map/ppermute | solution.py:27
  114.4 14.6 %collective-permute-start.9 = (bf16[2,256,256]{2,1,0:T(8,128)(2,1)S(1)}, bf16[2,256,256]{2,1,0:T(8,128)(2,1)S(1)}, u32[]{:S(2)}, u32[]{:S(2)}) collective-permute-start(bf16[2,256,256]{2,1,0:T(8,128)(2,1)S(1)} %get-tuple-element.85), channel_id=1, source_target_pairs={{0,4},{2,6},{4,0},{6,2},{8,12},{10,14},{12,8},{14,10},{16,20},{18,... | collective-permute-start | bytes 786440 | tf_op jit(solution)/shard_map/ppermute | solution.py:27
  115.0 17.8 %collective-permute-start.19 = (bf16[2,256,256]{2,1,0:T(8,128)(2,1)S(1)}, bf16[2,256,256]{2,1,0:T(8,128)(2,1)S(1)}, u32[]{:S(2)}, u32[]{:S(2)}) collective-permute-start(bf16[2,256,256]{2,1,0:T(8,128)(2,1)S(1)} %get-tuple-element.101), channel_id=1, source_target_pairs={{0,2},{2,0},{4,6},{6,4},{8,10},{10,8},{12,14},{14,12},{16,18},{18,... | collective-permute-start | bytes 786440 | tf_op jit(solution)/shard_map/ppermute | solution.py:27
  121.7 13.8 %collective-permute-start.20 = (bf16[2,256,256]{2,1,0:T(8,128)(2,1)S(1)}, bf16[2,256,256]{2,1,0:T(8,128)(2,1)S(1)}, u32[]{:S(2)}, u32[]{:S(2)}) collective-permute-start(bf16[2,256,256]{2,1,0:T(8,128)(2,1)S(1)} %get-tuple-element.102), channel_id=1, source_target_pairs={{0,4},{2,6},{4,0},{6,2},{8,12},{10,14},{12,8},{14,10},{16,20},{18,... | collective-permute-start | bytes 786440 | tf_op jit(solution)/shard_map/ppermute | solution.py:27
  127.3 9.3 %collective-permute-start.21 = (bf16[2,256,256]{2,1,0:T(8,128)(2,1)S(1)}, bf16[2,256,256]{2,1,0:T(8,128)(2,1)S(1)}, u32[]{:S(2)}, u32[]{:S(2)}) collective-permute-start(bf16[2,256,256]{2,1,0:T(8,128)(2,1)S(1)} %get-tuple-element.103), channel_id=1, source_target_pairs={{0,6},{2,4},{4,2},{6,0},{8,14},{10,12},{12,10},{14,8},{16,22},{18,... | collective-permute-start | bytes 786440 | tf_op jit(solution)/shard_map/ppermute | solution.py:27
  129.0 29.4 %collective-permute-start.28 = (bf16[2,672,256]{2,1,0:T(8,128)(2,1)S(1)}, bf16[2,672,256]{2,1,0:T(8,128)(2,1)S(1)}, u32[]{:S(2)}, u32[]{:S(2)}) collective-permute-start(bf16[2,672,256]{2,1,0:T(8,128)(2,1)S(1)} %get-tuple-element.98.refs_10_), channel_id=1, source_target_pairs={{0,8},{2,10},{4,12},{6,14},{8,0},{10,2},{12,4},{14,6},{16,24},{18,... | collective-permute-start | bytes 2064392 | tf_op jit(solution)/shard_map/ppermute | solution.py:27
  129.1 35.9 %collective-permute-start.24 = (bf16[2,4,256,128]{3,2,1,0:T(8,128)(2,1)S(1)}, bf16[2,4,256,128]{3,2,1,0:T(8,128)(2,1)S(1)}, u32[]{:S(2)}, u32[]{:S(2)}) collective-permute-start(bf16[2,4,256,128]{3,2,1,0:T(8,128)(2,1)S(1)} %get-tuple-element.115), channel_id=1, source_target_pairs={{8,0},{10,2},{12,4},{14,6},{16,8},{18,10},{20,12},{22,14},{24,16},... | collective-permute-start | bytes 1572872 | tf_op jit(solution)/shard_map/ppermute | solution.py:23
  132.9 34.5 %collective-permute-start.33 = (bf16[672,256]{1,0:T(8,128)(2,1)S(1)}, bf16[672,256]{1,0:T(8,128)(2,1)S(1)}, u32[]{:S(2)}, u32[]{:S(2)}) collective-permute-start(bf16[672,256]{1,0:T(8,128)(2,1)S(1)} %get-tuple-element.108.refs_8_), channel_id=1, source_target_pairs={{0,16},{2,18},{4,20},{6,22},{8,24},{10,26},{12,28},{14,30},{16,0},... | collective-permute-start | bytes 1032200 | tf_op jit(solution)/shard_map/ppermute | solution.py:27
  145.9 43.2 %collective-permute-start.23 = (bf16[1344,256]{1,0:T(8,128)(2,1)S(1)}, bf16[1344,256]{1,0:T(8,128)(2,1)S(1)}, u32[]{:S(2)}, u32[]{:S(2)}) collective-permute-start(bf16[1344,256]{1,0:T(8,128)(2,1)S(1)} %get-tuple-element.111), channel_id=1, source_target_pairs={{0,1},{1,0},{2,3},{3,2},{4,5},{5,4},{6,7},{7,6},{8,9},{9,8},{10,11... | collective-permute-start | bytes 2064392 | tf_op jit(solution)/shard_map/ppermute | solution.py:27
  159.1 15.9 %collective-permute-start.29 = (bf16[672,256]{1,0:T(8,128)(2,1)S(1)}, bf16[672,256]{1,0:T(8,128)(2,1)S(1)}, u32[]{:S(2)}, u32[]{:S(2)}) collective-permute-start(bf16[672,256]{1,0:T(8,128)(2,1)S(1)} %get-tuple-element.123), channel_id=1, source_target_pairs={{0,16},{2,18},{4,20},{6,22},{8,24},{10,26},{12,28},{14,30},{16,0},... | collective-permute-start | bytes 1032200 | tf_op jit(solution)/shard_map/ppermute | solution.py:27
  165.8 7.5 %collective-permute-start.25 = (bf16[256,512]{1,0:T(8,128)(2,1)S(1)}, bf16[256,512]{1,0:T(8,128)(2,1)S(1)}, u32[]{:S(2)}, u32[]{:S(2)}) collective-permute-start(bf16[256,512]{1,0:T(8,128)(2,1)S(1)} %get-tuple-element.117), channel_id=1, source_target_pairs={{0,2},{2,0},{4,6},{6,4},{8,10},{10,8},{12,14},{14,12},{16,18},{18,... | collective-permute-start | bytes 786440 | tf_op jit(solution)/shard_map/ppermute | solution.py:27
  167.0 10.4 %collective-permute-start.26 = (bf16[256,512]{1,0:T(8,128)(2,1)S(1)}, bf16[256,512]{1,0:T(8,128)(2,1)S(1)}, u32[]{:S(2)}, u32[]{:S(2)}) collective-permute-start(bf16[256,512]{1,0:T(8,128)(2,1)S(1)} %get-tuple-element.118), channel_id=1, source_target_pairs={{0,4},{2,6},{4,0},{6,2},{8,12},{10,14},{12,8},{14,10},{16,20},{18,... | collective-permute-start | bytes 786440 | tf_op jit(solution)/shard_map/ppermute | solution.py:27
  167.4 13.9 %collective-permute-start.27 = (bf16[256,512]{1,0:T(8,128)(2,1)S(1)}, bf16[256,512]{1,0:T(8,128)(2,1)S(1)}, u32[]{:S(2)}, u32[]{:S(2)}) collective-permute-start(bf16[256,512]{1,0:T(8,128)(2,1)S(1)} %get-tuple-element.119), channel_id=1, source_target_pairs={{0,6},{2,4},{4,2},{6,0},{8,14},{10,12},{12,10},{14,8},{16,22},{18,... | collective-permute-start | bytes 786440 | tf_op jit(solution)/shard_map/ppermute | solution.py:27
  173.3 8.2 %collective-permute-start.34 = (bf16[168,256]{1,0:T(8,128)(2,1)S(1)}, bf16[168,256]{1,0:T(8,128)(2,1)S(1)}, u32[]{:S(2)}, u32[]{:S(2)}) collective-permute-start(bf16[168,256]{1,0:T(8,128)(2,1)S(1)} %get-tuple-element.130), channel_id=1, source_target_pairs={{0,2},{2,0},{4,6},{6,4},{8,10},{10,8},{12,14},{14,12},{16,18},{18,... | collective-permute-start | bytes 258056 | tf_op jit(solution)/shard_map/ppermute | solution.py:27
  177.4 9.0 %collective-permute-start.36 = (bf16[168,256]{1,0:T(8,128)(2,1)S(1)}, bf16[168,256]{1,0:T(8,128)(2,1)S(1)}, u32[]{:S(2)}, u32[]{:S(2)}) collective-permute-start(bf16[168,256]{1,0:T(8,128)(2,1)S(1)} %get-tuple-element.132), channel_id=1, source_target_pairs={{0,6},{2,4},{4,2},{6,0},{8,14},{10,12},{12,10},{14,8},{16,22},{18,... | collective-permute-start | bytes 258056 | tf_op jit(solution)/shard_map/ppermute | solution.py:27
  (14 other events, 200.4 us)

commit v3 on v2

--- a/solution.py
+++ b/solution.py
@@ -31,20 +31,20 @@
 ANY = pl.BlockSpec(memory_space=pl.ANY)
 
 
-def attention_kernel(rows, skip, info, *refs):
-    q_refs = refs[:GROUP]
-    k_own, v_own, k_far, v_far = refs[GROUP : GROUP + 4]
-    outs = refs[GROUP + 4 + skip :]
-    back_refs = outs[:GROUP]
-    attn_cat, kv_own, kv_far = outs[GROUP : GROUP + 3]
-    q_all, g_all, k_all, v_all, k_tr, v_tr, k_acc, v_acc, back = outs[GROUP + 3 :]
+def attention_kernel(rows, held, info, *refs):
+    q_refs, g_refs = refs[:GROUP], refs[GROUP : 2 * GROUP]
+    k_own, v_own, k_far, v_far = refs[2 * GROUP : 2 * GROUP + 4]
+    held_refs = refs[2 * GROUP + 4 : 2 * GROUP + 4 + held]
+    outs = refs[2 * GROUP + 4 + held :]
+    back_refs = outs[: 2 * GROUP]
+    attn_cat, kv_own, kv_far = outs[2 * GROUP : 2 * GROUP + 3]
+    q_all, g_all, k_all, v_all, k_tr, v_tr, k_acc, v_acc, back = outs[2 * GROUP + 3 :]
     r, tp = info[0], info[1]
-    width = q_refs[0].shape[1] // 2
-    heads = width // HEAD
+    heads = q_refs[0].shape[1] // HEAD
     half = rows // 2
     for m in range(GROUP):
-        q_all[m] = q_refs[m][:, :width]
-        g_all[m] = q_refs[m][:, width:]
+        q_all[m] = q_refs[m][...]
+        g_all[m] = g_refs[m][...]
         spot = r ^ m
         for place, k, v in ((spot, k_far, v_far), (spot + GROUP, k_own, v_own)):
             k_all[place] = k[m]
@@ -53,8 +53,9 @@
             v_tr[place] = v[m].T
     k_acc[...] = jnp.zeros_like(k_acc)
     v_acc[...] = jnp.zeros_like(v_acc)
-    key_at = lax.broadcasted_iota(jnp.int32, (rows, rows), 0)
-    query_at = lax.broadcasted_iota(jnp.int32, (rows, rows), 1)
+    key_at = lax.broadcasted_iota(jnp.int32, (rows, heads * rows), 0)
+    query_at = lax.broadcasted_iota(jnp.int32, (rows, heads * rows), 1) % rows
+    far_seen, own_seen = key_at > query_at, key_at <= query_at
     nt = (((1,), (1,)), ((), ()))
 
     def dot(a, b):
@@ -63,48 +64,55 @@
     def block(m, carry):
         first = r ^ m
         own_doc = info[3 + first + GROUP]
+        q = jnp.concatenate([q_all[m, :, h * HEAD : (h + 1) * HEAD] for h in range(heads)], axis=0)
+        g = jnp.concatenate([g_all[m, :, h * HEAD : (h + 1) * HEAD] for h in range(heads)], axis=0)
+        scores, hidden = [], []
+        for j in range(GROUP + 1):
+            s = lax.dot_general(k_all[first + j], q, nt, preferred_element_type=jnp.float32)
+            if j == 0:
+                s = jnp.where(far_seen, s, HIDDEN)
+            if j == GROUP:
+                s = jnp.where(own_seen, s, HIDDEN)
+            scores.append(s)
+            hidden.append(jnp.where(info[3 + first + j] == own_doc, 0.0, HIDDEN))
+        tops = [jnp.max(s, axis=0, keepdims=True) + b for s, b in zip(scores, hidden)]
+        top = functools.reduce(jnp.maximum, tops) * (query_scale * LOG2E)
+        expo = [
+            jnp.exp2(s * (query_scale * LOG2E) - (top - b)) for s, b in zip(scores, hidden)
+        ]
+        whole = functools.reduce(jnp.add, [jnp.sum(e, axis=0, keepdims=True) for e in expo])
+        inverse = 1.0 / whole
+        probs = [e * inverse for e in expo]
+        low = [p.astype(jnp.bfloat16) for p in probs]
+        attn_tr = functools.reduce(jnp.add, [dot(v_tr[first + j], low[j]) for j in range(GROUP + 1)])
+        attn_tr = attn_tr.astype(jnp.bfloat16).astype(jnp.float32)
+        delta = jnp.sum(attn_tr * g.astype(jnp.float32).T, axis=0, keepdims=True)
+        dq_tr, d_scores = None, []
+        for j in range(GROUP + 1):
+            d_p = lax.dot_general(v_all[first + j], g, nt, preferred_element_type=jnp.float32)
+            d_s = (probs[j] * (d_p - delta)).astype(jnp.bfloat16)
+            term = dot(k_tr[first + j], d_s)
+            dq_tr = term if dq_tr is None else dq_tr + term
+            d_scores.append(d_s)
+        for j in range(GROUP + 1):
+            k_acc[first + j] += dot(d_scores[j], q)
+            v_acc[first + j] += dot(low[j], g)
+        attn = attn_tr.T.astype(jnp.bfloat16)
+        dq = (dq_tr * query_scale).T.astype(jnp.bfloat16)
         for h in range(heads):
-            cols = slice(h * HEAD, (h + 1) * HEAD)
-            q = q_all[m, :, cols]
-            g = g_all[m, :, cols]
-            scores = []
-            for j in range(GROUP + 1):
-                s = lax.dot_general(k_all[first + j], q, nt, preferred_element_type=jnp.float32)
-                if j == 0:
-                    s = jnp.where(key_at > query_at, s, HIDDEN)
-                if j == GROUP:
-                    s = jnp.where(key_at <= query_at, s, HIDDEN)
-                else:
-                    s = s + jnp.where(info[3 + first + j] == own_doc, 0.0, HIDDEN)
-                scores.append(s)
-            top = functools.reduce(jnp.maximum, [jnp.max(s, axis=0, keepdims=True) for s in scores])
-            top = top * (query_scale * LOG2E)
-            expo = [jnp.exp2(s * (query_scale * LOG2E) - top) for s in scores]
-            whole = functools.reduce(jnp.add, [jnp.sum(e, axis=0, keepdims=True) for e in expo])
-            inverse = 1.0 / whole
-            probs = [e * inverse for e in expo]
-            low = [p.astype(jnp.bfloat16) for p in probs]
-            attn_tr = functools.reduce(
-                jnp.add, [dot(v_tr[first + j], low[j]) for j in range(GROUP + 1)]
-            )
-            attn_tr = attn_tr.astype(jnp.bfloat16).astype(jnp.float32)
-            g_tr = g.astype(jnp.float32).T
-            delta = jnp.sum(attn_tr * g_tr, axis=0, keepdims=True)
-            dq_tr = None
-            for j in range(GROUP + 1):
-                d_p = lax.dot_general(v_all[first + j], g, nt, preferred_element_type=jnp.float32)
-                d_s = (probs[j] * (d_p - delta)).astype(jnp.bfloat16)
-                term = dot(k_tr[first + j], d_s)
-                dq_tr = term if dq_tr is None else dq_tr + term
-                k_acc[first + j] += dot(d_s, q)
-                v_acc[first + j] += dot(low[j], g)
-            back[m, 0, :, cols] = attn_tr.T.astype(jnp.bfloat16)
-            back[m, 1, :, cols] = (dq_tr * query_scale).T.astype(jnp.bfloat16)
+            back[m, 0, :, h * HEAD : (h + 1) * HEAD] = attn[h * rows : (h + 1) * rows]
+            back[m, 1, :, h * HEAD : (h + 1) * HEAD] = dq[h * rows : (h + 1) * rows]
         return carry
 
     lax.fori_loop(0, GROUP, block, 0)
     for m in range(GROUP):
-        back_refs[m][...] = back[m]
+        width = back.shape[3]
+        for i in range(2):
+            out = back_refs[i * GROUP + m]
+            at = out.shape[1] - width
+            out[:, at:] = back[m, i]
+            if held:
+                out[:, :at] = held_refs[i * GROUP + m][...]
         spot = r ^ m
         kv_far[0, m] = (k_acc[spot] * query_scale).astype(kv_far.dtype)
         kv_far[1, m] = v_acc[spot].astype(kv_far.dtype)
@@ -124,25 +132,29 @@
     return pl.BlockSpec(array.shape, lambda i: (0,) * len(array.shape))
 
 
-def attention(info, q_and_d, kv_own, kv_far, after=()):
-    rows, q_block = q_and_d[0].shape[0], q_and_d[0].shape[1] // 2
-    k_spec = pl.BlockSpec((GROUP, rows, HEAD), lambda i: (0, 0, 0))
-    v_spec = pl.BlockSpec((GROUP, rows, HEAD), lambda i: (0, 0, 1))
+def attention(info, q_and_d, kv_own, kv_far, g, held):
+    kv_heads = kv_own.shape[0] // GROUP
+    rows, q_block = q_and_d[0].shape[0], q_and_d[0].shape[1] // 2 // kv_heads
+    q_spec = pl.BlockSpec((rows, q_block), lambda i: (0, g))
+    g_spec = pl.BlockSpec((rows, q_block), lambda i: (0, g + kv_heads))
+    k_spec = pl.BlockSpec((GROUP, rows, HEAD), lambda i: (g, 0, 0))
+    v_spec = pl.BlockSpec((GROUP, rows, HEAD), lambda i: (g, 0, 1))
     kv_shape = (2, GROUP, rows, HEAD)
     bf16 = jnp.bfloat16
     blocks = 2 * GROUP
-    out = [jax.ShapeDtypeStruct((2, rows, q_block), bf16)] * GROUP + [
+    out = [jax.ShapeDtypeStruct((rows, (g + 1) * q_block), bf16)] * (2 * GROUP) + [
         jax.ShapeDtypeStruct((GROUP * rows, q_block), bf16),
         jax.ShapeDtypeStruct(kv_shape, jnp.float32),
         jax.ShapeDtypeStruct(kv_shape, bf16),
     ]
     return pl.pallas_call(
-        functools.partial(attention_kernel, rows, len(after)),
+        functools.partial(attention_kernel, rows, len(held)),
         grid=(1,),
         in_specs=[SMEM]
-        + [entire(a) for a in q_and_d]
+        + [q_spec] * GROUP
+        + [g_spec] * GROUP
         + [k_spec, v_spec, k_spec, v_spec]
-        + [ANY] * len(after),
+        + [entire(a) for a in held],
         out_specs=[entire(a) for a in out],
         out_shape=out,
         scratch_shapes=[
@@ -162,7 +174,7 @@
             bytes_accessed=5 * 1024 * 1024,
             transcendentals=0,
         ),
-    )(info, *q_and_d, kv_own, kv_own, kv_far, kv_far, *after)
+    )(info, *q_and_d, *q_and_d, kv_own, kv_own, kv_far, kv_far, *held)
 
 
 def moved(body, info, arrays, out, after=()):
@@ -187,10 +199,45 @@
     return ref[:, pl.ds(pl.multiple_of(start, HEAD), width)]
 
 
+def pack_kv(keys, values):
+    rows, width = keys.shape[0], keys.shape[1] // GROUP
+
+    def kernel(k_ref, v_ref, *refs):
+        outs, sems = refs[:GROUP], refs[GROUP]
+        r = lax.axis_index("ctx") % GROUP
+        copies = []
+        for m in range(GROUP):
+            for i, ref in enumerate((k_ref, v_ref)):
+                start = pl.multiple_of((r ^ m) * width, HEAD)
+                copies.append(
+                    pltpu.make_async_copy(
+                        ref.at[:, pl.ds(start, width)],
+                        outs[m].at[:, i * width : (i + 1) * width],
+                        sems.at[2 * m + i],
+                    )
+                )
+        for copy in copies:
+            copy.start()
+        for copy in copies:
+            copy.wait()
+
+    out = [jax.ShapeDtypeStruct((rows, 2 * width), keys.dtype)] * GROUP
+    return pl.pallas_call(
+        kernel,
+        in_specs=[ANY, ANY],
+        out_specs=[pl.BlockSpec(memory_space=pltpu.VMEM)] * GROUP,
+        out_shape=out,
+        scratch_shapes=[pltpu.SemaphoreType.DMA((2 * GROUP,))],
+        compiler_params=pltpu.CompilerParams(vmem_limit_bytes=32 * 1024 * 1024),
+        cost_estimate=pl.CostEstimate(
+            flops=0, bytes_accessed=4 * keys.size, transcendentals=0
+        ),
+    )(keys, values)
+
+
 def project_back(info, out_grad, out_weight):
     rows, d_out = out_grad.shape
-    per = 2
-    steps = GROUP * per
+    steps = GROUP
     block = out_weight.shape[0] // steps
 
     def kernel(info_ref, grad, weight, *outs):
@@ -205,9 +252,9 @@
                 outs[at][...] = part
 
     def weight_block(step, info_ref):
-        return ((info_ref[0] ^ (step % GROUP)) * per + step // GROUP, 0)
-
-    outs = pl.pallas_call(
+        return (info_ref[0] ^ step, 0)
+
+    return pl.pallas_call(
         kernel,
         grid_spec=pltpu.PrefetchScalarGridSpec(
             num_scalar_prefetch=1,
@@ -224,17 +271,15 @@
             flops=2 * rows * out_weight.size, bytes_accessed=2 * out_weight.size, transcendentals=0
         ),
     )(info, out_grad, out_weight)
-    return [outs[g * GROUP : (g + 1) * GROUP] for g in range(per)]
-
-
-def weight_terms(info, pieces, attn_cat):
+
+def weight_terms(info, pieces, attn_cat, after=()):
     d_out, width = pieces[0].shape[1], attn_cat.shape[1]
     block = 3 * HEAD if d_out % (3 * HEAD) == 0 else d_out
     steps, cut = d_out // block, d_out // GROUP
 
     def kernel(info_ref, *refs):
         inputs, attn = refs[: len(pieces)], refs[len(pieces)]
-        own, other, away, whole = refs[len(pieces) + 1 :]
+        own, other, away, whole = refs[len(pieces) + 1 + len(after) :]
         total, at = None, 0
         for piece in inputs:
             rows = piece.shape[0]
@@ -265,7 +310,8 @@
         grid=(steps,),
         in_specs=[SMEM]
         + [pl.BlockSpec((p.shape[0], block), lambda i: (0, i)) for p in pieces]
-        + [entire(attn_cat)],
+        + [entire(attn_cat)]
+        + [ANY] * len(after),
         out_specs=[entire(a) for a in out],
         out_shape=out,
         scratch_shapes=[pltpu.VMEM((d_out, width), jnp.bfloat16)],
@@ -275,39 +321,43 @@
             bytes_accessed=2 * (attn_cat.shape[0] + width) * d_out,
             transcendentals=0,
         ),
-    )(info, *pieces, attn_cat)
-
-
-def split_sum(info, own, met):
-    rows, width = own.shape
-    cut = rows // GROUP
-
-    def kernel(info_ref, own_ref, met_ref, *refs):
-        outs, total = refs[:GROUP], refs[GROUP]
-        total[...] = own_ref[...].astype(jnp.float32) + met_ref[...].astype(jnp.float32)
-        for m in range(GROUP):
-            start = pl.multiple_of((info_ref[0] ^ m) * cut, 8)
-            outs[m][...] = total[pl.ds(start, cut)].astype(outs[m].dtype)
-
-    out = [jax.ShapeDtypeStruct((cut, width), jnp.bfloat16)] * GROUP
+    )(info, *pieces, attn_cat, *after)
+
+
+def split_sums(info, pairs):
+    rows, width = pairs[0][0].shape
+    cut, count = rows // GROUP, len(pairs)
+
+    def kernel(info_ref, *refs):
+        outs, total = refs[2 * count : 2 * count + GROUP], refs[2 * count + GROUP]
+        for g in range(count):
+            total[...] = refs[2 * g][...].astype(jnp.float32) + refs[2 * g + 1][...].astype(jnp.float32)
+            for m in range(GROUP):
+                start = pl.multiple_of((info_ref[0] ^ m) * cut, 8)
+                block = total[pl.ds(start, cut)].astype(outs[m].dtype)
+                outs[m][:, g * width : (g + 1) * width] = block
+
+    flat = [a for pair in pairs for a in pair]
+    out = [jax.ShapeDtypeStruct((cut, count * width), jnp.bfloat16)] * GROUP
     return pl.pallas_call(
         kernel,
         grid=(1,),
-        in_specs=[SMEM, entire(own), entire(met)],
+        in_specs=[SMEM] + [entire(a) for a in flat],
         out_specs=[entire(a) for a in out],
         out_shape=out,
         scratch_shapes=[pltpu.VMEM((rows, width), jnp.float32)],
         compiler_params=pltpu.CompilerParams(vmem_limit_bytes=32 * 1024 * 1024),
-    )(info, own, met)
-
-
-def project(info, attn, out_weight):
+    )(info, *flat)
+
+
+def project(info, attn, out_weight, after):
     rows, depth = attn.shape
     d_out = out_weight.shape[1]
     block = 3 * HEAD if d_out % (3 * HEAD) == 0 else d_out
     steps, half = d_out // block, d_out // 2
 
-    def kernel(info_ref, attn_ref, weight, mine, theirs, whole):
+    def kernel(info_ref, attn_ref, weight, *refs):
+        mine, theirs, whole = refs[len(after) :]
         step = pl.program_id(0)
         part = jnp.dot(attn_ref[...], weight[...], preferred_element_type=jnp.float32)
         whole[pl.ds(pl.multiple_of(step * block, block), block)] = part.T
@@ -323,7 +373,8 @@
     return pl.pallas_call(
         kernel,
         grid=(steps,),
-        in_specs=[SMEM, entire(attn), pl.BlockSpec((depth, block), lambda i: (0, i))],
+        in_specs=[SMEM, entire(attn), pl.BlockSpec((depth, block), lambda i: (0, i))]
+        + [ANY] * len(after),
         out_specs=[entire(a) for a in out],
         out_shape=out,
         scratch_shapes=[pltpu.VMEM((d_out, rows), jnp.float32)],
@@ -331,7 +382,7 @@
         cost_estimate=pl.CostEstimate(
             flops=2 * attn.size * d_out, bytes_accessed=2 * out_weight.size, transcendentals=0
         ),
-    )(info, attn, out_weight)
+    )(info, attn, out_weight, *after)
 
 
 def grouped(queries, keys, values, out_weight, out_grad, block_doc):
@@ -354,94 +405,64 @@
     def traded(blocks):
         return [blocks[0]] + [swapped(blocks[m], "ctx", m) for m in members[1:]]
 
-    def pack_kv(info_ref, ins, outs):
+    kv = traded(pack_kv(keys, values))
+    d_attn = project_back(info, out_grad, out_weight)
+
+    def pack_queries(info_ref, ins, outs):
         for m in members:
-            start = (info_ref[0] ^ m) * kv_width
-            for i in range(2):
-                outs[m][:, i * kv_width : (i + 1) * kv_width] = columns(ins[i], start, kv_width)
-
-    kv = traded(moved(pack_kv, info, [keys, values], [shape(rows, 2 * kv_width)] * GROUP))
+            outs[m][:, :q_width] = columns(ins[0], (info_ref[0] ^ m) * q_width, q_width)
+            outs[m][:, q_width:] = ins[1 + m][...]
+
+    packed = moved(pack_queries, info, [queries, *d_attn], [shape(rows, 2 * q_width)] * GROUP)
+    q_and_d = traded(packed)
 
     def pack_heads(info_ref, ins, outs):
         for m in members:
             for g in range(kv_heads):
                 for i in range(2):
                     at = (i * kv_heads + g) * HEAD
-                    outs[g][m, :, i * HEAD : (i + 1) * HEAD] = ins[m][:, at : at + HEAD]
-
-    d_attn = project_back(info, out_grad, out_weight)
-    heads_shape = [shape(GROUP, rows, 2 * HEAD)] * kv_heads
-    kv_own = moved(pack_heads, info, kv, heads_shape, d_attn[0])
-    kv_far = [shifted(a, "ctx", GROUP) for a in kv_own]
-
-    def pack_queries(g, after):
-        def body(info_ref, ins, outs):
-            for m in members:
-                start = (info_ref[0] ^ m) * q_width + g * head_width
-                outs[m][:, :head_width] = columns(ins[0], start, head_width)
-                outs[m][:, head_width:] = ins[1 + m][...]
-
-        return traded(
-            moved(body, info, [queries, *d_attn[g]], [shape(rows, 2 * head_width)] * GROUP, after)
-        )
+                    outs[0][g * GROUP + m, :, i * HEAD : (i + 1) * HEAD] = ins[m][:, at : at + HEAD]
+
+    kv_own = moved(pack_heads, info, kv, [shape(kv_heads * GROUP, rows, 2 * HEAD)], packed)[0]
+    kv_far = shifted(kv_own, "ctx", GROUP)
 
     def pack_half(info_ref, ins, outs):
         outs[0][...] = ins[0][pl.ds(pl.multiple_of(info_ref[1] * (rows // 2), 16), rows // 2), :]
 
-    q_and_d = [pack_queries(0, kv[1:])]
-    half = moved(pack_half, info, [out_grad], [shape(rows // 2, d_out)], [*q_and_d[0][1:], kv_far[0]])[0]
+    half = moved(pack_half, info, [out_grad], [shape(rows // 2, d_out)], q_and_d[1:])[0]
     near = traded([half] * GROUP)[1:]
-    q_and_d += [pack_queries(g, near) for g in range(1, kv_heads)]
 
     def pack_near(info_ref, ins, outs):
         for i in range(GROUP - 1):
             outs[0][i * (rows // 2) : (i + 1) * (rows // 2)] = ins[i][...]
 
-    back, own_grads, far_grads, all_terms = [], [], [], []
-    pieces, after = None, kv_far[1:]
+    parts, held = [], []
     for g in range(kv_heads):
-        *blocks, attn_cat, own_grad, far_grad = attention(
-            info, q_and_d[g], kv_own[g], kv_far[g], after
-        )
-        far_grads.append(shifted(far_grad, "ctx", -GROUP))
-        if pieces is None:
-            near_shape = shape((GROUP - 1) * (rows // 2), d_out)
-            near = moved(pack_near, info, near, [near_shape], [attn_cat])[0]
-            pieces = [out_grad, near, swapped(near, "tp", 1)]
-        terms = weight_terms(info, pieces, attn_cat)
-        after = [*terms, *far_grads]
-        all_terms.append(terms)
-        back += traded(blocks)
-        own_grads.append(own_grad)
+        parts.append(attention(info, q_and_d, kv_own, kv_far, g, held))
+        held = parts[-1][: 2 * GROUP]
+    far_grads = [shifted(p[-1], "ctx", -GROUP) for p in parts]
+    own_grads = [p[-2] for p in parts]
+    attn_cats = [p[-3] for p in parts]
+    attn, query_grad = traded(held[:GROUP]), traded(held[GROUP:])
+    near_shape = shape((GROUP - 1) * (rows // 2), d_out)
+    near = moved(pack_near, info, near, [near_shape], [*attn_cats, far_grads[0]])[0]
+    pieces = [out_grad, near, swapped(near, "tp", 1)]
+    all_terms = [weight_terms(info, pieces, attn_cats[0])]
+    for g in range(1, kv_heads):
+        all_terms.append(weight_terms(info, pieces, attn_cats[g], [far_grads[g]]))
 
     def add_pair(info_ref, ins, outs):
         for i in range(2):
             outs[i][...] = (ins[i][...].astype(f32) + ins[2][i].astype(f32)).astype(outs[i].dtype)
 
-    weight_blocks = []
-    for own, other, away in all_terms:
+    def add_layers(terms, after):
+        own, other, away = terms
         met = swapped(away, "ctx", GROUP)
         pair_shape = [shape(*own.shape, dtype=f32), shape(*own.shape)]
-        own, other = moved(add_pair, info, [own, other, met], pair_shape, all_terms[-1][:1])
-        weight_blocks += traded(split_sum(info, own, swapped(other, "ctx", 2 * GROUP)))
-
-    def lay_out(info_ref, ins, outs):
-        for g in range(kv_heads):
-            for m in members:
-                start = pl.multiple_of((info_ref[0] ^ m) * q_width + g * head_width, HEAD)
-                block = ins[g * GROUP + m]
-                for i, out in enumerate(outs):
-                    piece = block[...] if len(block.shape) == 2 else block[i]
-                    out[:, pl.ds(start, head_width)] = piece.astype(out.dtype)
-
-    attn, query_grad = moved(lay_out, info, back, [shape(rows, GROUP * q_width)] * 2, [other])
-    mine, theirs = project(info, attn, out_weight)
-
-    def add_shares(info_ref, ins, outs):
-        outs[0][...] = (ins[0][...] + ins[1][...].astype(f32)).astype(bf16)
-
-    theirs = swapped(theirs, "tp", 1)
-    attn_output = moved(add_shares, info, [mine, theirs], [shape(d_out // 2, rows)])[0]
+        own, other = moved(add_pair, info, [own, other, met], pair_shape, after)
+        return own, other, swapped(other, "ctx", 2 * GROUP)
+
+    sums = [add_layers(all_terms[0], all_terms[-1][:1])]
 
     def add_up(info_ref, ins, outs):
         for g in range(kv_heads):
@@ -457,11 +478,36 @@
             for i in range(2):
                 outs[i][:, pl.ds(start, kv_width)] = ins[m][:, i * kv_width : (i + 1) * kv_width]
 
-    totals = moved(add_up, info, own_grads + far_grads, [shape(rows, 2 * kv_width)] * GROUP)
+    total_shape = [shape(rows, 2 * kv_width)] * GROUP
+    totals = moved(add_up, info, own_grads + far_grads, total_shape, [*attn[1:], *query_grad[1:], sums[0][1]])
     key_grad, value_grad = moved(lay_out_kv, info, traded(totals), [shape(rows, GROUP * kv_width)] * 2)
-    out_weight_grad = moved(
-        lay_out, info, weight_blocks, [shape(d_out // GROUP // GROUP, GROUP * q_width, dtype=f32)]
-    )[0].T
+
+    def lay_out(info_ref, ins, outs):
+        for m in members:
+            start = pl.multiple_of((info_ref[0] ^ m) * q_width, HEAD)
+            outs[0][:, pl.ds(start, q_width)] = ins[m][...]
+
+    attn = moved(lay_out, info, attn, [shape(rows, GROUP * q_width)], sums[0][1:2])[0]
+    mine, theirs = project(info, attn, out_weight, [])
+    for terms in all_terms[1:]:
+        sums.append(add_layers(terms, [sums[-1][2], theirs]))
+    query_grad = moved(lay_out, info, query_grad, [shape(rows, GROUP * q_width)], totals)[0]
+
+    def add_shares(info_ref, ins, outs):
+        outs[0][...] = (ins[0][...] + ins[1][...].astype(f32)).astype(bf16)
+
+    theirs = swapped(theirs, "tp", 1)
+    attn_output = moved(add_shares, info, [mine, theirs], [shape(d_out // 2, rows)])[0]
+
+    def lay_out_weight(info_ref, ins, outs):
+        for m in members:
+            start = pl.multiple_of((info_ref[0] ^ m) * q_width, HEAD)
+            outs[0][:, pl.ds(start, q_width)] = ins[m][...].astype(f32)
+
+    blocks = traded(split_sums(info, [(own, met) for own, other, met in sums]))
+    grad_shape = [shape(d_out // GROUP // GROUP, GROUP * q_width, dtype=f32)]
+    late = [attn_output, key_grad, query_grad]
+    out_weight_grad = moved(lay_out_weight, info, blocks, grad_shape, late)[0].T
     return (attn_output.T, query_grad, key_grad, value_grad, out_weight_grad)
 
 

time: 191 us -> 171 us (0.90)
  starting transfers between devices: 52.4 us -> 40 us
  Pallas kernels: 69.5 us -> 61.3 us
    ppermute x33 -> x27, starting transfers between devices: 42.6 us -> 33.3 us  [swapped(): lax.ppermute(shard, axis, [(i, i ^ by) for i in range(lax.axis_size(axis))])]
    ppermute x4 -> x3, waiting for transfers between devices: 14.7 us -> 6.29 us  [shifted(): return lax.ppermute(shard, axis, pairs)]
    ppermute x33 -> x27, waiting for transfers between devices: 44.7 us -> 52.5 us  [swapped(): lax.ppermute(shard, axis, [(i, i ^ by) for i in range(lax.axis_size(axis))])]
    pallas_call x4, Pallas kernels: 34.6 us -> 28.3 us  [the longest x2 27.3 us: attention(): pl.pallas_call(functools.partial(attention_kernel, rows, len(held)), grid...]
    ppermute x4 -> x3, starting transfers between devices: 9.74 us -> 6.72 us  [shifted(): return lax.ppermute(shard, axis, pairs)]
    unnamed x18 -> x24, local copies, waits for them, and re-layouts: 7.57 us -> 8.68 us
    pallas_call x13 -> x12, Pallas kernels: 12.7 us -> 11.9 us  [moved(): pl.pallas_call(kernel, grid=(1,), in_specs=[SMEM] + [entire(a) for a in a...]
  transfers between devices with their start and end apart: 37 -> 30, of which waited for: 16 -> 11; matrix products, arithmetic and copies ran while one was open for 0% -> 0% of each run, Pallas kernels for 23% -> 34%
where the time goes in v3:
time: 171 us
  Pallas kernels  61.3 us (36%)
  waiting for transfers between devices  58.8 us (34%)
  starting transfers between devices  40 us (23%)
  local copies, waits for them, and re-layouts  9.41 us (6%)
    ppermute x27, waiting for transfers between devices, swapped(): lax.ppermute(shard, axis, [(i, i ^ by) for i in range(lax.axis_size(axis))])  52.5 us
    ppermute x27, starting transfers between devices, swapped(): lax.ppermute(shard, axis, [(i, i ^ by) for i in range(lax.axis_size(axis))])  33.3 us
    pallas_call x2, Pallas kernels, attention(): pl.pallas_call(functools.partial(attention_kernel, rows, len(held)), grid...  27.3 us
    pallas_call x12, Pallas kernels, moved(): pl.pallas_call(kernel, grid=(1,), in_specs=[SMEM] + [entire(a) for a in a...  11.9 us
    pallas_call x2, Pallas kernels, weight_terms(): pl.pallas_call(kernel, grid=(steps,), in_specs=[SMEM] + [pl.BlockSpec((p....  9.04 us
    unnamed x24, local copies, waits for them, and re-layouts  8.68 us
    pallas_call x1, Pallas kernels, project(): pl.pallas_call(kernel, grid=(steps,), in_specs=[SMEM, entire(attn), pl.Bl...  7.53 us
    ppermute x3, starting transfers between devices, shifted(): return lax.ppermute(shard, axis, pairs)  6.72 us
  transfers between devices with their start and end apart: 30, of which 11 were waited for; matrix products, arithmetic and copies ran while one was open for 0% of the time, Pallas kernels for 34%

profile of v3, /device:TPU:0, one launch (start us, length us, event | category | flops | bytes accessed | tf_op | source)
XLA Modules:
  0.0 170.5 jit_solution(14741147472230622128)
XLA Ops:
  3.0 3.0 %collective-permute-start.3 = (bf16[256,512]{1,0:T(8,128)(2,1)S(1)}, bf16[256,512]{1,0:T(8,128)(2,1)S(1)}, u32[]{:S(2)}, u32[]{:S(2)}) collective-permute-start(bf16[256,512]{1,0:T(8,128)(2,1)S(1)} %get-tuple-element.70), channel_id=1, source_target_pairs={{0,2},{2,0},{4,6},{6,4},{8,10},{10,8},{12,14},{14,12},{16,18},{18,... | collective-permute-start | bytes 786440 | tf_op jit(solution)/shard_map/ppermute | solution.py:27
  6.0 1.5 collective-permute-start.4
  8.3 4.1 %copy-done = bf16[2048,2688]{1,0:T(8,128)(2,1)S(1)} copy-done((bf16[2048,2688]{1,0:T(8,128)(2,1)S(1)}, bf16[2048,2688]{1,0:T(8,128)(2,1)}, u32[]{:S(2)}) %copy-start) | copy-done | bytes 11010072
  13.8 4.5 %shard_map.101 = (bf16[256,512]{1,0:T(8,128)(2,1)S(1)}, bf16[256,512]{1,0:T(8,128)(2,1)S(1)}, bf16[256,512]{1,0:T(8,128)(2,1)S(1)}, bf16[256,512]{1,0:T(8,128)(2,1)S(1)}) custom-call(s32[11]{0:T(128)S(1)} %pad_add_fusion.info_ref.info, bf16[256,2688]{1,0:T(8,128)(2,1)S(1)} %copy-done.1, bf16[2048,2688]{1,0:T(8,128)(2,1)S(1)} %copy-done), custom_call_target="tpu_custom_call" | custom-call | flops 2818572288 | bytes 11010048 | tf_op jit(solution)/shard_map/pallas_call | solution.py:257
  20.1 3.7 %collective-permute-start.6 = (bf16[8,256,256]{2,1,0:T(8,128)(2,1)S(1)}, bf16[8,256,256]{2,1,0:T(8,128)(2,1)S(1)}, u32[]{:S(2)}, u32[]{:S(2)}) collective-permute-start(bf16[8,256,256]{2,1,0:T(8,128)(2,1)S(1)} %shard_map.104.refs_8_.refs_9_), channel_id=1, source_target_pairs={{0,8},{2,10},{4,12},{6,14},{8,16},{10,18},{12,20},{14,22},{16,24},... | collective-permute-start | bytes 3145736 | tf_op jit(solution)/shard_map/ppermute | solution.py:23
  23.8 1.6 collective-permute-start
  25.3 1.5 collective-permute-start.1
  27.3 11.4 %collective-permute-done.refs_1_.refs_5_ = bf16[256,1024]{1,0:T(8,128)(2,1)S(1)} collective-permute-done((bf16[256,1024]{1,0:T(8,128)(2,1)S(1)}, bf16[256,1024]{1,0:T(8,128)(2,1)S(1)}, u32[]{:S(2)}, u32[]{:S(2)}) %collective-permute-start) | collective-permute-done | bytes 524320 | tf_op jit(solution)/shard_map/ppermute | solution.py:27
  38.7 10.1 %collective-permute-done.1.refs_2_.refs_6_ = bf16[256,1024]{1,0:T(8,128)(2,1)S(1)} collective-permute-done((bf16[256,1024]{1,0:T(8,128)(2,1)S(1)}, bf16[256,1024]{1,0:T(8,128)(2,1)S(1)}, u32[]{:S(2)}, u32[]{:S(2)}) %collective-permute-start.1) | collective-permute-done | bytes 524320 | tf_op jit(solution)/shard_map/ppermute | solution.py:27
  51.6 1.4 collective-permute-start.12
  53.0 13.6 %shard_map.105 = (bf16[256,256]{1,0:T(8,128)(2,1)S(1)}, bf16[256,256]{1,0:T(8,128)(2,1)S(1)}, bf16[256,256]{1,0:T(8,128)(2,1)S(1)}, bf16[256,256]{1,0:T(8,128)(2...) custom-call(s32[11]{0:T(128)S(1)} %pad_add_fusion.info_ref.info, ...), custom_call_target="tpu_custom_call" | custom-call | flops 4026531840 | bytes 5242880 | tf_op jit(solution)/shard_map/pallas_call | solution.py:150
  67.9 13.7 %shard_map.106 = (bf16[256,512]{1,0:T(8,128)(2,1)S(1)}, bf16[256,512]{1,0:T(8,128)(2,1)S(1)}, bf16[256,512]{1,0:T(8,128)(2,1)S(1)}, bf16[256,512]{1,0:T(8,128)(2...) custom-call(s32[11]{0:T(128)S(1)} %pad_add_fusion.info_ref.info, ...), custom_call_target="tpu_custom_call" | custom-call | flops 4026531840 | bytes 5242880 | tf_op jit(solution)/shard_map/pallas_call | solution.py:150
  82.5 1.7 %collective-permute-start.16 = (bf16[2,4,256,128]{3,2,1,0:T(8,128)(2,1)S(1)}, bf16[2,4,256,128]{3,2,1,0:T(8,128)(2,1)S(1)}, u32[]{:S(2)}, u32[]{:S(2)}) collective-permute-start(bf16[2,4,256,128]{3,2,1,0:T(8,128)(2,1)S(1)} %get-tuple-element.91), channel_id=1, source_target_pairs={{8,0},{10,2},{12,4},{14,6},{16,8},{18,10},{20,12},{22,14},{24,16},... | collective-permute-start | bytes 1572872 | tf_op jit(solution)/shard_map/ppermute | solution.py:23
  84.2 2.3 %collective-permute-done.14.refs_2_ = bf16[384,2688]{1,0:T(8,128)(2,1)S(1)} collective-permute-done((bf16[384,2688]{1,0:T(8,128)(2,1)S(1)}, bf16[384,2688]{1,0:T(8,128)(2,1)S(1)}, u32[]{:S(2)}, u32[]{:S(2)}) %collective-permute-start.14) | collective-permute-done | bytes 2064416 | tf_op jit(solution)/shard_map/ppermute | solution.py:27
  86.6 4.5 %shard_map.109 = (bf16[672,256]{1,0:T(8,128)(2,1)S(1)}, bf16[672,256]{1,0:T(8,128)(2,1)S(1)}, bf16[2,672,256]{2,1,0:T(8,128)(2,1)S(1)}) custom-call(s32[11]{0:T(128)S(1)} %pad_add_fusion.info_ref.info, bf16[256,2688]{1,0:T(8,128)(2,1)S(1)} %copy-done.2, bf16[384,2688]{1,0:T(8,128)(2,1)S(1)} %shard_map.108.refs_1_, ...), custom_call_target="tpu_custom_call" | custom-call | flops 1409286144 | bytes 6881280 | tf_op jit(solution)/shard_map/pallas_call | solution.py:308
  91.1 2.7 %collective-permute-start.15 = (bf16[2,672,256]{2,1,0:T(8,128)(2,1)S(1)}, bf16[2,672,256]{2,1,0:T(8,128)(2,1)S(1)}, u32[]{:S(2)}, u32[]{:S(2)}) collective-permute-start(bf16[2,672,256]{2,1,0:T(8,128)(2,1)S(1)} %get-tuple-element.90), channel_id=1, source_target_pairs={{0,8},{2,10},{4,12},{6,14},{8,0},{10,2},{12,4},{14,6},{16,24},{18,... | collective-permute-start | bytes 2064392 | tf_op jit(solution)/shard_map/ppermute | solution.py:27
  93.8 6.3 %collective-permute-done.16.refs_4_.refs_3_ = bf16[2,4,256,128]{3,2,1,0:T(8,128)(2,1)S(1)} collective-permute-done((bf16[2,4,256,128]{3,2,1,0:T(8,128)(2,1)S(1)}, bf16[2,4,256,128]{3,2,1,0:T(8,128)(2,1)S(1)}, u32[]{:S(2)}, u32[]{:S(2)}) %collective-permute-start.16) | collective-permute-done | bytes 524320 | tf_op jit(solution)/shard_map/ppermute | solution.py:23
  100.1 4.5 %shard_map.110 = (bf16[672,256]{1,0:T(8,128)(2,1)S(1)}, bf16[672,256]{1,0:T(8,128)(2,1)S(1)}, bf16[2,672,256]{2,1,0:T(8,128)(2,1)S(1)}) custom-call(s32[11]{0:T(128)S(1)} %pad_add_fusion.info_ref.info, bf16[256,2688]{1,0:T(8,128)(2,1)S(1)} %copy-done.2, bf16[384,2688]{1,0:T(8,128)(2,1)S(1)} %shard_map.108.refs_1_, ...), custom_call_target="tpu_custom_call" | custom-call | flops 1409286144 | bytes 6881280 | tf_op jit(solution)/shard_map/pallas_call | solution.py:308
  104.6 1.6 collective-permute-start.25
  108.2 1.5 collective-permute-start.9
  109.7 5.2 %collective-permute-done.15.refs_2_ = bf16[2,672,256]{2,1,0:T(8,128)(2,1)S(1)} collective-permute-done((bf16[2,672,256]{2,1,0:T(8,128)(2,1)S(1)}, bf16[2,672,256]{2,1,0:T(8,128)(2,1)S(1)}, u32[]{:S(2)}, u32[]{:S(2)}) %collective-permute-start.15) | collective-permute-done | bytes 688160 | tf_op jit(solution)/shard_map/ppermute | solution.py:27
  117.6 3.7 %collective-permute-start.20 = (bf16[256,512]{1,0:T(8,128)(2,1)S(1)}, bf16[256,512]{1,0:T(8,128)(2,1)S(1)}, u32[]{:S(2)}, u32[]{:S(2)}) collective-permute-start(bf16[256,512]{1,0:T(8,128)(2,1)S(1)} %get-tuple-element.99), channel_id=1, source_target_pairs={{0,6},{2,4},{4,2},{6,0},{8,14},{10,12},{12,10},{14,8},{16,22},{18,... | collective-permute-start | bytes 786440 | tf_op jit(solution)/shard_map/ppermute | solution.py:27
  123.5 7.5 %shard_map.113 = (f32[1344,256]{1,0:T(8,128)S(1)}, bf16[1344,256]{1,0:T(8,128)(2,1)S(1)}) custom-call(s32[11]{0:T(128)S(1)} %pad_add_fusion.info_ref.info, bf16[256,2048]{1,0:T(8,128)(2,1)S(1)} %shard_map.112.attn_ref, bf16[2048,2688]{1,0:T(8,128)(2,1)S(1)} %bitcast.6), custom_call_target="tpu_custom_call" | custom-call | flops 2818572288 | bytes 11010048 | tf_op jit(solution)/shard_map/pallas_call | solution.py:373
  131.0 5.7 %collective-permute-done.25.refs_2_ = bf16[2,672,256]{2,1,0:T(8,128)(2,1)S(1)} collective-permute-done((bf16[2,672,256]{2,1,0:T(8,128)(2,1)S(1)}, bf16[2,672,256]{2,1,0:T(8,128)(2,1)S(1)}, u32[]{:S(2)}, u32[]{:S(2)}) %collective-permute-start.25) | collective-permute-done | bytes 688160 | tf_op jit(solution)/shard_map/ppermute | solution.py:27
  140.4 1.5 collective-permute-start.23
  141.8 14.4 %collective-permute-done.26.refs_3_ = bf16[672,256]{1,0:T(8,128)(2,1)S(1)} collective-permute-done((bf16[672,256]{1,0:T(8,128)(2,1)S(1)}, bf16[672,256]{1,0:T(8,128)(2,1)S(1)}, u32[]{:S(2)}, u32[]{:S(2)}) %collective-permute-start.26) | collective-permute-done | bytes 344096 | tf_op jit(solution)/shard_map/ppermute | solution.py:27
  159.1 1.5 collective-permute-start.29
  160.6 1.6 shard_map.116.refs_6_
  162.2 1.6 shard_map.117
  163.8 1.5 shard_map.114.refs_4_
  166.1 1.7 collective-permute-done.29.refs_3_
  168.8 1.7 %shard_map.120 = f32[168,2048]{1,0:T(8,128)} custom-call(s32[11]{0:T(128)S(1)} %pad_add_fusion.info_ref.info, bf16[168,512]{1,0:T(8,128)(2,1)S(1)} %get-tuple-element.113.refs_0_, bf16[168,512]{1,0:T(8,128)(2,1)S(1)} %collective-permute-done.27.refs_1_, bf16[168,512]{1,0:T(8,128)(2,1)S(1)} %collective-permute-done.28.refs_2_, ...), custom_call_target="tpu_custom_call" | custom-call | bytes 2064384 | tf_op jit(solution)/shard_map/pallas_call | solution.py:187
  (75 shorter events, 26.7 us)
Async XLA Ops:
  3.0 16.0 %collective-permute-start.3 = (bf16[256,512]{1,0:T(8,128)(2,1)S(1)}, bf16[256,512]{1,0:T(8,128)(2,1)S(1)}, u32[]{:S(2)}, u32[]{:S(2)}) collective-permute-start(bf16[256,512]{1,0:T(8,128)(2,1)S(1)} %get-tuple-element.70), channel_id=1, source_target_pairs={{0,2},{2,0},{4,6},{6,4},{8,10},{10,8},{12,14},{14,12},{16,18},{18,... | collective-permute-start | bytes 786440 | tf_op jit(solution)/shard_map/ppermute | solution.py:27
  6.0 13.4 %collective-permute-start.4 = (bf16[256,512]{1,0:T(8,128)(2,1)S(1)}, bf16[256,512]{1,0:T(8,128)(2,1)S(1)}, u32[]{:S(2)}, u32[]{:S(2)}) collective-permute-start(bf16[256,512]{1,0:T(8,128)(2,1)S(1)} %get-tuple-element.71), channel_id=1, source_target_pairs={{0,4},{2,6},{4,0},{6,2},{8,12},{10,14},{12,8},{14,10},{16,20},{18,... | collective-permute-start | bytes 786440 | tf_op jit(solution)/shard_map/ppermute | solution.py:27
  7.5 11.9 %collective-permute-start.5 = (bf16[256,512]{1,0:T(8,128)(2,1)S(1)}, bf16[256,512]{1,0:T(8,128)(2,1)S(1)}, u32[]{:S(2)}, u32[]{:S(2)}) collective-permute-start(bf16[256,512]{1,0:T(8,128)(2,1)S(1)} %get-tuple-element.72), channel_id=1, source_target_pairs={{0,6},{2,4},{4,2},{6,0},{8,14},{10,12},{12,10},{14,8},{16,22},{18,... | collective-permute-start | bytes 786440 | tf_op jit(solution)/shard_map/ppermute | solution.py:27
  20.1 32.9 %collective-permute-start.6 = (bf16[8,256,256]{2,1,0:T(8,128)(2,1)S(1)}, bf16[8,256,256]{2,1,0:T(8,128)(2,1)S(1)}, u32[]{:S(2)}, u32[]{:S(2)}) collective-permute-start(bf16[8,256,256]{2,1,0:T(8,128)(2,1)S(1)} %shard_map.104.refs_8_.refs_9_), channel_id=1, source_target_pairs={{0,8},{2,10},{4,12},{6,14},{8,16},{10,18},{12,20},{14,22},{16,24},... | collective-permute-start | bytes 3145736 | tf_op jit(solution)/shard_map/ppermute | solution.py:23
  23.8 14.9 %collective-permute-start = (bf16[256,1024]{1,0:T(8,128)(2,1)S(1)}, bf16[256,1024]{1,0:T(8,128)(2,1)S(1)}, u32[]{:S(2)}, u32[]{:S(2)}) collective-permute-start(bf16[256,1024]{1,0:T(8,128)(2,1)S(1)} %get-tuple-element.66.refs_5_), channel_id=1, source_target_pairs={{0,2},{2,0},{4,6},{6,4},{8,10},{10,8},{12,14},{14,12},{16,18},{18,... | collective-permute-start | bytes 1572872 | tf_op jit(solution)/shard_map/ppermute | solution.py:27
  25.3 23.5 %collective-permute-start.1 = (bf16[256,1024]{1,0:T(8,128)(2,1)S(1)}, bf16[256,1024]{1,0:T(8,128)(2,1)S(1)}, u32[]{:S(2)}, u32[]{:S(2)}) collective-permute-start(bf16[256,1024]{1,0:T(8,128)(2,1)S(1)} %get-tuple-element.67.refs_6_), channel_id=1, source_target_pairs={{0,4},{2,6},{4,0},{6,2},{8,12},{10,14},{12,8},{14,10},{16,20},{18,... | collective-permute-start | bytes 1572872 | tf_op jit(solution)/shard_map/ppermute | solution.py:27
  26.9 22.0 %collective-permute-start.2 = (bf16[256,1024]{1,0:T(8,128)(2,1)S(1)}, bf16[256,1024]{1,0:T(8,128)(2,1)S(1)}, u32[]{:S(2)}, u32[]{:S(2)}) collective-permute-start(bf16[256,1024]{1,0:T(8,128)(2,1)S(1)} %get-tuple-element.68.refs_7_), channel_id=1, source_target_pairs={{0,6},{2,4},{4,2},{6,0},{8,14},{10,12},{12,10},{14,8},{16,22},{18,... | collective-permute-start | bytes 1572872 | tf_op jit(solution)/shard_map/ppermute | solution.py:27
  49.4 32.2 %collective-permute-start.10 = (bf16[128,2688]{1,0:T(8,128)(2,1)S(1)}, bf16[128,2688]{1,0:T(8,128)(2,1)S(1)}, u32[]{:S(2)}, u32[]{:S(2)}) collective-permute-start(bf16[128,2688]{1,0:T(8,128)(2,1)S(1)} %shard_map.107), channel_id=1, source_target_pairs={{0,2},{2,0},{4,6},{6,4},{8,10},{10,8},{12,14},{14,12},{16,18},{18,... | collective-permute-start | bytes 2064392 | tf_op jit(solution)/shard_map/ppermute | solution.py:27
  50.7 30.9 %collective-permute-start.11 = (bf16[128,2688]{1,0:T(8,128)(2,1)S(1)}, bf16[128,2688]{1,0:T(8,128)(2,1)S(1)}, u32[]{:S(2)}, u32[]{:S(2)}) collective-permute-start(bf16[128,2688]{1,0:T(8,128)(2,1)S(1)} %shard_map.107), channel_id=1, source_target_pairs={{0,4},{2,6},{4,0},{6,2},{8,12},{10,14},{12,8},{14,10},{16,20},{18,... | collective-permute-start | bytes 2064392 | tf_op jit(solution)/shard_map/ppermute | solution.py:27
  51.6 30.1 %collective-permute-start.12 = (bf16[128,2688]{1,0:T(8,128)(2,1)S(1)}, bf16[128,2688]{1,0:T(8,128)(2,1)S(1)}, u32[]{:S(2)}, u32[]{:S(2)}) collective-permute-start(bf16[128,2688]{1,0:T(8,128)(2,1)S(1)} %shard_map.107), channel_id=1, source_target_pairs={{0,6},{2,4},{4,2},{6,0},{8,14},{10,12},{12,10},{14,8},{16,22},{18,... | collective-permute-start | bytes 2064392 | tf_op jit(solution)/shard_map/ppermute | solution.py:27
  66.6 15.1 %collective-permute-start.13 = (bf16[2,4,256,128]{3,2,1,0:T(8,128)(2,1)S(1)}, bf16[2,4,256,128]{3,2,1,0:T(8,128)(2,1)S(1)}, u32[]{:S(2)}, u32[]{:S(2)}) collective-permute-start(bf16[2,4,256,128]{3,2,1,0:T(8,128)(2,1)S(1)} %get-tuple-element.87), channel_id=1, source_target_pairs={{8,0},{10,2},{12,4},{14,6},{16,8},{18,10},{20,12},{22,14},{24,16},... | collective-permute-start | bytes 1572872 | tf_op jit(solution)/shard_map/ppermute | solution.py:23
  81.7 41.8 %slice-start = ((s8[11010048]{0:T(1024)(128)(4,1)}), s8[4194304]{0:T(1024)(128)(4,1)S(1)}, s32[]{:S(2)}) async-start(s8[11010048]{0:T(1024)(128)(4,1)} %bitcast.5), calls=%async_computation | async-start | bytes 8388608
  82.4 4.2 %collective-permute-start.14 = (bf16[384,2688]{1,0:T(8,128)(2,1)S(1)}, bf16[384,2688]{1,0:T(8,128)(2,1)S(1)}, u32[]{:S(2)}, u32[]{:S(2)}) collective-permute-start(bf16[384,2688]{1,0:T(8,128)(2,1)S(1)} %shard_map.108.refs_1_), channel_id=1, source_target_pairs={{0,1},{1,0},{2,3},{3,2},{4,5},{5,4},{6,7},{7,6},{8,9},{9,8},{10,11... | collective-permute-start | bytes 6193160 | tf_op jit(solution)/shard_map/ppermute | solution.py:27
  82.5 41.0 %slice-start.1 = ((s8[11010048]{0:T(1024)(128)(4,1)}), s8[4194304]{0:T(1024)(128)(4,1)S(1)}, s32[]{:S(2)}) async-start(s8[11010048]{0:T(1024)(128)(4,1)} %bitcast.5), calls=%async_computation.1 | async-start | bytes 8388608
  82.5 17.6 %collective-permute-start.16 = (bf16[2,4,256,128]{3,2,1,0:T(8,128)(2,1)S(1)}, bf16[2,4,256,128]{3,2,1,0:T(8,128)(2,1)S(1)}, u32[]{:S(2)}, u32[]{:S(2)}) collective-permute-start(bf16[2,4,256,128]{3,2,1,0:T(8,128)(2,1)S(1)} %get-tuple-element.91), channel_id=1, source_target_pairs={{8,0},{10,2},{12,4},{14,6},{16,8},{18,10},{20,12},{22,14},{24,16},... | collective-permute-start | bytes 1572872 | tf_op jit(solution)/shard_map/ppermute | solution.py:23
  91.1 23.7 %collective-permute-start.15 = (bf16[2,672,256]{2,1,0:T(8,128)(2,1)S(1)}, bf16[2,672,256]{2,1,0:T(8,128)(2,1)S(1)}, u32[]{:S(2)}, u32[]{:S(2)}) collective-permute-start(bf16[2,672,256]{2,1,0:T(8,128)(2,1)S(1)} %get-tuple-element.90), channel_id=1, source_target_pairs={{0,8},{2,10},{4,12},{6,14},{8,0},{10,2},{12,4},{14,6},{16,24},{18,... | collective-permute-start | bytes 2064392 | tf_op jit(solution)/shard_map/ppermute | solution.py:27
  104.6 32.1 %collective-permute-start.25 = (bf16[2,672,256]{2,1,0:T(8,128)(2,1)S(1)}, bf16[2,672,256]{2,1,0:T(8,128)(2,1)S(1)}, u32[]{:S(2)}, u32[]{:S(2)}) collective-permute-start(bf16[2,672,256]{2,1,0:T(8,128)(2,1)S(1)} %get-tuple-element.110), channel_id=1, source_target_pairs={{0,8},{2,10},{4,12},{6,14},{8,0},{10,2},{12,4},{14,6},{16,24},{18,... | collective-permute-start | bytes 2064392 | tf_op jit(solution)/shard_map/ppermute | solution.py:27
  106.2 10.6 %collective-permute-start.7 = (bf16[256,512]{1,0:T(8,128)(2,1)S(1)}, bf16[256,512]{1,0:T(8,128)(2,1)S(1)}, u32[]{:S(2)}, u32[]{:S(2)}) collective-permute-start(bf16[256,512]{1,0:T(8,128)(2,1)S(1)} %get-tuple-element.82), channel_id=1, source_target_pairs={{0,2},{2,0},{4,6},{6,4},{8,10},{10,8},{12,14},{14,12},{16,18},{18,... | collective-permute-start | bytes 786440 | tf_op jit(solution)/shard_map/ppermute | solution.py:27
  107.4 10.3 %collective-permute-start.8 = (bf16[256,512]{1,0:T(8,128)(2,1)S(1)}, bf16[256,512]{1,0:T(8,128)(2,1)S(1)}, u32[]{:S(2)}, u32[]{:S(2)}) collective-permute-start(bf16[256,512]{1,0:T(8,128)(2,1)S(1)} %get-tuple-element.83), channel_id=1, source_target_pairs={{0,4},{2,6},{4,0},{6,2},{8,12},{10,14},{12,8},{14,10},{16,20},{18,... | collective-permute-start | bytes 786440 | tf_op jit(solution)/shard_map/ppermute | solution.py:27
  108.2 13.8 %collective-permute-start.9 = (bf16[256,512]{1,0:T(8,128)(2,1)S(1)}, bf16[256,512]{1,0:T(8,128)(2,1)S(1)}, u32[]{:S(2)}, u32[]{:S(2)}) collective-permute-start(bf16[256,512]{1,0:T(8,128)(2,1)S(1)} %get-tuple-element.84), channel_id=1, source_target_pairs={{0,6},{2,4},{4,2},{6,0},{8,14},{10,12},{12,10},{14,8},{16,22},{18,... | collective-permute-start | bytes 786440 | tf_op jit(solution)/shard_map/ppermute | solution.py:27
  114.8 22.7 %collective-permute-start.18 = (bf16[256,512]{1,0:T(8,128)(2,1)S(1)}, bf16[256,512]{1,0:T(8,128)(2,1)S(1)}, u32[]{:S(2)}, u32[]{:S(2)}) collective-permute-start(bf16[256,512]{1,0:T(8,128)(2,1)S(1)} %get-tuple-element.97), channel_id=1, source_target_pairs={{0,2},{2,0},{4,6},{6,4},{8,10},{10,8},{12,14},{14,12},{16,18},{18,... | collective-permute-start | bytes 786440 | tf_op jit(solution)/shard_map/ppermute | solution.py:27
  116.8 20.8 %collective-permute-start.19 = (bf16[256,512]{1,0:T(8,128)(2,1)S(1)}, bf16[256,512]{1,0:T(8,128)(2,1)S(1)}, u32[]{:S(2)}, u32[]{:S(2)}) collective-permute-start(bf16[256,512]{1,0:T(8,128)(2,1)S(1)} %get-tuple-element.98), channel_id=1, source_target_pairs={{0,4},{2,6},{4,0},{6,2},{8,12},{10,14},{12,8},{14,10},{16,20},{18,... | collective-permute-start | bytes 786440 | tf_op jit(solution)/shard_map/ppermute | solution.py:27
  117.6 19.9 %collective-permute-start.20 = (bf16[256,512]{1,0:T(8,128)(2,1)S(1)}, bf16[256,512]{1,0:T(8,128)(2,1)S(1)}, u32[]{:S(2)}, u32[]{:S(2)}) collective-permute-start(bf16[256,512]{1,0:T(8,128)(2,1)S(1)} %get-tuple-element.99), channel_id=1, source_target_pairs={{0,6},{2,4},{4,2},{6,0},{8,14},{10,12},{12,10},{14,8},{16,22},{18,... | collective-permute-start | bytes 786440 | tf_op jit(solution)/shard_map/ppermute | solution.py:27
  122.0 14.7 %collective-permute-start.24 = (bf16[672,256]{1,0:T(8,128)(2,1)S(1)}, bf16[672,256]{1,0:T(8,128)(2,1)S(1)}, u32[]{:S(2)}, u32[]{:S(2)}) collective-permute-start(bf16[672,256]{1,0:T(8,128)(2,1)S(1)} %get-tuple-element.93.refs_4_.refs_10_), channel_id=1, source_target_pairs={{0,16},{2,18},{4,20},{6,22},{8,24},{10,26},{12,28},{14,30},{16,0},... | collective-permute-start | bytes 1032200 | tf_op jit(solution)/shard_map/ppermute | solution.py:27
  136.7 27.1 %collective-permute-start.17 = (bf16[1344,256]{1,0:T(8,128)(2,1)S(1)}, bf16[1344,256]{1,0:T(8,128)(2,1)S(1)}, u32[]{:S(2)}, u32[]{:S(2)}) collective-permute-start(bf16[1344,256]{1,0:T(8,128)(2,1)S(1)} %get-tuple-element.95.refs_4_), channel_id=1, source_target_pairs={{0,1},{1,0},{2,3},{3,2},{4,5},{5,4},{6,7},{7,6},{8,9},{9,8},{10,11... | collective-permute-start | bytes 2064392 | tf_op jit(solution)/shard_map/ppermute | solution.py:27
  137.4 18.8 %collective-permute-start.26 = (bf16[672,256]{1,0:T(8,128)(2,1)S(1)}, bf16[672,256]{1,0:T(8,128)(2,1)S(1)}, u32[]{:S(2)}, u32[]{:S(2)}) collective-permute-start(bf16[672,256]{1,0:T(8,128)(2,1)S(1)} %get-tuple-element.112), channel_id=1, source_target_pairs={{0,16},{2,18},{4,20},{6,22},{8,24},{10,26},{12,28},{14,30},{16,0},... | collective-permute-start | bytes 1032200 | tf_op jit(solution)/shard_map/ppermute | solution.py:27
  138.3 20.0 %collective-permute-start.21 = (bf16[256,512]{1,0:T(8,128)(2,1)S(1)}, bf16[256,512]{1,0:T(8,128)(2,1)S(1)}, u32[]{:S(2)}, u32[]{:S(2)}) collective-permute-start(bf16[256,512]{1,0:T(8,128)(2,1)S(1)} %get-tuple-element.103.refs_5_), channel_id=1, source_target_pairs={{0,2},{2,0},{4,6},{6,4},{8,10},{10,8},{12,14},{14,12},{16,18},{18,... | collective-permute-start | bytes 786440 | tf_op jit(solution)/shard_map/ppermute | solution.py:27
  139.6 19.5 %collective-permute-start.22 = (bf16[256,512]{1,0:T(8,128)(2,1)S(1)}, bf16[256,512]{1,0:T(8,128)(2,1)S(1)}, u32[]{:S(2)}, u32[]{:S(2)}) collective-permute-start(bf16[256,512]{1,0:T(8,128)(2,1)S(1)} %get-tuple-element.104.refs_6_), channel_id=1, source_target_pairs={{0,4},{2,6},{4,0},{6,2},{8,12},{10,14},{12,8},{14,10},{16,20},{18,... | collective-permute-start | bytes 786440 | tf_op jit(solution)/shard_map/ppermute | solution.py:27
  140.4 21.8 %collective-permute-start.23 = (bf16[256,512]{1,0:T(8,128)(2,1)S(1)}, bf16[256,512]{1,0:T(8,128)(2,1)S(1)}, u32[]{:S(2)}, u32[]{:S(2)}) collective-permute-start(bf16[256,512]{1,0:T(8,128)(2,1)S(1)} %get-tuple-element.105.refs_7_), channel_id=1, source_target_pairs={{0,6},{2,4},{4,2},{6,0},{8,14},{10,12},{12,10},{14,8},{16,22},{18,... | collective-permute-start | bytes 786440 | tf_op jit(solution)/shard_map/ppermute | solution.py:27
  157.0 8.3 %collective-permute-start.27 = (bf16[168,512]{1,0:T(8,128)(2,1)S(1)}, bf16[168,512]{1,0:T(8,128)(2,1)S(1)}, u32[]{:S(2)}, u32[]{:S(2)}) collective-permute-start(bf16[168,512]{1,0:T(8,128)(2,1)S(1)} %get-tuple-element.114), channel_id=1, source_target_pairs={{0,2},{2,0},{4,6},{6,4},{8,10},{10,8},{12,14},{14,12},{16,18},{18,... | collective-permute-start | bytes 516104 | tf_op jit(solution)/shard_map/ppermute | solution.py:27
  158.3 7.8 %collective-permute-start.28 = (bf16[168,512]{1,0:T(8,128)(2,1)S(1)}, bf16[168,512]{1,0:T(8,128)(2,1)S(1)}, u32[]{:S(2)}, u32[]{:S(2)}) collective-permute-start(bf16[168,512]{1,0:T(8,128)(2,1)S(1)} %get-tuple-element.115), channel_id=1, source_target_pairs={{0,4},{2,6},{4,0},{6,2},{8,12},{10,14},{12,8},{14,10},{16,20},{18,... | collective-permute-start | bytes 516104 | tf_op jit(solution)/shard_map/ppermute | solution.py:27
  159.1 8.6 %collective-permute-start.29 = (bf16[168,512]{1,0:T(8,128)(2,1)S(1)}, bf16[168,512]{1,0:T(8,128)(2,1)S(1)}, u32[]{:S(2)}, u32[]{:S(2)}) collective-permute-start(bf16[168,512]{1,0:T(8,128)(2,1)S(1)} %get-tuple-element.116), channel_id=1, source_target_pairs={{0,6},{2,4},{4,2},{6,0},{8,14},{10,12},{12,10},{14,8},{16,22},{18,... | collective-permute-start | bytes 516104 | tf_op jit(solution)/shard_map/ppermute | solution.py:27
  (10 other events, 84.5 us)

commit v4 on v3

--- a/solution.py
+++ b/solution.py
@@ -104,7 +104,8 @@
             back[m, 1, :, h * HEAD : (h + 1) * HEAD] = dq[h * rows : (h + 1) * rows]
         return carry
 
-    lax.fori_loop(0, GROUP, block, 0)
+    for m in range(GROUP):
+        block(m, 0)
     for m in range(GROUP):
         width = back.shape[3]
         for i in range(2):
@@ -272,7 +273,7 @@
         ),
     )(info, out_grad, out_weight)
 
-def weight_terms(info, pieces, attn_cat, after=()):
+def weight_terms(info, pieces, attn_cat, near, after=()):
     d_out, width = pieces[0].shape[1], attn_cat.shape[1]
     block = 3 * HEAD if d_out % (3 * HEAD) == 0 else d_out
     steps, cut = d_out // block, d_out // GROUP
@@ -299,8 +300,8 @@
                 return whole[pl.ds(pl.multiple_of((info_ref[2] ^ m) * cut, 16), cut)]
 
             own[...] = chunk(0)
-            other[...] = chunk(2)
-            away[0] = chunk(1)
+            other[...] = chunk(3 ^ near)
+            away[0] = chunk(near)
             away[1] = chunk(3)
 
     shapes = [(cut, width), (cut, width), (2, cut, width)]
@@ -324,12 +325,12 @@
     )(info, *pieces, attn_cat, *after)
 
 
-def split_sums(info, pairs):
+def split_sums(info, pairs, after):
     rows, width = pairs[0][0].shape
     cut, count = rows // GROUP, len(pairs)
 
     def kernel(info_ref, *refs):
-        outs, total = refs[2 * count : 2 * count + GROUP], refs[2 * count + GROUP]
+        outs, total = refs[-1 - GROUP : -1], refs[-1]
         for g in range(count):
             total[...] = refs[2 * g][...].astype(jnp.float32) + refs[2 * g + 1][...].astype(jnp.float32)
             for m in range(GROUP):
@@ -342,12 +343,12 @@
     return pl.pallas_call(
         kernel,
         grid=(1,),
-        in_specs=[SMEM] + [entire(a) for a in flat],
+        in_specs=[SMEM] + [entire(a) for a in flat] + [ANY] * len(after),
         out_specs=[entire(a) for a in out],
         out_shape=out,
         scratch_shapes=[pltpu.VMEM((rows, width), jnp.float32)],
         compiler_params=pltpu.CompilerParams(vmem_limit_bytes=32 * 1024 * 1024),
-    )(info, *flat)
+    )(info, *flat, *after)
 
 
 def project(info, attn, out_weight, after):
@@ -447,22 +448,33 @@
     near_shape = shape((GROUP - 1) * (rows // 2), d_out)
     near = moved(pack_near, info, near, [near_shape], [*attn_cats, far_grads[0]])[0]
     pieces = [out_grad, near, swapped(near, "tp", 1)]
-    all_terms = [weight_terms(info, pieces, attn_cats[0])]
+    steps = [1, 2]
+    all_terms = [weight_terms(info, pieces, attn_cats[0], steps[0])]
     for g in range(1, kv_heads):
-        all_terms.append(weight_terms(info, pieces, attn_cats[g], [far_grads[g]]))
+        all_terms.append(weight_terms(info, pieces, attn_cats[g], steps[g], [far_grads[g], all_terms[0][0]]))
 
     def add_pair(info_ref, ins, outs):
         for i in range(2):
             outs[i][...] = (ins[i][...].astype(f32) + ins[2][i].astype(f32)).astype(outs[i].dtype)
 
-    def add_layers(terms, after):
+    def add_layers(terms, near, after):
         own, other, away = terms
-        met = swapped(away, "ctx", GROUP)
+        met = swapped(away, "ctx", near * GROUP)
         pair_shape = [shape(*own.shape, dtype=f32), shape(*own.shape)]
         own, other = moved(add_pair, info, [own, other, met], pair_shape, after)
-        return own, other, swapped(other, "ctx", 2 * GROUP)
-
-    sums = [add_layers(all_terms[0], all_terms[-1][:1])]
+        return own, other, swapped(other, "ctx", (3 ^ near) * GROUP)
+
+    def lay_out(info_ref, ins, outs):
+        for m in members:
+            start = pl.multiple_of((info_ref[0] ^ m) * q_width, HEAD)
+            outs[0][:, pl.ds(start, q_width)] = ins[m][...]
+
+    attn = moved(lay_out, info, attn, [shape(rows, GROUP * q_width)], all_terms[-1][:1])[0]
+    mine, theirs = project(info, attn, out_weight, [])
+    sums, after = [], [theirs]
+    for terms, near in zip(all_terms, steps):
+        sums.append(add_layers(terms, near, after))
+        after = [sums[-1][1]]
 
     def add_up(info_ref, ins, outs):
         for g in range(kv_heads):
@@ -479,18 +491,10 @@
                 outs[i][:, pl.ds(start, kv_width)] = ins[m][:, i * kv_width : (i + 1) * kv_width]
 
     total_shape = [shape(rows, 2 * kv_width)] * GROUP
-    totals = moved(add_up, info, own_grads + far_grads, total_shape, [*attn[1:], *query_grad[1:], sums[0][1]])
-    key_grad, value_grad = moved(lay_out_kv, info, traded(totals), [shape(rows, GROUP * kv_width)] * 2)
-
-    def lay_out(info_ref, ins, outs):
-        for m in members:
-            start = pl.multiple_of((info_ref[0] ^ m) * q_width, HEAD)
-            outs[0][:, pl.ds(start, q_width)] = ins[m][...]
-
-    attn = moved(lay_out, info, attn, [shape(rows, GROUP * q_width)], sums[0][1:2])[0]
-    mine, theirs = project(info, attn, out_weight, [])
-    for terms in all_terms[1:]:
-        sums.append(add_layers(terms, [sums[-1][2], theirs]))
+    totals = moved(add_up, info, own_grads + far_grads, total_shape, [*query_grad[1:], sums[0][1]])
+    handed = traded(totals)
+    key_grad, value_grad = moved(lay_out_kv, info, handed, [shape(rows, GROUP * kv_width)] * 2)
+
     query_grad = moved(lay_out, info, query_grad, [shape(rows, GROUP * q_width)], totals)[0]
 
     def add_shares(info_ref, ins, outs):
@@ -504,9 +508,9 @@
             start = pl.multiple_of((info_ref[0] ^ m) * q_width, HEAD)
             outs[0][:, pl.ds(start, q_width)] = ins[m][...].astype(f32)
 
-    blocks = traded(split_sums(info, [(own, met) for own, other, met in sums]))
+    blocks = traded(split_sums(info, [(own, met) for own, other, met in sums], handed[1:]))
     grad_shape = [shape(d_out // GROUP // GROUP, GROUP * q_width, dtype=f32)]
-    late = [attn_output, key_grad, query_grad]
+    late = []
     out_weight_grad = moved(lay_out_weight, info, blocks, grad_shape, late)[0].T
     return (attn_output.T, query_grad, key_grad, value_grad, out_weight_grad)
 

time: 171 us -> 165 us (0.965)
  waiting for transfers between devices: 58.8 us -> 54.9 us
    ppermute x3, waiting for transfers between devices: 6.29 us -> 2.81 us  [shifted(): return lax.ppermute(shard, axis, pairs)]
    unnamed x24 -> x18, local copies, waits for them, and re-layouts: 8.68 us -> 7.57 us
  transfers between devices with their start and end apart: 30 -> 30, of which waited for: 11 -> 12; matrix products, arithmetic and copies ran while one was open for 0% -> 0% of each run, Pallas kernels for 34% -> 34%
where the time goes in v4:
time: 165 us
  Pallas kernels  59.7 us (36%)
  waiting for transfers between devices  54.9 us (33%)
  starting transfers between devices  40.9 us (25%)
  local copies, waits for them, and re-layouts  8.3 us (5%)
    ppermute x27, waiting for transfers between devices, swapped(): lax.ppermute(shard, axis, [(i, i ^ by) for i in range(lax.axis_size(axis))])  52.1 us
    ppermute x27, starting transfers between devices, swapped(): lax.ppermute(shard, axis, [(i, i ^ by) for i in range(lax.axis_size(axis))])  33.9 us
    pallas_call x2, Pallas kernels, attention(): pl.pallas_call(functools.partial(attention_kernel, rows, len(held)), grid...  25.8 us
    pallas_call x12, Pallas kernels, moved(): pl.pallas_call(kernel, grid=(1,), in_specs=[SMEM] + [entire(a) for a in a...  11.9 us
    pallas_call x2, Pallas kernels, weight_terms(): pl.pallas_call(kernel, grid=(steps,), in_specs=[SMEM] + [pl.BlockSpec((p....  9.05 us
    unnamed x18, local copies, waits for them, and re-layouts  7.57 us
    pallas_call x1, Pallas kernels, project(): pl.pallas_call(kernel, grid=(steps,), in_specs=[SMEM, entire(attn), pl.Bl...  7.54 us
    ppermute x3, starting transfers between devices, shifted(): return lax.ppermute(shard, axis, pairs)  6.94 us
  transfers between devices with their start and end apart: 30, of which 12 were waited for; matrix products, arithmetic and copies ran while one was open for 0% of the time, Pallas kernels for 34%

profile of v4, /device:TPU:0, one launch (start us, length us, event | category | flops | bytes accessed | tf_op | source)
XLA Modules:
  0.0 164.8 jit_solution(13044765791899963534)
XLA Ops:
  3.0 3.0 %collective-permute-start.3 = (bf16[256,512]{1,0:T(8,128)(2,1)S(1)}, bf16[256,512]{1,0:T(8,128)(2,1)S(1)}, u32[]{:S(2)}, u32[]{:S(2)}) collective-permute-start(bf16[256,512]{1,0:T(8,128)(2,1)S(1)} %get-tuple-element.70), channel_id=1, source_target_pairs={{0,2},{2,0},{4,6},{6,4},{8,10},{10,8},{12,14},{14,12},{16,18},{18,... | collective-permute-start | bytes 786440 | tf_op jit(solution)/shard_map/ppermute | solution.py:27
  6.0 1.5 collective-permute-start.4
  8.3 4.1 %copy-done = bf16[2048,2688]{1,0:T(8,128)(2,1)S(1)} copy-done((bf16[2048,2688]{1,0:T(8,128)(2,1)S(1)}, bf16[2048,2688]{1,0:T(8,128)(2,1)}, u32[]{:S(2)}) %copy-start) | copy-done | bytes 11010072
  13.8 4.5 %shard_map.101 = (bf16[256,512]{1,0:T(8,128)(2,1)S(1)}, bf16[256,512]{1,0:T(8,128)(2,1)S(1)}, bf16[256,512]{1,0:T(8,128)(2,1)S(1)}, bf16[256,512]{1,0:T(8,128)(2,1)S(1)}) custom-call(s32[11]{0:T(128)S(1)} %pad_add_fusion.info_ref.info, bf16[256,2688]{1,0:T(8,128)(2,1)S(1)} %copy-done.1, bf16[2048,2688]{1,0:T(8,128)(2,1)S(1)} %copy-done), custom_call_target="tpu_custom_call" | custom-call | flops 2818572288 | bytes 11010048 | tf_op jit(solution)/shard_map/pallas_call | solution.py:258
  20.1 3.7 %collective-permute-start.6 = (bf16[8,256,256]{2,1,0:T(8,128)(2,1)S(1)}, bf16[8,256,256]{2,1,0:T(8,128)(2,1)S(1)}, u32[]{:S(2)}, u32[]{:S(2)}) collective-permute-start(bf16[8,256,256]{2,1,0:T(8,128)(2,1)S(1)} %shard_map.104.refs_8_.refs_9_), channel_id=1, source_target_pairs={{0,8},{2,10},{4,12},{6,14},{8,16},{10,18},{12,20},{14,22},{16,24},... | collective-permute-start | bytes 3145736 | tf_op jit(solution)/shard_map/ppermute | solution.py:23
  23.8 1.6 collective-permute-start
  25.3 1.5 collective-permute-start.1
  27.3 11.4 %collective-permute-done.refs_1_.refs_5_ = bf16[256,1024]{1,0:T(8,128)(2,1)S(1)} collective-permute-done((bf16[256,1024]{1,0:T(8,128)(2,1)S(1)}, bf16[256,1024]{1,0:T(8,128)(2,1)S(1)}, u32[]{:S(2)}, u32[]{:S(2)}) %collective-permute-start) | collective-permute-done | bytes 524320 | tf_op jit(solution)/shard_map/ppermute | solution.py:27
  38.7 10.1 %collective-permute-done.1.refs_2_.refs_6_ = bf16[256,1024]{1,0:T(8,128)(2,1)S(1)} collective-permute-done((bf16[256,1024]{1,0:T(8,128)(2,1)S(1)}, bf16[256,1024]{1,0:T(8,128)(2,1)S(1)}, u32[]{:S(2)}, u32[]{:S(2)}) %collective-permute-start.1) | collective-permute-done | bytes 524320 | tf_op jit(solution)/shard_map/ppermute | solution.py:27
  51.6 1.4 collective-permute-start.12
  53.0 12.8 %shard_map.105 = (bf16[256,256]{1,0:T(8,128)(2,1)S(1)}, bf16[256,256]{1,0:T(8,128)(2,1)S(1)}, bf16[256,256]{1,0:T(8,128)(2,1)S(1)}, bf16[256,256]{1,0:T(8,128)(2...) custom-call(s32[11]{0:T(128)S(1)} %pad_add_fusion.info_ref.info, ...), custom_call_target="tpu_custom_call" | custom-call | flops 4026531840 | bytes 5242880 | tf_op jit(solution)/shard_map/pallas_call | solution.py:151
  65.8 1.5 collective-permute-start.13
  67.3 12.9 %shard_map.106 = (bf16[256,512]{1,0:T(8,128)(2,1)S(1)}, bf16[256,512]{1,0:T(8,128)(2,1)S(1)}, bf16[256,512]{1,0:T(8,128)(2,1)S(1)}, bf16[256,512]{1,0:T(8,128)(2...) custom-call(s32[11]{0:T(128)S(1)} %pad_add_fusion.info_ref.info, ...), custom_call_target="tpu_custom_call" | custom-call | flops 4026531840 | bytes 5242880 | tf_op jit(solution)/shard_map/pallas_call | solution.py:151
  81.1 1.8 %collective-permute-start.15 = (bf16[2,4,256,128]{3,2,1,0:T(8,128)(2,1)S(1)}, bf16[2,4,256,128]{3,2,1,0:T(8,128)(2,1)S(1)}, u32[]{:S(2)}, u32[]{:S(2)}) collective-permute-start(bf16[2,4,256,128]{3,2,1,0:T(8,128)(2,1)S(1)} %get-tuple-element.88), channel_id=1, source_target_pairs={{8,0},{10,2},{12,4},{14,6},{16,8},{18,10},{20,12},{22,14},{24,16},... | collective-permute-start | bytes 1572872 | tf_op jit(solution)/shard_map/ppermute | solution.py:23
  82.9 2.3 %collective-permute-done.14.refs_2_ = bf16[384,2688]{1,0:T(8,128)(2,1)S(1)} collective-permute-done((bf16[384,2688]{1,0:T(8,128)(2,1)S(1)}, bf16[384,2688]{1,0:T(8,128)(2,1)S(1)}, u32[]{:S(2)}, u32[]{:S(2)}) %collective-permute-start.14) | collective-permute-done | bytes 2064416 | tf_op jit(solution)/shard_map/ppermute | solution.py:27
  85.2 4.5 %shard_map.109 = (bf16[672,256]{1,0:T(8,128)(2,1)S(1)}, bf16[672,256]{1,0:T(8,128)(2,1)S(1)}, bf16[2,672,256]{2,1,0:T(8,128)(2,1)S(1)}) custom-call(s32[11]{0:T(128)S(1)} %pad_add_fusion.info_ref.info, bf16[256,2688]{1,0:T(8,128)(2,1)S(1)} %copy-done.2, bf16[384,2688]{1,0:T(8,128)(2,1)S(1)} %shard_map.108.refs_1_, ...), custom_call_target="tpu_custom_call" | custom-call | flops 1409286144 | bytes 6881280 | tf_op jit(solution)/shard_map/pallas_call | solution.py:309
  89.7 2.7 %collective-permute-start.20 = (bf16[2,672,256]{2,1,0:T(8,128)(2,1)S(1)}, bf16[2,672,256]{2,1,0:T(8,128)(2,1)S(1)}, u32[]{:S(2)}, u32[]{:S(2)}) collective-permute-start(bf16[2,672,256]{2,1,0:T(8,128)(2,1)S(1)} %get-tuple-element.100), channel_id=1, source_target_pairs={{0,8},{2,10},{4,12},{6,14},{8,0},{10,2},{12,4},{14,6},{16,24},{18,... | collective-permute-start | bytes 2064392 | tf_op jit(solution)/shard_map/ppermute | solution.py:27
  95.9 2.8 %collective-permute-done.15.refs_4_.refs_3_ = bf16[2,4,256,128]{3,2,1,0:T(8,128)(2,1)S(1)} collective-permute-done((bf16[2,4,256,128]{3,2,1,0:T(8,128)(2,1)S(1)}, bf16[2,4,256,128]{3,2,1,0:T(8,128)(2,1)S(1)}, u32[]{:S(2)}, u32[]{:S(2)}) %collective-permute-start.15) | collective-permute-done | bytes 524320 | tf_op jit(solution)/shard_map/ppermute | solution.py:23
  98.7 4.5 %shard_map.110 = (bf16[672,256]{1,0:T(8,128)(2,1)S(1)}, bf16[672,256]{1,0:T(8,128)(2,1)S(1)}, bf16[2,672,256]{2,1,0:T(8,128)(2,1)S(1)}) custom-call(s32[11]{0:T(128)S(1)} %pad_add_fusion.info_ref.info, bf16[256,2688]{1,0:T(8,128)(2,1)S(1)} %copy-done.2, bf16[384,2688]{1,0:T(8,128)(2,1)S(1)} %shard_map.108.refs_1_, ...), custom_call_target="tpu_custom_call" | custom-call | flops 1409286144 | bytes 6881280 | tf_op jit(solution)/shard_map/pallas_call | solution.py:309
  103.2 2.9 %collective-permute-start.25 = (bf16[2,672,256]{2,1,0:T(8,128)(2,1)S(1)}, bf16[2,672,256]{2,1,0:T(8,128)(2,1)S(1)}, u32[]{:S(2)}, u32[]{:S(2)}) collective-permute-start(bf16[2,672,256]{2,1,0:T(8,128)(2,1)S(1)} %get-tuple-element.110), channel_id=1, source_target_pairs={{0,16},{2,18},{4,20},{6,22},{8,24},{10,26},{12,28},{14,30},{16,0},... | collective-permute-start | bytes 2064392 | tf_op jit(solution)/shard_map/ppermute | solution.py:27
  108.2 1.4 collective-permute-start.19
  110.3 7.5 %shard_map.112 = (f32[1344,256]{1,0:T(8,128)S(1)}, bf16[1344,256]{1,0:T(8,128)(2,1)S(1)}) custom-call(s32[11]{0:T(128)S(1)} %pad_add_fusion.info_ref.info, bf16[256,2048]{1,0:T(8,128)(2,1)S(1)} %shard_map.111.attn_ref, bf16[2048,2688]{1,0:T(8,128)(2,1)S(1)} %bitcast.6), custom_call_target="tpu_custom_call" | custom-call | flops 2818572288 | bytes 11010048 | tf_op jit(solution)/shard_map/pallas_call | solution.py:374
  117.9 4.3 %collective-permute-done.20.refs_2_ = bf16[2,672,256]{2,1,0:T(8,128)(2,1)S(1)} collective-permute-done((bf16[2,672,256]{2,1,0:T(8,128)(2,1)S(1)}, bf16[2,672,256]{2,1,0:T(8,128)(2,1)S(1)}, u32[]{:S(2)}, u32[]{:S(2)}) %collective-permute-start.20) | collective-permute-done | bytes 688160 | tf_op jit(solution)/shard_map/ppermute | solution.py:27
  125.0 11.0 %collective-permute-done.25.refs_2_ = bf16[2,672,256]{2,1,0:T(8,128)(2,1)S(1)} collective-permute-done((bf16[2,672,256]{2,1,0:T(8,128)(2,1)S(1)}, bf16[2,672,256]{2,1,0:T(8,128)(2,1)S(1)}, u32[]{:S(2)}, u32[]{:S(2)}) %collective-permute-start.25) | collective-permute-done | bytes 688160 | tf_op jit(solution)/shard_map/ppermute | solution.py:27
  136.7 2.1 %collective-permute-start.24 = (bf16[672,256]{1,0:T(8,128)(2,1)S(1)}, bf16[672,256]{1,0:T(8,128)(2,1)S(1)}, u32[]{:S(2)}, u32[]{:S(2)}) collective-permute-start(bf16[672,256]{1,0:T(8,128)(2,1)S(1)} %get-tuple-element.101.refs_7_.refs_3_), channel_id=1, source_target_pairs={{0,16},{2,18},{4,20},{6,22},{8,24},{10,26},{12,28},{14,30},{16,0},... | collective-permute-start | bytes 1032200 | tf_op jit(solution)/shard_map/ppermute | solution.py:27
  138.8 1.5 collective-permute-start.22
  141.5 9.0 %collective-permute-done.22.refs_2_.refs_5_ = bf16[256,512]{1,0:T(8,128)(2,1)S(1)} collective-permute-done((bf16[256,512]{1,0:T(8,128)(2,1)S(1)}, bf16[256,512]{1,0:T(8,128)(2,1)S(1)}, u32[]{:S(2)}, u32[]{:S(2)}) %collective-permute-start.22) | collective-permute-done | bytes 262176 | tf_op jit(solution)/shard_map/ppermute | solution.py:27
  151.3 2.5 %collective-permute-done.24.refs_1_ = bf16[672,256]{1,0:T(8,128)(2,1)S(1)} collective-permute-done((bf16[672,256]{1,0:T(8,128)(2,1)S(1)}, bf16[672,256]{1,0:T(8,128)(2,1)S(1)}, u32[]{:S(2)}, u32[]{:S(2)}) %collective-permute-start.24) | collective-permute-done | bytes 344096 | tf_op jit(solution)/shard_map/ppermute | solution.py:27
  158.1 1.6 shard_map.116
  159.7 1.5 shard_map.113
  161.2 1.6 shard_map.117
  163.1 1.7 %shard_map.120 = f32[168,2048]{1,0:T(8,128)} custom-call(s32[11]{0:T(128)S(1)} %pad_add_fusion.info_ref.info, bf16[168,512]{1,0:T(8,128)(2,1)S(1)} %get-tuple-element.113.refs_0_, bf16[168,512]{1,0:T(8,128)(2,1)S(1)} %collective-permute-done.27.refs_1_, bf16[168,512]{1,0:T(8,128)(2,1)S(1)} %collective-permute-done.28.refs_2_, ...), custom_call_target="tpu_custom_call" | custom-call | bytes 2064384 | tf_op jit(solution)/shard_map/pallas_call | solution.py:188
  (69 shorter events, 26.6 us)
Async XLA Ops:
  3.0 16.0 %collective-permute-start.3 = (bf16[256,512]{1,0:T(8,128)(2,1)S(1)}, bf16[256,512]{1,0:T(8,128)(2,1)S(1)}, u32[]{:S(2)}, u32[]{:S(2)}) collective-permute-start(bf16[256,512]{1,0:T(8,128)(2,1)S(1)} %get-tuple-element.70), channel_id=1, source_target_pairs={{0,2},{2,0},{4,6},{6,4},{8,10},{10,8},{12,14},{14,12},{16,18},{18,... | collective-permute-start | bytes 786440 | tf_op jit(solution)/shard_map/ppermute | solution.py:27
  6.0 13.4 %collective-permute-start.4 = (bf16[256,512]{1,0:T(8,128)(2,1)S(1)}, bf16[256,512]{1,0:T(8,128)(2,1)S(1)}, u32[]{:S(2)}, u32[]{:S(2)}) collective-permute-start(bf16[256,512]{1,0:T(8,128)(2,1)S(1)} %get-tuple-element.71), channel_id=1, source_target_pairs={{0,4},{2,6},{4,0},{6,2},{8,12},{10,14},{12,8},{14,10},{16,20},{18,... | collective-permute-start | bytes 786440 | tf_op jit(solution)/shard_map/ppermute | solution.py:27
  7.5 11.9 %collective-permute-start.5 = (bf16[256,512]{1,0:T(8,128)(2,1)S(1)}, bf16[256,512]{1,0:T(8,128)(2,1)S(1)}, u32[]{:S(2)}, u32[]{:S(2)}) collective-permute-start(bf16[256,512]{1,0:T(8,128)(2,1)S(1)} %get-tuple-element.72), channel_id=1, source_target_pairs={{0,6},{2,4},{4,2},{6,0},{8,14},{10,12},{12,10},{14,8},{16,22},{18,... | collective-permute-start | bytes 786440 | tf_op jit(solution)/shard_map/ppermute | solution.py:27
  19.3 29.5 %copy-start.2 = (bf16[256,2688]{1,0:T(8,128)(2,1)S(1)}, bf16[256,2688]{1,0:T(8,128)(2,1)}, u32[]{:S(2)}) copy-start(bf16[256,2688]{1,0:T(8,128)(2,1)} %refs_0_.7) | copy-start | bytes 4128772
  20.1 32.9 %collective-permute-start.6 = (bf16[8,256,256]{2,1,0:T(8,128)(2,1)S(1)}, bf16[8,256,256]{2,1,0:T(8,128)(2,1)S(1)}, u32[]{:S(2)}, u32[]{:S(2)}) collective-permute-start(bf16[8,256,256]{2,1,0:T(8,128)(2,1)S(1)} %shard_map.104.refs_8_.refs_9_), channel_id=1, source_target_pairs={{0,8},{2,10},{4,12},{6,14},{8,16},{10,18},{12,20},{14,22},{16,24},... | collective-permute-start | bytes 3145736 | tf_op jit(solution)/shard_map/ppermute | solution.py:23
  23.8 14.9 %collective-permute-start = (bf16[256,1024]{1,0:T(8,128)(2,1)S(1)}, bf16[256,1024]{1,0:T(8,128)(2,1)S(1)}, u32[]{:S(2)}, u32[]{:S(2)}) collective-permute-start(bf16[256,1024]{1,0:T(8,128)(2,1)S(1)} %get-tuple-element.66.refs_5_), channel_id=1, source_target_pairs={{0,2},{2,0},{4,6},{6,4},{8,10},{10,8},{12,14},{14,12},{16,18},{18,... | collective-permute-start | bytes 1572872 | tf_op jit(solution)/shard_map/ppermute | solution.py:27
  25.3 23.5 %collective-permute-start.1 = (bf16[256,1024]{1,0:T(8,128)(2,1)S(1)}, bf16[256,1024]{1,0:T(8,128)(2,1)S(1)}, u32[]{:S(2)}, u32[]{:S(2)}) collective-permute-start(bf16[256,1024]{1,0:T(8,128)(2,1)S(1)} %get-tuple-element.67.refs_6_), channel_id=1, source_target_pairs={{0,4},{2,6},{4,0},{6,2},{8,12},{10,14},{12,8},{14,10},{16,20},{18,... | collective-permute-start | bytes 1572872 | tf_op jit(solution)/shard_map/ppermute | solution.py:27
  26.9 22.0 %collective-permute-start.2 = (bf16[256,1024]{1,0:T(8,128)(2,1)S(1)}, bf16[256,1024]{1,0:T(8,128)(2,1)S(1)}, u32[]{:S(2)}, u32[]{:S(2)}) collective-permute-start(bf16[256,1024]{1,0:T(8,128)(2,1)S(1)} %get-tuple-element.68.refs_7_), channel_id=1, source_target_pairs={{0,6},{2,4},{4,2},{6,0},{8,14},{10,12},{12,10},{14,8},{16,22},{18,... | collective-permute-start | bytes 1572872 | tf_op jit(solution)/shard_map/ppermute | solution.py:27
  49.4 30.8 %collective-permute-start.10 = (bf16[128,2688]{1,0:T(8,128)(2,1)S(1)}, bf16[128,2688]{1,0:T(8,128)(2,1)S(1)}, u32[]{:S(2)}, u32[]{:S(2)}) collective-permute-start(bf16[128,2688]{1,0:T(8,128)(2,1)S(1)} %shard_map.107), channel_id=1, source_target_pairs={{0,2},{2,0},{4,6},{6,4},{8,10},{10,8},{12,14},{14,12},{16,18},{18,... | collective-permute-start | bytes 2064392 | tf_op jit(solution)/shard_map/ppermute | solution.py:27
  50.7 29.6 %collective-permute-start.11 = (bf16[128,2688]{1,0:T(8,128)(2,1)S(1)}, bf16[128,2688]{1,0:T(8,128)(2,1)S(1)}, u32[]{:S(2)}, u32[]{:S(2)}) collective-permute-start(bf16[128,2688]{1,0:T(8,128)(2,1)S(1)} %shard_map.107), channel_id=1, source_target_pairs={{0,4},{2,6},{4,0},{6,2},{8,12},{10,14},{12,8},{14,10},{16,20},{18,... | collective-permute-start | bytes 2064392 | tf_op jit(solution)/shard_map/ppermute | solution.py:27
  51.6 28.8 %collective-permute-start.12 = (bf16[128,2688]{1,0:T(8,128)(2,1)S(1)}, bf16[128,2688]{1,0:T(8,128)(2,1)S(1)}, u32[]{:S(2)}, u32[]{:S(2)}) collective-permute-start(bf16[128,2688]{1,0:T(8,128)(2,1)S(1)} %shard_map.107), channel_id=1, source_target_pairs={{0,6},{2,4},{4,2},{6,0},{8,14},{10,12},{12,10},{14,8},{16,22},{18,... | collective-permute-start | bytes 2064392 | tf_op jit(solution)/shard_map/ppermute | solution.py:27
  65.8 14.5 %collective-permute-start.13 = (bf16[2,4,256,128]{3,2,1,0:T(8,128)(2,1)S(1)}, bf16[2,4,256,128]{3,2,1,0:T(8,128)(2,1)S(1)}, u32[]{:S(2)}, u32[]{:S(2)}) collective-permute-start(bf16[2,4,256,128]{3,2,1,0:T(8,128)(2,1)S(1)} %get-tuple-element.87), channel_id=1, source_target_pairs={{8,0},{10,2},{12,4},{14,6},{16,8},{18,10},{20,12},{22,14},{24,16},... | collective-permute-start | bytes 1572872 | tf_op jit(solution)/shard_map/ppermute | solution.py:23
  80.3 29.9 %slice-start = ((s8[11010048]{0:T(1024)(128)(4,1)}), s8[4194304]{0:T(1024)(128)(4,1)S(1)}, s32[]{:S(2)}) async-start(s8[11010048]{0:T(1024)(128)(4,1)} %bitcast.5), calls=%async_computation | async-start | bytes 8388608
  81.0 4.2 %collective-permute-start.14 = (bf16[384,2688]{1,0:T(8,128)(2,1)S(1)}, bf16[384,2688]{1,0:T(8,128)(2,1)S(1)}, u32[]{:S(2)}, u32[]{:S(2)}) collective-permute-start(bf16[384,2688]{1,0:T(8,128)(2,1)S(1)} %shard_map.108.refs_1_), channel_id=1, source_target_pairs={{0,1},{1,0},{2,3},{3,2},{4,5},{5,4},{6,7},{7,6},{8,9},{9,8},{10,11... | collective-permute-start | bytes 6193160 | tf_op jit(solution)/shard_map/ppermute | solution.py:27
  81.1 17.6 %collective-permute-start.15 = (bf16[2,4,256,128]{3,2,1,0:T(8,128)(2,1)S(1)}, bf16[2,4,256,128]{3,2,1,0:T(8,128)(2,1)S(1)}, u32[]{:S(2)}, u32[]{:S(2)}) collective-permute-start(bf16[2,4,256,128]{3,2,1,0:T(8,128)(2,1)S(1)} %get-tuple-element.88), channel_id=1, source_target_pairs={{8,0},{10,2},{12,4},{14,6},{16,8},{18,10},{20,12},{22,14},{24,16},... | collective-permute-start | bytes 1572872 | tf_op jit(solution)/shard_map/ppermute | solution.py:23
  89.7 32.4 %collective-permute-start.20 = (bf16[2,672,256]{2,1,0:T(8,128)(2,1)S(1)}, bf16[2,672,256]{2,1,0:T(8,128)(2,1)S(1)}, u32[]{:S(2)}, u32[]{:S(2)}) collective-permute-start(bf16[2,672,256]{2,1,0:T(8,128)(2,1)S(1)} %get-tuple-element.100), channel_id=1, source_target_pairs={{0,8},{2,10},{4,12},{6,14},{8,0},{10,2},{12,4},{14,6},{16,24},{18,... | collective-permute-start | bytes 2064392 | tf_op jit(solution)/shard_map/ppermute | solution.py:27
  92.4 13.7 %collective-permute-start.7 = (bf16[256,512]{1,0:T(8,128)(2,1)S(1)}, bf16[256,512]{1,0:T(8,128)(2,1)S(1)}, u32[]{:S(2)}, u32[]{:S(2)}) collective-permute-start(bf16[256,512]{1,0:T(8,128)(2,1)S(1)} %get-tuple-element.82), channel_id=1, source_target_pairs={{0,2},{2,0},{4,6},{6,4},{8,10},{10,8},{12,14},{14,12},{16,18},{18,... | collective-permute-start | bytes 786440 | tf_op jit(solution)/shard_map/ppermute | solution.py:27
  93.6 13.7 %collective-permute-start.8 = (bf16[256,512]{1,0:T(8,128)(2,1)S(1)}, bf16[256,512]{1,0:T(8,128)(2,1)S(1)}, u32[]{:S(2)}, u32[]{:S(2)}) collective-permute-start(bf16[256,512]{1,0:T(8,128)(2,1)S(1)} %get-tuple-element.83), channel_id=1, source_target_pairs={{0,4},{2,6},{4,0},{6,2},{8,12},{10,14},{12,8},{14,10},{16,20},{18,... | collective-permute-start | bytes 786440 | tf_op jit(solution)/shard_map/ppermute | solution.py:27
  94.5 13.7 %collective-permute-start.9 = (bf16[256,512]{1,0:T(8,128)(2,1)S(1)}, bf16[256,512]{1,0:T(8,128)(2,1)S(1)}, u32[]{:S(2)}, u32[]{:S(2)}) collective-permute-start(bf16[256,512]{1,0:T(8,128)(2,1)S(1)} %get-tuple-element.84), channel_id=1, source_target_pairs={{0,6},{2,4},{4,2},{6,0},{8,14},{10,12},{12,10},{14,8},{16,22},{18,... | collective-permute-start | bytes 786440 | tf_op jit(solution)/shard_map/ppermute | solution.py:27
  103.2 32.7 %collective-permute-start.25 = (bf16[2,672,256]{2,1,0:T(8,128)(2,1)S(1)}, bf16[2,672,256]{2,1,0:T(8,128)(2,1)S(1)}, u32[]{:S(2)}, u32[]{:S(2)}) collective-permute-start(bf16[2,672,256]{2,1,0:T(8,128)(2,1)S(1)} %get-tuple-element.110), channel_id=1, source_target_pairs={{0,16},{2,18},{4,20},{6,22},{8,24},{10,26},{12,28},{14,30},{16,0},... | collective-permute-start | bytes 2064392 | tf_op jit(solution)/shard_map/ppermute | solution.py:27
  106.2 16.7 %collective-permute-start.17 = (bf16[256,512]{1,0:T(8,128)(2,1)S(1)}, bf16[256,512]{1,0:T(8,128)(2,1)S(1)}, u32[]{:S(2)}, u32[]{:S(2)}) collective-permute-start(bf16[256,512]{1,0:T(8,128)(2,1)S(1)} %get-tuple-element.94), channel_id=1, source_target_pairs={{0,2},{2,0},{4,6},{6,4},{8,10},{10,8},{12,14},{14,12},{16,18},{18,... | collective-permute-start | bytes 786440 | tf_op jit(solution)/shard_map/ppermute | solution.py:27
  107.4 15.5 %collective-permute-start.18 = (bf16[256,512]{1,0:T(8,128)(2,1)S(1)}, bf16[256,512]{1,0:T(8,128)(2,1)S(1)}, u32[]{:S(2)}, u32[]{:S(2)}) collective-permute-start(bf16[256,512]{1,0:T(8,128)(2,1)S(1)} %get-tuple-element.95), channel_id=1, source_target_pairs={{0,4},{2,6},{4,0},{6,2},{8,12},{10,14},{12,8},{14,10},{16,20},{18,... | collective-permute-start | bytes 786440 | tf_op jit(solution)/shard_map/ppermute | solution.py:27
  108.2 14.7 %collective-permute-start.19 = (bf16[256,512]{1,0:T(8,128)(2,1)S(1)}, bf16[256,512]{1,0:T(8,128)(2,1)S(1)}, u32[]{:S(2)}, u32[]{:S(2)}) collective-permute-start(bf16[256,512]{1,0:T(8,128)(2,1)S(1)} %get-tuple-element.96), channel_id=1, source_target_pairs={{0,6},{2,4},{4,2},{6,0},{8,14},{10,12},{12,10},{14,8},{16,22},{18,... | collective-permute-start | bytes 786440 | tf_op jit(solution)/shard_map/ppermute | solution.py:27
  123.7 16.6 %collective-permute-start.21 = (bf16[256,512]{1,0:T(8,128)(2,1)S(1)}, bf16[256,512]{1,0:T(8,128)(2,1)S(1)}, u32[]{:S(2)}, u32[]{:S(2)}) collective-permute-start(bf16[256,512]{1,0:T(8,128)(2,1)S(1)} %get-tuple-element.103.refs_5_), channel_id=1, source_target_pairs={{0,2},{2,0},{4,6},{6,4},{8,10},{10,8},{12,14},{14,12},{16,18},{18,... | collective-permute-start | bytes 786440 | tf_op jit(solution)/shard_map/ppermute | solution.py:27
  125.0 34.7 %collective-permute-start.16 = (bf16[1344,256]{1,0:T(8,128)(2,1)S(1)}, bf16[1344,256]{1,0:T(8,128)(2,1)S(1)}, u32[]{:S(2)}, u32[]{:S(2)}) collective-permute-start(bf16[1344,256]{1,0:T(8,128)(2,1)S(1)} %get-tuple-element.92.refs_3_), channel_id=1, source_target_pairs={{0,1},{1,0},{2,3},{3,2},{4,5},{5,4},{6,7},{7,6},{8,9},{9,8},{10,11... | collective-permute-start | bytes 2064392 | tf_op jit(solution)/shard_map/ppermute | solution.py:27
  136.6 14.6 %collective-permute-start.26 = (bf16[672,256]{1,0:T(8,128)(2,1)S(1)}, bf16[672,256]{1,0:T(8,128)(2,1)S(1)}, u32[]{:S(2)}, u32[]{:S(2)}) collective-permute-start(bf16[672,256]{1,0:T(8,128)(2,1)S(1)} %get-tuple-element.112), channel_id=1, source_target_pairs={{0,8},{2,10},{4,12},{6,14},{8,0},{10,2},{12,4},{14,6},{16,24},{18,... | collective-permute-start | bytes 1032200 | tf_op jit(solution)/shard_map/ppermute | solution.py:27
  136.7 17.1 %collective-permute-start.24 = (bf16[672,256]{1,0:T(8,128)(2,1)S(1)}, bf16[672,256]{1,0:T(8,128)(2,1)S(1)}, u32[]{:S(2)}, u32[]{:S(2)}) collective-permute-start(bf16[672,256]{1,0:T(8,128)(2,1)S(1)} %get-tuple-element.101.refs_7_.refs_3_), channel_id=1, source_target_pairs={{0,16},{2,18},{4,20},{6,22},{8,24},{10,26},{12,28},{14,30},{16,0},... | collective-permute-start | bytes 1032200 | tf_op jit(solution)/shard_map/ppermute | solution.py:27
  138.8 11.7 %collective-permute-start.22 = (bf16[256,512]{1,0:T(8,128)(2,1)S(1)}, bf16[256,512]{1,0:T(8,128)(2,1)S(1)}, u32[]{:S(2)}, u32[]{:S(2)}) collective-permute-start(bf16[256,512]{1,0:T(8,128)(2,1)S(1)} %get-tuple-element.104.refs_6_), channel_id=1, source_target_pairs={{0,4},{2,6},{4,0},{6,2},{8,12},{10,14},{12,8},{14,10},{16,20},{18,... | collective-permute-start | bytes 786440 | tf_op jit(solution)/shard_map/ppermute | solution.py:27
  140.3 10.1 %collective-permute-start.23 = (bf16[256,512]{1,0:T(8,128)(2,1)S(1)}, bf16[256,512]{1,0:T(8,128)(2,1)S(1)}, u32[]{:S(2)}, u32[]{:S(2)}) collective-permute-start(bf16[256,512]{1,0:T(8,128)(2,1)S(1)} %get-tuple-element.105.refs_7_), channel_id=1, source_target_pairs={{0,6},{2,4},{4,2},{6,0},{8,14},{10,12},{12,10},{14,8},{16,22},{18,... | collective-permute-start | bytes 786440 | tf_op jit(solution)/shard_map/ppermute | solution.py:27
  154.6 8.3 %collective-permute-start.27 = (bf16[168,512]{1,0:T(8,128)(2,1)S(1)}, bf16[168,512]{1,0:T(8,128)(2,1)S(1)}, u32[]{:S(2)}, u32[]{:S(2)}) collective-permute-start(bf16[168,512]{1,0:T(8,128)(2,1)S(1)} %get-tuple-element.114), channel_id=1, source_target_pairs={{0,2},{2,0},{4,6},{6,4},{8,10},{10,8},{12,14},{14,12},{16,18},{18,... | collective-permute-start | bytes 516104 | tf_op jit(solution)/shard_map/ppermute | solution.py:27
  155.9 7.0 %collective-permute-start.28 = (bf16[168,512]{1,0:T(8,128)(2,1)S(1)}, bf16[168,512]{1,0:T(8,128)(2,1)S(1)}, u32[]{:S(2)}, u32[]{:S(2)}) collective-permute-start(bf16[168,512]{1,0:T(8,128)(2,1)S(1)} %get-tuple-element.115), channel_id=1, source_target_pairs={{0,4},{2,6},{4,0},{6,2},{8,12},{10,14},{12,8},{14,10},{16,20},{18,... | collective-permute-start | bytes 516104 | tf_op jit(solution)/shard_map/ppermute | solution.py:27
  156.7 6.4 %collective-permute-start.29 = (bf16[168,512]{1,0:T(8,128)(2,1)S(1)}, bf16[168,512]{1,0:T(8,128)(2,1)S(1)}, u32[]{:S(2)}, u32[]{:S(2)}) collective-permute-start(bf16[168,512]{1,0:T(8,128)(2,1)S(1)} %get-tuple-element.116), channel_id=1, source_target_pairs={{0,6},{2,4},{4,2},{6,0},{8,14},{10,12},{12,10},{14,8},{16,22},{18,... | collective-permute-start | bytes 516104 | tf_op jit(solution)/shard_map/ppermute | solution.py:27
  (7 other events, 52.8 us)

commit v5 on v4

--- a/solution.py
+++ b/solution.py
@@ -133,13 +133,12 @@
     return pl.BlockSpec(array.shape, lambda i: (0,) * len(array.shape))
 
 
-def attention(info, q_and_d, kv_own, kv_far, g, held):
-    kv_heads = kv_own.shape[0] // GROUP
+def attention(info, q_and_d, kv_own, kv_far, g, kv_heads, held):
     rows, q_block = q_and_d[0].shape[0], q_and_d[0].shape[1] // 2 // kv_heads
     q_spec = pl.BlockSpec((rows, q_block), lambda i: (0, g))
     g_spec = pl.BlockSpec((rows, q_block), lambda i: (0, g + kv_heads))
-    k_spec = pl.BlockSpec((GROUP, rows, HEAD), lambda i: (g, 0, 0))
-    v_spec = pl.BlockSpec((GROUP, rows, HEAD), lambda i: (g, 0, 1))
+    k_spec = pl.BlockSpec((GROUP, rows, HEAD), lambda i: (0, 0, 0))
+    v_spec = pl.BlockSpec((GROUP, rows, HEAD), lambda i: (0, 0, 1))
     kv_shape = (2, GROUP, rows, HEAD)
     bf16 = jnp.bfloat16
     blocks = 2 * GROUP
@@ -422,10 +421,10 @@
             for g in range(kv_heads):
                 for i in range(2):
                     at = (i * kv_heads + g) * HEAD
-                    outs[0][g * GROUP + m, :, i * HEAD : (i + 1) * HEAD] = ins[m][:, at : at + HEAD]
-
-    kv_own = moved(pack_heads, info, kv, [shape(kv_heads * GROUP, rows, 2 * HEAD)], packed)[0]
-    kv_far = shifted(kv_own, "ctx", GROUP)
+                    outs[g][m, :, i * HEAD : (i + 1) * HEAD] = ins[m][:, at : at + HEAD]
+
+    kv_own = moved(pack_heads, info, kv, [shape(GROUP, rows, 2 * HEAD)] * kv_heads, packed)
+    kv_far = [shifted(a, "ctx", GROUP) for a in kv_own]
 
     def pack_half(info_ref, ins, outs):
         outs[0][...] = ins[0][pl.ds(pl.multiple_of(info_ref[1] * (rows // 2), 16), rows // 2), :]
@@ -439,7 +438,7 @@
 
     parts, held = [], []
     for g in range(kv_heads):
-        parts.append(attention(info, q_and_d, kv_own, kv_far, g, held))
+        parts.append(attention(info, q_and_d, kv_own[g], kv_far[g], g, kv_heads, held))
         held = parts[-1][: 2 * GROUP]
     far_grads = [shifted(p[-1], "ctx", -GROUP) for p in parts]
     own_grads = [p[-2] for p in parts]

time: 165 us -> 161 us (0.976)
  waiting for transfers between devices: 54.9 us -> 47 us
  starting transfers between devices: 40.9 us -> 44.8 us
    ppermute x27, waiting for transfers between devices: 52.1 us -> 44.2 us  [swapped(): lax.ppermute(shard, axis, [(i, i ^ by) for i in range(lax.axis_size(axis))])]
    ppermute x3 -> x4, starting transfers between devices: 6.94 us -> 10.7 us  [shifted(): return lax.ppermute(shard, axis, pairs)]
  transfers between devices with their start and end apart: 30 -> 31, of which waited for: 12 -> 11; matrix products, arithmetic and copies ran while one was open for 0% -> 1% of each run, Pallas kernels for 34% -> 36%
where the time goes in v5:
time: 161 us
  Pallas kernels  59.7 us (37%)
  waiting for transfers between devices  47 us (29%)
  starting transfers between devices  44.8 us (28%)
  local copies, waits for them, and re-layouts  8.3 us (5%)
    ppermute x27, waiting for transfers between devices, swapped(): lax.ppermute(shard, axis, [(i, i ^ by) for i in range(lax.axis_size(axis))])  44.2 us
    ppermute x27, starting transfers between devices, swapped(): lax.ppermute(shard, axis, [(i, i ^ by) for i in range(lax.axis_size(axis))])  34.1 us
    pallas_call x2, Pallas kernels, attention(): pl.pallas_call(functools.partial(attention_kernel, rows, len(held)), grid...  25.8 us
    pallas_call x12, Pallas kernels, moved(): pl.pallas_call(kernel, grid=(1,), in_specs=[SMEM] + [entire(a) for a in a...  11.9 us
    ppermute x4, starting transfers between devices, shifted(): return lax.ppermute(shard, axis, pairs)  10.7 us
    pallas_call x2, Pallas kernels, weight_terms(): pl.pallas_call(kernel, grid=(steps,), in_specs=[SMEM] + [pl.BlockSpec((p....  9.05 us
    unnamed x18, local copies, waits for them, and re-layouts  7.57 us
    pallas_call x1, Pallas kernels, project(): pl.pallas_call(kernel, grid=(steps,), in_specs=[SMEM, entire(attn), pl.Bl...  7.54 us
  transfers between devices with their start and end apart: 31, of which 11 were waited for; matrix products, arithmetic and copies ran while one was open for 1% of the time, Pallas kernels for 36%

profile of v5, /device:TPU:0, one launch (start us, length us, event | category | flops | bytes accessed | tf_op | source)
XLA Modules:
  0.0 160.8 jit_solution(6203148892146459900)
XLA Ops:
  3.0 3.0 %collective-permute-start.3 = (bf16[256,512]{1,0:T(8,128)(2,1)S(1)}, bf16[256,512]{1,0:T(8,128)(2,1)S(1)}, u32[]{:S(2)}, u32[]{:S(2)}) collective-permute-start(bf16[256,512]{1,0:T(8,128)(2,1)S(1)} %get-tuple-element.72), channel_id=1, source_target_pairs={{0,2},{2,0},{4,6},{6,4},{8,10},{10,8},{12,14},{14,12},{16,18},{18,... | collective-permute-start | bytes 786440 | tf_op jit(solution)/shard_map/ppermute | solution.py:27
  6.0 1.5 collective-permute-start.4
  8.3 4.1 %copy-done = bf16[2048,2688]{1,0:T(8,128)(2,1)S(1)} copy-done((bf16[2048,2688]{1,0:T(8,128)(2,1)S(1)}, bf16[2048,2688]{1,0:T(8,128)(2,1)}, u32[]{:S(2)}) %copy-start) | copy-done | bytes 11010072
  13.8 4.5 %shard_map.101 = (bf16[256,512]{1,0:T(8,128)(2,1)S(1)}, bf16[256,512]{1,0:T(8,128)(2,1)S(1)}, bf16[256,512]{1,0:T(8,128)(2,1)S(1)}, bf16[256,512]{1,0:T(8,128)(2,1)S(1)}) custom-call(s32[11]{0:T(128)S(1)} %pad_add_fusion.info_ref.info, bf16[256,2688]{1,0:T(8,128)(2,1)S(1)} %copy-done.1, bf16[2048,2688]{1,0:T(8,128)(2,1)S(1)} %copy-done), custom_call_target="tpu_custom_call" | custom-call | flops 2818572288 | bytes 11010048 | tf_op jit(solution)/shard_map/pallas_call | solution.py:257
  19.0 2.0 %collective-permute-start = (bf16[256,1024]{1,0:T(8,128)(2,1)S(1)}, bf16[256,1024]{1,0:T(8,128)(2,1)S(1)}, u32[]{:S(2)}, u32[]{:S(2)}) collective-permute-start(bf16[256,1024]{1,0:T(8,128)(2,1)S(1)} %get-tuple-element.68.refs_5_), channel_id=1, source_target_pairs={{0,2},{2,0},{4,6},{6,4},{8,10},{10,8},{12,14},{14,12},{16,18},{18,... | collective-permute-start | bytes 1572872 | tf_op jit(solution)/shard_map/ppermute | solution.py:27
  21.0 1.5 collective-permute-start.1
  23.3 4.0 %collective-permute-start.7 = (bf16[4,256,256]{2,1,0:T(8,128)(2,1)S(1)}, bf16[4,256,256]{2,1,0:T(8,128)(2,1)S(1)}, u32[]{:S(2)}, u32[]{:S(2)}) collective-permute-start(bf16[4,256,256]{2,1,0:T(8,128)(2,1)S(1)} %get-tuple-element.76.refs_8_.refs_9_), channel_id=1, source_target_pairs={{0,8},{2,10},{4,12},{6,14},{8,16},{10,18},{12,20},{14,22},{16,24},... | collective-permute-start | bytes 1572872 | tf_op jit(solution)/shard_map/ppermute | solution.py:23
  27.3 3.5 %collective-permute-start.6 = (bf16[4,256,256]{2,1,0:T(8,128)(2,1)S(1)}, bf16[4,256,256]{2,1,0:T(8,128)(2,1)S(1)}, u32[]{:S(2)}, u32[]{:S(2)}) collective-permute-start(bf16[4,256,256]{2,1,0:T(8,128)(2,1)S(1)} %get-tuple-element.75.refs_8_.refs_9_), channel_id=1, source_target_pairs={{0,8},{2,10},{4,12},{6,14},{8,16},{10,18},{12,20},{14,22},{16,24},... | collective-permute-start | bytes 1572872 | tf_op jit(solution)/shard_map/ppermute | solution.py:23
  30.8 3.2 %collective-permute-done.refs_1_.refs_5_ = bf16[256,1024]{1,0:T(8,128)(2,1)S(1)} collective-permute-done((bf16[256,1024]{1,0:T(8,128)(2,1)S(1)}, bf16[256,1024]{1,0:T(8,128)(2,1)S(1)}, u32[]{:S(2)}, u32[]{:S(2)}) %collective-permute-start) | collective-permute-done | bytes 524320 | tf_op jit(solution)/shard_map/ppermute | solution.py:27
  33.9 10.9 %collective-permute-done.1.refs_2_.refs_6_ = bf16[256,1024]{1,0:T(8,128)(2,1)S(1)} collective-permute-done((bf16[256,1024]{1,0:T(8,128)(2,1)S(1)}, bf16[256,1024]{1,0:T(8,128)(2,1)S(1)}, u32[]{:S(2)}, u32[]{:S(2)}) %collective-permute-start.1) | collective-permute-done | bytes 524320 | tf_op jit(solution)/shard_map/ppermute | solution.py:27
  45.4 1.6 collective-permute-start.13
  49.0 12.8 %shard_map.105 = (bf16[256,256]{1,0:T(8,128)(2,1)S(1)}, bf16[256,256]{1,0:T(8,128)(2,1)S(1)}, bf16[256,256]{1,0:T(8,128)(2,1)S(1)}, bf16[256,256]{1,0:T(8,128)(2...) custom-call(s32[11]{0:T(128)S(1)} %pad_add_fusion.info_ref.info, ...), custom_call_target="tpu_custom_call" | custom-call | flops 4026531840 | bytes 5242880 | tf_op jit(solution)/shard_map/pallas_call | solution.py:150
  61.8 1.5 collective-permute-start.14
  63.3 13.0 %shard_map.106 = (bf16[256,512]{1,0:T(8,128)(2,1)S(1)}, bf16[256,512]{1,0:T(8,128)(2,1)S(1)}, bf16[256,512]{1,0:T(8,128)(2,1)S(1)}, bf16[256,512]{1,0:T(8,128)(2...) custom-call(s32[11]{0:T(128)S(1)} %pad_add_fusion.info_ref.info, ...), custom_call_target="tpu_custom_call" | custom-call | flops 4026531840 | bytes 5242880 | tf_op jit(solution)/shard_map/pallas_call | solution.py:150
  77.1 1.8 %collective-permute-start.16 = (bf16[2,4,256,128]{3,2,1,0:T(8,128)(2,1)S(1)}, bf16[2,4,256,128]{3,2,1,0:T(8,128)(2,1)S(1)}, u32[]{:S(2)}, u32[]{:S(2)}) collective-permute-start(bf16[2,4,256,128]{3,2,1,0:T(8,128)(2,1)S(1)} %get-tuple-element.92), channel_id=1, source_target_pairs={{8,0},{10,2},{12,4},{14,6},{16,8},{18,10},{20,12},{22,14},{24,16},... | collective-permute-start | bytes 1572872 | tf_op jit(solution)/shard_map/ppermute | solution.py:23
  78.9 2.3 %collective-permute-done.15.refs_2_ = bf16[384,2688]{1,0:T(8,128)(2,1)S(1)} collective-permute-done((bf16[384,2688]{1,0:T(8,128)(2,1)S(1)}, bf16[384,2688]{1,0:T(8,128)(2,1)S(1)}, u32[]{:S(2)}, u32[]{:S(2)}) %collective-permute-start.15) | collective-permute-done | bytes 2064416 | tf_op jit(solution)/shard_map/ppermute | solution.py:27
  81.2 4.5 %shard_map.109 = (bf16[672,256]{1,0:T(8,128)(2,1)S(1)}, bf16[672,256]{1,0:T(8,128)(2,1)S(1)}, bf16[2,672,256]{2,1,0:T(8,128)(2,1)S(1)}) custom-call(s32[11]{0:T(128)S(1)} %pad_add_fusion.info_ref.info, bf16[256,2688]{1,0:T(8,128)(2,1)S(1)} %copy-done.2, bf16[384,2688]{1,0:T(8,128)(2,1)S(1)} %shard_map.108.refs_1_, ...), custom_call_target="tpu_custom_call" | custom-call | flops 1409286144 | bytes 6881280 | tf_op jit(solution)/shard_map/pallas_call | solution.py:308
  85.7 2.7 %collective-permute-start.21 = (bf16[2,672,256]{2,1,0:T(8,128)(2,1)S(1)}, bf16[2,672,256]{2,1,0:T(8,128)(2,1)S(1)}, u32[]{:S(2)}, u32[]{:S(2)}) collective-permute-start(bf16[2,672,256]{2,1,0:T(8,128)(2,1)S(1)} %get-tuple-element.104), channel_id=1, source_target_pairs={{0,8},{2,10},{4,12},{6,14},{8,0},{10,2},{12,4},{14,6},{16,24},{18,... | collective-permute-start | bytes 2064392 | tf_op jit(solution)/shard_map/ppermute | solution.py:27
  91.9 2.8 %collective-permute-done.16.refs_4_.refs_3_ = bf16[2,4,256,128]{3,2,1,0:T(8,128)(2,1)S(1)} collective-permute-done((bf16[2,4,256,128]{3,2,1,0:T(8,128)(2,1)S(1)}, bf16[2,4,256,128]{3,2,1,0:T(8,128)(2,1)S(1)}, u32[]{:S(2)}, u32[]{:S(2)}) %collective-permute-start.16) | collective-permute-done | bytes 524320 | tf_op jit(solution)/shard_map/ppermute | solution.py:23
  94.7 4.5 %shard_map.110 = (bf16[672,256]{1,0:T(8,128)(2,1)S(1)}, bf16[672,256]{1,0:T(8,128)(2,1)S(1)}, bf16[2,672,256]{2,1,0:T(8,128)(2,1)S(1)}) custom-call(s32[11]{0:T(128)S(1)} %pad_add_fusion.info_ref.info, bf16[256,2688]{1,0:T(8,128)(2,1)S(1)} %copy-done.2, bf16[384,2688]{1,0:T(8,128)(2,1)S(1)} %shard_map.108.refs_1_, ...), custom_call_target="tpu_custom_call" | custom-call | flops 1409286144 | bytes 6881280 | tf_op jit(solution)/shard_map/pallas_call | solution.py:308
  99.2 3.0 %collective-permute-start.26 = (bf16[2,672,256]{2,1,0:T(8,128)(2,1)S(1)}, bf16[2,672,256]{2,1,0:T(8,128)(2,1)S(1)}, u32[]{:S(2)}, u32[]{:S(2)}) collective-permute-start(bf16[2,672,256]{2,1,0:T(8,128)(2,1)S(1)} %get-tuple-element.114), channel_id=1, source_target_pairs={{0,16},{2,18},{4,20},{6,22},{8,24},{10,26},{12,28},{14,30},{16,0},... | collective-permute-start | bytes 2064392 | tf_op jit(solution)/shard_map/ppermute | solution.py:27
  106.4 7.5 %shard_map.112 = (f32[1344,256]{1,0:T(8,128)S(1)}, bf16[1344,256]{1,0:T(8,128)(2,1)S(1)}) custom-call(s32[11]{0:T(128)S(1)} %pad_add_fusion.info_ref.info, bf16[256,2048]{1,0:T(8,128)(2,1)S(1)} %shard_map.111.attn_ref, bf16[2048,2688]{1,0:T(8,128)(2,1)S(1)} %bitcast.6), custom_call_target="tpu_custom_call" | custom-call | flops 2818572288 | bytes 11010048 | tf_op jit(solution)/shard_map/pallas_call | solution.py:373
  113.9 4.3 %collective-permute-done.21.refs_2_ = bf16[2,672,256]{2,1,0:T(8,128)(2,1)S(1)} collective-permute-done((bf16[2,672,256]{2,1,0:T(8,128)(2,1)S(1)}, bf16[2,672,256]{2,1,0:T(8,128)(2,1)S(1)}, u32[]{:S(2)}, u32[]{:S(2)}) %collective-permute-start.21) | collective-permute-done | bytes 688160 | tf_op jit(solution)/shard_map/ppermute | solution.py:27
  121.0 10.9 %collective-permute-done.26.refs_2_ = bf16[2,672,256]{2,1,0:T(8,128)(2,1)S(1)} collective-permute-done((bf16[2,672,256]{2,1,0:T(8,128)(2,1)S(1)}, bf16[2,672,256]{2,1,0:T(8,128)(2,1)S(1)}, u32[]{:S(2)}, u32[]{:S(2)}) %collective-permute-start.26) | collective-permute-done | bytes 688160 | tf_op jit(solution)/shard_map/ppermute | solution.py:27
  132.7 2.1 %collective-permute-start.25 = (bf16[672,256]{1,0:T(8,128)(2,1)S(1)}, bf16[672,256]{1,0:T(8,128)(2,1)S(1)}, u32[]{:S(2)}, u32[]{:S(2)}) collective-permute-start(bf16[672,256]{1,0:T(8,128)(2,1)S(1)} %get-tuple-element.105.refs_7_.refs_3_), channel_id=1, source_target_pairs={{0,16},{2,18},{4,20},{6,22},{8,24},{10,26},{12,28},{14,30},{16,0},... | collective-permute-start | bytes 1032200 | tf_op jit(solution)/shard_map/ppermute | solution.py:27
  134.8 1.5 collective-permute-start.23
  137.5 9.0 %collective-permute-done.23.refs_2_.refs_5_ = bf16[256,512]{1,0:T(8,128)(2,1)S(1)} collective-permute-done((bf16[256,512]{1,0:T(8,128)(2,1)S(1)}, bf16[256,512]{1,0:T(8,128)(2,1)S(1)}, u32[]{:S(2)}, u32[]{:S(2)}) %collective-permute-start.23) | collective-permute-done | bytes 262176 | tf_op jit(solution)/shard_map/ppermute | solution.py:27
  147.3 2.5 %collective-permute-done.25.refs_1_ = bf16[672,256]{1,0:T(8,128)(2,1)S(1)} collective-permute-done((bf16[672,256]{1,0:T(8,128)(2,1)S(1)}, bf16[672,256]{1,0:T(8,128)(2,1)S(1)}, u32[]{:S(2)}, u32[]{:S(2)}) %collective-permute-start.25) | collective-permute-done | bytes 344096 | tf_op jit(solution)/shard_map/ppermute | solution.py:27
  154.1 1.6 shard_map.116
  155.7 1.5 shard_map.113
  157.2 1.6 %shard_map.117 = (bf16[256,1024]{1,0:T(8,128)(2,1)}, bf16[256,1024]{1,0:T(8,128)(2,1)}) custom-call(s32[11]{0:T(128)S(1)} %pad_add_fusion.info_ref.info, bf16[256,512]{1,0:T(8,128)(2,1)S(1)} %get-tuple-element.106.refs_4_.refs_0_, bf16[256,512]{1,0:T(8,128)(2,1)S(1)} %collective-permute-done.22.refs_1_.refs_4_, ...), custom_call_target="tpu_custom_call" | custom-call | bytes 2097152 | tf_op jit(solution)/shard_map/pallas_call | solution.py:187
  159.1 1.7 %shard_map.120 = f32[168,2048]{1,0:T(8,128)} custom-call(s32[11]{0:T(128)S(1)} %pad_add_fusion.info_ref.info, bf16[168,512]{1,0:T(8,128)(2,1)S(1)} %get-tuple-element.117.refs_0_, bf16[168,512]{1,0:T(8,128)(2,1)S(1)} %collective-permute-done.28.refs_1_, bf16[168,512]{1,0:T(8,128)(2,1)S(1)} %collective-permute-done.29.refs_2_, ...), custom_call_target="tpu_custom_call" | custom-call | bytes 2064384 | tf_op jit(solution)/shard_map/pallas_call | solution.py:187
  (71 shorter events, 27.1 us)
Async XLA Ops:
  3.0 19.6 %collective-permute-start.3 = (bf16[256,512]{1,0:T(8,128)(2,1)S(1)}, bf16[256,512]{1,0:T(8,128)(2,1)S(1)}, u32[]{:S(2)}, u32[]{:S(2)}) collective-permute-start(bf16[256,512]{1,0:T(8,128)(2,1)S(1)} %get-tuple-element.72), channel_id=1, source_target_pairs={{0,2},{2,0},{4,6},{6,4},{8,10},{10,8},{12,14},{14,12},{16,18},{18,... | collective-permute-start | bytes 786440 | tf_op jit(solution)/shard_map/ppermute | solution.py:27
  6.0 16.6 %collective-permute-start.4 = (bf16[256,512]{1,0:T(8,128)(2,1)S(1)}, bf16[256,512]{1,0:T(8,128)(2,1)S(1)}, u32[]{:S(2)}, u32[]{:S(2)}) collective-permute-start(bf16[256,512]{1,0:T(8,128)(2,1)S(1)} %get-tuple-element.73), channel_id=1, source_target_pairs={{0,4},{2,6},{4,0},{6,2},{8,12},{10,14},{12,8},{14,10},{16,20},{18,... | collective-permute-start | bytes 786440 | tf_op jit(solution)/shard_map/ppermute | solution.py:27
  7.5 15.1 %collective-permute-start.5 = (bf16[256,512]{1,0:T(8,128)(2,1)S(1)}, bf16[256,512]{1,0:T(8,128)(2,1)S(1)}, u32[]{:S(2)}, u32[]{:S(2)}) collective-permute-start(bf16[256,512]{1,0:T(8,128)(2,1)S(1)} %get-tuple-element.74), channel_id=1, source_target_pairs={{0,6},{2,4},{4,2},{6,0},{8,14},{10,12},{12,10},{14,8},{16,22},{18,... | collective-permute-start | bytes 786440 | tf_op jit(solution)/shard_map/ppermute | solution.py:27
  19.0 14.9 %collective-permute-start = (bf16[256,1024]{1,0:T(8,128)(2,1)S(1)}, bf16[256,1024]{1,0:T(8,128)(2,1)S(1)}, u32[]{:S(2)}, u32[]{:S(2)}) collective-permute-start(bf16[256,1024]{1,0:T(8,128)(2,1)S(1)} %get-tuple-element.68.refs_5_), channel_id=1, source_target_pairs={{0,2},{2,0},{4,6},{6,4},{8,10},{10,8},{12,14},{14,12},{16,18},{18,... | collective-permute-start | bytes 1572872 | tf_op jit(solution)/shard_map/ppermute | solution.py:27
  21.0 23.8 %collective-permute-start.1 = (bf16[256,1024]{1,0:T(8,128)(2,1)S(1)}, bf16[256,1024]{1,0:T(8,128)(2,1)S(1)}, u32[]{:S(2)}, u32[]{:S(2)}) collective-permute-start(bf16[256,1024]{1,0:T(8,128)(2,1)S(1)} %get-tuple-element.69.refs_6_), channel_id=1, source_target_pairs={{0,4},{2,6},{4,0},{6,2},{8,12},{10,14},{12,8},{14,10},{16,20},{18,... | collective-permute-start | bytes 1572872 | tf_op jit(solution)/shard_map/ppermute | solution.py:27
  22.5 22.3 %collective-permute-start.2 = (bf16[256,1024]{1,0:T(8,128)(2,1)S(1)}, bf16[256,1024]{1,0:T(8,128)(2,1)S(1)}, u32[]{:S(2)}, u32[]{:S(2)}) collective-permute-start(bf16[256,1024]{1,0:T(8,128)(2,1)S(1)} %get-tuple-element.70.refs_7_), channel_id=1, source_target_pairs={{0,6},{2,4},{4,2},{6,0},{8,14},{10,12},{12,10},{14,8},{16,22},{18,... | collective-permute-start | bytes 1572872 | tf_op jit(solution)/shard_map/ppermute | solution.py:27
  23.3 25.7 %collective-permute-start.7 = (bf16[4,256,256]{2,1,0:T(8,128)(2,1)S(1)}, bf16[4,256,256]{2,1,0:T(8,128)(2,1)S(1)}, u32[]{:S(2)}, u32[]{:S(2)}) collective-permute-start(bf16[4,256,256]{2,1,0:T(8,128)(2,1)S(1)} %get-tuple-element.76.refs_8_.refs_9_), channel_id=1, source_target_pairs={{0,8},{2,10},{4,12},{6,14},{8,16},{10,18},{12,20},{14,22},{16,24},... | collective-permute-start | bytes 1572872 | tf_op jit(solution)/shard_map/ppermute | solution.py:23
  27.3 36.0 %collective-permute-start.6 = (bf16[4,256,256]{2,1,0:T(8,128)(2,1)S(1)}, bf16[4,256,256]{2,1,0:T(8,128)(2,1)S(1)}, u32[]{:S(2)}, u32[]{:S(2)}) collective-permute-start(bf16[4,256,256]{2,1,0:T(8,128)(2,1)S(1)} %get-tuple-element.75.refs_8_.refs_9_), channel_id=1, source_target_pairs={{0,8},{2,10},{4,12},{6,14},{8,16},{10,18},{12,20},{14,22},{16,24},... | collective-permute-start | bytes 1572872 | tf_op jit(solution)/shard_map/ppermute | solution.py:23
  45.4 30.8 %collective-permute-start.13 = (bf16[128,2688]{1,0:T(8,128)(2,1)S(1)}, bf16[128,2688]{1,0:T(8,128)(2,1)S(1)}, u32[]{:S(2)}, u32[]{:S(2)}) collective-permute-start(bf16[128,2688]{1,0:T(8,128)(2,1)S(1)} %shard_map.107), channel_id=1, source_target_pairs={{0,6},{2,4},{4,2},{6,0},{8,14},{10,12},{12,10},{14,8},{16,22},{18,... | collective-permute-start | bytes 2064392 | tf_op jit(solution)/shard_map/ppermute | solution.py:27
  47.0 29.3 %collective-permute-start.12 = (bf16[128,2688]{1,0:T(8,128)(2,1)S(1)}, bf16[128,2688]{1,0:T(8,128)(2,1)S(1)}, u32[]{:S(2)}, u32[]{:S(2)}) collective-permute-start(bf16[128,2688]{1,0:T(8,128)(2,1)S(1)} %shard_map.107), channel_id=1, source_target_pairs={{0,4},{2,6},{4,0},{6,2},{8,12},{10,14},{12,8},{14,10},{16,20},{18,... | collective-permute-start | bytes 2064392 | tf_op jit(solution)/shard_map/ppermute | solution.py:27
  48.2 28.2 %collective-permute-start.11 = (bf16[128,2688]{1,0:T(8,128)(2,1)S(1)}, bf16[128,2688]{1,0:T(8,128)(2,1)S(1)}, u32[]{:S(2)}, u32[]{:S(2)}) collective-permute-start(bf16[128,2688]{1,0:T(8,128)(2,1)S(1)} %shard_map.107), channel_id=1, source_target_pairs={{0,2},{2,0},{4,6},{6,4},{8,10},{10,8},{12,14},{14,12},{16,18},{18,... | collective-permute-start | bytes 2064392 | tf_op jit(solution)/shard_map/ppermute | solution.py:27
  61.8 14.5 %collective-permute-start.14 = (bf16[2,4,256,128]{3,2,1,0:T(8,128)(2,1)S(1)}, bf16[2,4,256,128]{3,2,1,0:T(8,128)(2,1)S(1)}, u32[]{:S(2)}, u32[]{:S(2)}) collective-permute-start(bf16[2,4,256,128]{3,2,1,0:T(8,128)(2,1)S(1)} %get-tuple-element.91), channel_id=1, source_target_pairs={{8,0},{10,2},{12,4},{14,6},{16,8},{18,10},{20,12},{22,14},{24,16},... | collective-permute-start | bytes 1572872 | tf_op jit(solution)/shard_map/ppermute | solution.py:23
  76.3 30.0 %slice-start = ((s8[11010048]{0:T(1024)(128)(4,1)}), s8[4194304]{0:T(1024)(128)(4,1)S(1)}, s32[]{:S(2)}) async-start(s8[11010048]{0:T(1024)(128)(4,1)} %bitcast.5), calls=%async_computation | async-start | bytes 8388608
  77.0 4.2 %collective-permute-start.15 = (bf16[384,2688]{1,0:T(8,128)(2,1)S(1)}, bf16[384,2688]{1,0:T(8,128)(2,1)S(1)}, u32[]{:S(2)}, u32[]{:S(2)}) collective-permute-start(bf16[384,2688]{1,0:T(8,128)(2,1)S(1)} %shard_map.108.refs_1_), channel_id=1, source_target_pairs={{0,1},{1,0},{2,3},{3,2},{4,5},{5,4},{6,7},{7,6},{8,9},{9,8},{10,11... | collective-permute-start | bytes 6193160 | tf_op jit(solution)/shard_map/ppermute | solution.py:27
  77.1 17.6 %collective-permute-start.16 = (bf16[2,4,256,128]{3,2,1,0:T(8,128)(2,1)S(1)}, bf16[2,4,256,128]{3,2,1,0:T(8,128)(2,1)S(1)}, u32[]{:S(2)}, u32[]{:S(2)}) collective-permute-start(bf16[2,4,256,128]{3,2,1,0:T(8,128)(2,1)S(1)} %get-tuple-element.92), channel_id=1, source_target_pairs={{8,0},{10,2},{12,4},{14,6},{16,8},{18,10},{20,12},{22,14},{24,16},... | collective-permute-start | bytes 1572872 | tf_op jit(solution)/shard_map/ppermute | solution.py:23
  85.7 32.5 %collective-permute-start.21 = (bf16[2,672,256]{2,1,0:T(8,128)(2,1)S(1)}, bf16[2,672,256]{2,1,0:T(8,128)(2,1)S(1)}, u32[]{:S(2)}, u32[]{:S(2)}) collective-permute-start(bf16[2,672,256]{2,1,0:T(8,128)(2,1)S(1)} %get-tuple-element.104), channel_id=1, source_target_pairs={{0,8},{2,10},{4,12},{6,14},{8,0},{10,2},{12,4},{14,6},{16,24},{18,... | collective-permute-start | bytes 2064392 | tf_op jit(solution)/shard_map/ppermute | solution.py:27
  88.4 13.8 %collective-permute-start.8 = (bf16[256,512]{1,0:T(8,128)(2,1)S(1)}, bf16[256,512]{1,0:T(8,128)(2,1)S(1)}, u32[]{:S(2)}, u32[]{:S(2)}) collective-permute-start(bf16[256,512]{1,0:T(8,128)(2,1)S(1)} %get-tuple-element.86), channel_id=1, source_target_pairs={{0,2},{2,0},{4,6},{6,4},{8,10},{10,8},{12,14},{14,12},{16,18},{18,... | collective-permute-start | bytes 786440 | tf_op jit(solution)/shard_map/ppermute | solution.py:27
  89.6 13.8 %collective-permute-start.9 = (bf16[256,512]{1,0:T(8,128)(2,1)S(1)}, bf16[256,512]{1,0:T(8,128)(2,1)S(1)}, u32[]{:S(2)}, u32[]{:S(2)}) collective-permute-start(bf16[256,512]{1,0:T(8,128)(2,1)S(1)} %get-tuple-element.87), channel_id=1, source_target_pairs={{0,4},{2,6},{4,0},{6,2},{8,12},{10,14},{12,8},{14,10},{16,20},{18,... | collective-permute-start | bytes 786440 | tf_op jit(solution)/shard_map/ppermute | solution.py:27
  90.5 13.8 %collective-permute-start.10 = (bf16[256,512]{1,0:T(8,128)(2,1)S(1)}, bf16[256,512]{1,0:T(8,128)(2,1)S(1)}, u32[]{:S(2)}, u32[]{:S(2)}) collective-permute-start(bf16[256,512]{1,0:T(8,128)(2,1)S(1)} %get-tuple-element.88), channel_id=1, source_target_pairs={{0,6},{2,4},{4,2},{6,0},{8,14},{10,12},{12,10},{14,8},{16,22},{18,... | collective-permute-start | bytes 786440 | tf_op jit(solution)/shard_map/ppermute | solution.py:27
  99.2 32.7 %collective-permute-start.26 = (bf16[2,672,256]{2,1,0:T(8,128)(2,1)S(1)}, bf16[2,672,256]{2,1,0:T(8,128)(2,1)S(1)}, u32[]{:S(2)}, u32[]{:S(2)}) collective-permute-start(bf16[2,672,256]{2,1,0:T(8,128)(2,1)S(1)} %get-tuple-element.114), channel_id=1, source_target_pairs={{0,16},{2,18},{4,20},{6,22},{8,24},{10,26},{12,28},{14,30},{16,0},... | collective-permute-start | bytes 2064392 | tf_op jit(solution)/shard_map/ppermute | solution.py:27
  102.2 16.7 %collective-permute-start.18 = (bf16[256,512]{1,0:T(8,128)(2,1)S(1)}, bf16[256,512]{1,0:T(8,128)(2,1)S(1)}, u32[]{:S(2)}, u32[]{:S(2)}) collective-permute-start(bf16[256,512]{1,0:T(8,128)(2,1)S(1)} %get-tuple-element.98), channel_id=1, source_target_pairs={{0,2},{2,0},{4,6},{6,4},{8,10},{10,8},{12,14},{14,12},{16,18},{18,... | collective-permute-start | bytes 786440 | tf_op jit(solution)/shard_map/ppermute | solution.py:27
  103.4 15.5 %collective-permute-start.19 = (bf16[256,512]{1,0:T(8,128)(2,1)S(1)}, bf16[256,512]{1,0:T(8,128)(2,1)S(1)}, u32[]{:S(2)}, u32[]{:S(2)}) collective-permute-start(bf16[256,512]{1,0:T(8,128)(2,1)S(1)} %get-tuple-element.99), channel_id=1, source_target_pairs={{0,4},{2,6},{4,0},{6,2},{8,12},{10,14},{12,8},{14,10},{16,20},{18,... | collective-permute-start | bytes 786440 | tf_op jit(solution)/shard_map/ppermute | solution.py:27
  104.3 14.7 %collective-permute-start.20 = (bf16[256,512]{1,0:T(8,128)(2,1)S(1)}, bf16[256,512]{1,0:T(8,128)(2,1)S(1)}, u32[]{:S(2)}, u32[]{:S(2)}) collective-permute-start(bf16[256,512]{1,0:T(8,128)(2,1)S(1)} %get-tuple-element.100), channel_id=1, source_target_pairs={{0,6},{2,4},{4,2},{6,0},{8,14},{10,12},{12,10},{14,8},{16,22},{18,... | collective-permute-start | bytes 786440 | tf_op jit(solution)/shard_map/ppermute | solution.py:27
  119.7 16.6 %collective-permute-start.22 = (bf16[256,512]{1,0:T(8,128)(2,1)S(1)}, bf16[256,512]{1,0:T(8,128)(2,1)S(1)}, u32[]{:S(2)}, u32[]{:S(2)}) collective-permute-start(bf16[256,512]{1,0:T(8,128)(2,1)S(1)} %get-tuple-element.107.refs_5_), channel_id=1, source_target_pairs={{0,2},{2,0},{4,6},{6,4},{8,10},{10,8},{12,14},{14,12},{16,18},{18,... | collective-permute-start | bytes 786440 | tf_op jit(solution)/shard_map/ppermute | solution.py:27
  121.0 34.6 %collective-permute-start.17 = (bf16[1344,256]{1,0:T(8,128)(2,1)S(1)}, bf16[1344,256]{1,0:T(8,128)(2,1)S(1)}, u32[]{:S(2)}, u32[]{:S(2)}) collective-permute-start(bf16[1344,256]{1,0:T(8,128)(2,1)S(1)} %get-tuple-element.96.refs_3_), channel_id=1, source_target_pairs={{0,1},{1,0},{2,3},{3,2},{4,5},{5,4},{6,7},{7,6},{8,9},{9,8},{10,11... | collective-permute-start | bytes 2064392 | tf_op jit(solution)/shard_map/ppermute | solution.py:27
  132.6 14.7 %collective-permute-start.27 = (bf16[672,256]{1,0:T(8,128)(2,1)S(1)}, bf16[672,256]{1,0:T(8,128)(2,1)S(1)}, u32[]{:S(2)}, u32[]{:S(2)}) collective-permute-start(bf16[672,256]{1,0:T(8,128)(2,1)S(1)} %get-tuple-element.116), channel_id=1, source_target_pairs={{0,8},{2,10},{4,12},{6,14},{8,0},{10,2},{12,4},{14,6},{16,24},{18,... | collective-permute-start | bytes 1032200 | tf_op jit(solution)/shard_map/ppermute | solution.py:27
  132.7 17.1 %collective-permute-start.25 = (bf16[672,256]{1,0:T(8,128)(2,1)S(1)}, bf16[672,256]{1,0:T(8,128)(2,1)S(1)}, u32[]{:S(2)}, u32[]{:S(2)}) collective-permute-start(bf16[672,256]{1,0:T(8,128)(2,1)S(1)} %get-tuple-element.105.refs_7_.refs_3_), channel_id=1, source_target_pairs={{0,16},{2,18},{4,20},{6,22},{8,24},{10,26},{12,28},{14,30},{16,0},... | collective-permute-start | bytes 1032200 | tf_op jit(solution)/shard_map/ppermute | solution.py:27
  134.8 11.7 %collective-permute-start.23 = (bf16[256,512]{1,0:T(8,128)(2,1)S(1)}, bf16[256,512]{1,0:T(8,128)(2,1)S(1)}, u32[]{:S(2)}, u32[]{:S(2)}) collective-permute-start(bf16[256,512]{1,0:T(8,128)(2,1)S(1)} %get-tuple-element.108.refs_6_), channel_id=1, source_target_pairs={{0,4},{2,6},{4,0},{6,2},{8,12},{10,14},{12,8},{14,10},{16,20},{18,... | collective-permute-start | bytes 786440 | tf_op jit(solution)/shard_map/ppermute | solution.py:27
  136.3 10.1 %collective-permute-start.24 = (bf16[256,512]{1,0:T(8,128)(2,1)S(1)}, bf16[256,512]{1,0:T(8,128)(2,1)S(1)}, u32[]{:S(2)}, u32[]{:S(2)}) collective-permute-start(bf16[256,512]{1,0:T(8,128)(2,1)S(1)} %get-tuple-element.109.refs_7_), channel_id=1, source_target_pairs={{0,6},{2,4},{4,2},{6,0},{8,14},{10,12},{12,10},{14,8},{16,22},{18,... | collective-permute-start | bytes 786440 | tf_op jit(solution)/shard_map/ppermute | solution.py:27
  150.5 8.3 %collective-permute-start.28 = (bf16[168,512]{1,0:T(8,128)(2,1)S(1)}, bf16[168,512]{1,0:T(8,128)(2,1)S(1)}, u32[]{:S(2)}, u32[]{:S(2)}) collective-permute-start(bf16[168,512]{1,0:T(8,128)(2,1)S(1)} %get-tuple-element.118), channel_id=1, source_target_pairs={{0,2},{2,0},{4,6},{6,4},{8,10},{10,8},{12,14},{14,12},{16,18},{18,... | collective-permute-start | bytes 516104 | tf_op jit(solution)/shard_map/ppermute | solution.py:27
  151.8 7.2 %collective-permute-start.29 = (bf16[168,512]{1,0:T(8,128)(2,1)S(1)}, bf16[168,512]{1,0:T(8,128)(2,1)S(1)}, u32[]{:S(2)}, u32[]{:S(2)}) collective-permute-start(bf16[168,512]{1,0:T(8,128)(2,1)S(1)} %get-tuple-element.119), channel_id=1, source_target_pairs={{0,4},{2,6},{4,0},{6,2},{8,12},{10,14},{12,8},{14,10},{16,20},{18,... | collective-permute-start | bytes 516104 | tf_op jit(solution)/shard_map/ppermute | solution.py:27
  152.7 6.4 %collective-permute-start.30 = (bf16[168,512]{1,0:T(8,128)(2,1)S(1)}, bf16[168,512]{1,0:T(8,128)(2,1)S(1)}, u32[]{:S(2)}, u32[]{:S(2)}) collective-permute-start(bf16[168,512]{1,0:T(8,128)(2,1)S(1)} %get-tuple-element.120), channel_id=1, source_target_pairs={{0,6},{2,4},{4,2},{6,0},{8,14},{10,12},{12,10},{14,8},{16,22},{18,... | collective-permute-start | bytes 516104 | tf_op jit(solution)/shard_map/ppermute | solution.py:27
  (8 other events, 78.8 us)

commit v6 on v5

--- a/solution.py
+++ b/solution.py
@@ -272,15 +272,51 @@
         ),
     )(info, out_grad, out_weight)
 
-def weight_terms(info, pieces, attn_cat, near, after=()):
+def early_terms(pieces, attn_cat):
+    d_out, width = pieces[0].shape[1], attn_cat.shape[1]
+    block = 3 * HEAD if d_out % (3 * HEAD) == 0 else d_out
+
+    def kernel(*refs):
+        attn, out = refs[-2:]
+        total, at = None, 0
+        for piece in refs[:-2]:
+            rows = piece.shape[0]
+            term = lax.dot_general(
+                piece[...],
+                attn[at : at + rows],
+                (((0,), (0,)), ((), ())),
+                preferred_element_type=jnp.float32,
+            )
+            total, at = term if total is None else total + term, at + rows
+        out[...] = total
+
+    return pl.pallas_call(
+        kernel,
+        grid=(d_out // block,),
+        in_specs=[pl.BlockSpec((p.shape[0], block), lambda i: (0, i)) for p in pieces]
+        + [entire(attn_cat)],
+        out_specs=pl.BlockSpec((block, width), lambda i: (i, 0)),
+        out_shape=jax.ShapeDtypeStruct((d_out, width), jnp.float32),
+        compiler_params=pltpu.CompilerParams(vmem_limit_bytes=32 * 1024 * 1024),
+        cost_estimate=pl.CostEstimate(
+            flops=2 * sum(p.shape[0] for p in pieces) * width * d_out,
+            bytes_accessed=2 * (attn_cat.shape[0] + 2 * width) * d_out,
+            transcendentals=0,
+        ),
+    )(*pieces, attn_cat)
+
+
+def weight_terms(info, pieces, attn_cat, near, after=(), base=()):
     d_out, width = pieces[0].shape[1], attn_cat.shape[1]
     block = 3 * HEAD if d_out % (3 * HEAD) == 0 else d_out
     steps, cut = d_out // block, d_out // GROUP
 
     def kernel(info_ref, *refs):
         inputs, attn = refs[: len(pieces)], refs[len(pieces)]
-        own, other, away, whole = refs[len(pieces) + 1 + len(after) :]
-        total, at = None, 0
+        bases = refs[len(pieces) + 1 : len(pieces) + 1 + len(base)]
+        own, other, away, whole = refs[len(pieces) + 1 + len(base) + len(after) :]
+        at = attn.shape[0] - sum(piece.shape[0] for piece in inputs)
+        total = bases[0][...] if bases else None
         for piece in inputs:
             rows = piece.shape[0]
             term = lax.dot_general(
@@ -311,6 +347,7 @@
         in_specs=[SMEM]
         + [pl.BlockSpec((p.shape[0], block), lambda i: (0, i)) for p in pieces]
         + [entire(attn_cat)]
+        + [pl.BlockSpec((block, width), lambda i: (i, 0))] * len(base)
         + [ANY] * len(after),
         out_specs=[entire(a) for a in out],
         out_shape=out,
@@ -321,7 +358,7 @@
             bytes_accessed=2 * (attn_cat.shape[0] + width) * d_out,
             transcendentals=0,
         ),
-    )(info, *pieces, attn_cat, *after)
+    )(info, *pieces, attn_cat, *base, *after)
 
 
 def split_sums(info, pairs, after):
@@ -429,7 +466,8 @@
     def pack_half(info_ref, ins, outs):
         outs[0][...] = ins[0][pl.ds(pl.multiple_of(info_ref[1] * (rows // 2), 16), rows // 2), :]
 
-    half = moved(pack_half, info, [out_grad], [shape(rows // 2, d_out)], q_and_d[1:])[0]
+    half = moved(pack_half, info, [out_grad], [shape(rows // 2, d_out)])[0]
+    half, *_ = lax.optimization_barrier((half, *q_and_d[1:]))
     near = traded([half] * GROUP)[1:]
 
     def pack_near(info_ref, ins, outs):
@@ -447,8 +485,9 @@
     near_shape = shape((GROUP - 1) * (rows // 2), d_out)
     near = moved(pack_near, info, near, [near_shape], [*attn_cats, far_grads[0]])[0]
     pieces = [out_grad, near, swapped(near, "tp", 1)]
-    steps = [1, 2]
-    all_terms = [weight_terms(info, pieces, attn_cats[0], steps[0])]
+    steps = [2, 1]
+    early = early_terms(pieces[:2], attn_cats[0])
+    all_terms = [weight_terms(info, pieces[2:], attn_cats[0], steps[0], (), [early])]
     for g in range(1, kv_heads):
         all_terms.append(weight_terms(info, pieces, attn_cats[g], steps[g], [far_grads[g], all_terms[0][0]]))
 

time: 161 us -> 160 us (level)
  waiting for transfers between devices: 47 us -> 40 us
  starting transfers between devices: 44.8 us -> 49.5 us
    ppermute x27, waiting for transfers between devices: 44.2 us -> 38.8 us  [swapped(): lax.ppermute(shard, axis, [(i, i ^ by) for i in range(lax.axis_size(axis))])]
    ppermute x27, starting transfers between devices: 34.1 us -> 38.8 us  [swapped(): lax.ppermute(shard, axis, [(i, i ^ by) for i in range(lax.axis_size(axis))])]
    pallas_call x0 -> x1, Pallas kernels: none -> 2.94 us  [early_terms(): pl.pallas_call(kernel, grid=(d_out // block,), in_specs=[pl.BlockSpec((p....]
  transfers between devices with their start and end apart: 31 -> 31, of which waited for: 11 -> 10; matrix products, arithmetic and copies ran while one was open for 1% -> 1% of each run, Pallas kernels for 36% -> 37%
where the time goes in v6:
time: 160 us
  Pallas kernels  61.3 us (38%)
  starting transfers between devices  49.5 us (31%)
  waiting for transfers between devices  40 us (25%)
  local copies, waits for them, and re-layouts  8.3 us (5%)
    ppermute x27, starting transfers between devices, swapped(): lax.ppermute(shard, axis, [(i, i ^ by) for i in range(lax.axis_size(axis))])  38.8 us
    ppermute x27, waiting for transfers between devices, swapped(): lax.ppermute(shard, axis, [(i, i ^ by) for i in range(lax.axis_size(axis))])  38.8 us
    pallas_call x2, Pallas kernels, attention(): pl.pallas_call(functools.partial(attention_kernel, rows, len(held)), grid...  25.8 us
    pallas_call x12, Pallas kernels, moved(): pl.pallas_call(kernel, grid=(1,), in_specs=[SMEM] + [entire(a) for a in a...  11.9 us
    ppermute x4, starting transfers between devices, shifted(): return lax.ppermute(shard, axis, pairs)  10.7 us
    pallas_call x2, Pallas kernels, weight_terms(): pl.pallas_call(kernel, grid=(steps,), in_specs=[SMEM] + [pl.BlockSpec((p....  7.64 us
    unnamed x18, local copies, waits for them, and re-layouts  7.57 us
    pallas_call x1, Pallas kernels, project(): pl.pallas_call(kernel, grid=(steps,), in_specs=[SMEM, entire(attn), pl.Bl...  7.54 us
  transfers between devices with their start and end apart: 31, of which 10 were waited for; matrix products, arithmetic and copies ran while one was open for 1% of the time, Pallas kernels for 37%

profile of v6, /device:TPU:0, one launch (start us, length us, event | category | flops | bytes accessed | tf_op | source)
XLA Modules:
  0.0 160.1 jit_solution(7898971645655792594)
XLA Ops:
  3.0 3.0 %collective-permute-start.3 = (bf16[256,512]{1,0:T(8,128)(2,1)S(1)}, bf16[256,512]{1,0:T(8,128)(2,1)S(1)}, u32[]{:S(2)}, u32[]{:S(2)}) collective-permute-start(bf16[256,512]{1,0:T(8,128)(2,1)S(1)} %get-tuple-element.73), channel_id=1, source_target_pairs={{0,2},{2,0},{4,6},{6,4},{8,10},{10,8},{12,14},{14,12},{16,18},{18,... | collective-permute-start | bytes 786440 | tf_op jit(solution)/shard_map/ppermute | solution.py:27
  6.0 1.5 collective-permute-start.4
  8.3 4.1 %copy-done = bf16[2048,2688]{1,0:T(8,128)(2,1)S(1)} copy-done((bf16[2048,2688]{1,0:T(8,128)(2,1)S(1)}, bf16[2048,2688]{1,0:T(8,128)(2,1)}, u32[]{:S(2)}) %copy-start) | copy-done | bytes 11010072
  13.8 4.5 %shard_map.101 = (bf16[256,512]{1,0:T(8,128)(2,1)S(1)}, bf16[256,512]{1,0:T(8,128)(2,1)S(1)}, bf16[256,512]{1,0:T(8,128)(2,1)S(1)}, bf16[256,512]{1,0:T(8,128)(2,1)S(1)}) custom-call(s32[11]{0:T(128)S(1)} %pad_add_fusion.info_ref.info, bf16[256,2688]{1,0:T(8,128)(2,1)S(1)} %copy-done.1, bf16[2048,2688]{1,0:T(8,128)(2,1)S(1)} %copy-done), custom_call_target="tpu_custom_call" | custom-call | flops 2818572288 | bytes 11010048 | tf_op jit(solution)/shard_map/pallas_call | solution.py:257
  19.0 2.0 %collective-permute-start = (bf16[256,1024]{1,0:T(8,128)(2,1)S(1)}, bf16[256,1024]{1,0:T(8,128)(2,1)S(1)}, u32[]{:S(2)}, u32[]{:S(2)}) collective-permute-start(bf16[256,1024]{1,0:T(8,128)(2,1)S(1)} %get-tuple-element.69.refs_5_), channel_id=1, source_target_pairs={{0,2},{2,0},{4,6},{6,4},{8,10},{10,8},{12,14},{14,12},{16,18},{18,... | collective-permute-start | bytes 1572872 | tf_op jit(solution)/shard_map/ppermute | solution.py:27
  21.0 1.5 collective-permute-start.1
  23.3 4.0 %collective-permute-start.7 = (bf16[4,256,256]{2,1,0:T(8,128)(2,1)S(1)}, bf16[4,256,256]{2,1,0:T(8,128)(2,1)S(1)}, u32[]{:S(2)}, u32[]{:S(2)}) collective-permute-start(bf16[4,256,256]{2,1,0:T(8,128)(2,1)S(1)} %get-tuple-element.77.refs_8_.refs_9_), channel_id=1, source_target_pairs={{0,8},{2,10},{4,12},{6,14},{8,16},{10,18},{12,20},{14,22},{16,24},... | collective-permute-start | bytes 1572872 | tf_op jit(solution)/shard_map/ppermute | solution.py:23
  27.9 3.5 %collective-permute-start.6 = (bf16[4,256,256]{2,1,0:T(8,128)(2,1)S(1)}, bf16[4,256,256]{2,1,0:T(8,128)(2,1)S(1)}, u32[]{:S(2)}, u32[]{:S(2)}) collective-permute-start(bf16[4,256,256]{2,1,0:T(8,128)(2,1)S(1)} %get-tuple-element.76.refs_8_.refs_9_), channel_id=1, source_target_pairs={{0,8},{2,10},{4,12},{6,14},{8,16},{10,18},{12,20},{14,22},{16,24},... | collective-permute-start | bytes 1572872 | tf_op jit(solution)/shard_map/ppermute | solution.py:23
  31.4 2.6 %collective-permute-done.refs_1_.refs_5_ = bf16[256,1024]{1,0:T(8,128)(2,1)S(1)} collective-permute-done((bf16[256,1024]{1,0:T(8,128)(2,1)S(1)}, bf16[256,1024]{1,0:T(8,128)(2,1)S(1)}, u32[]{:S(2)}, u32[]{:S(2)}) %collective-permute-start) | collective-permute-done | bytes 524320 | tf_op jit(solution)/shard_map/ppermute | solution.py:27
  33.9 10.9 %collective-permute-done.1.refs_2_.refs_6_ = bf16[256,1024]{1,0:T(8,128)(2,1)S(1)} collective-permute-done((bf16[256,1024]{1,0:T(8,128)(2,1)S(1)}, bf16[256,1024]{1,0:T(8,128)(2,1)S(1)}, u32[]{:S(2)}, u32[]{:S(2)}) %collective-permute-start.1) | collective-permute-done | bytes 524320 | tf_op jit(solution)/shard_map/ppermute | solution.py:27
  44.8 1.5 collective-permute-start.13
  48.3 12.8 %shard_map.105 = (bf16[256,256]{1,0:T(8,128)(2,1)S(1)}, bf16[256,256]{1,0:T(8,128)(2,1)S(1)}, bf16[256,256]{1,0:T(8,128)(2,1)S(1)}, bf16[256,256]{1,0:T(8,128)(2...) custom-call(s32[11]{0:T(128)S(1)} %pad_add_fusion.info_ref.info, ...), custom_call_target="tpu_custom_call" | custom-call | flops 4026531840 | bytes 5242880 | tf_op jit(solution)/shard_map/pallas_call | solution.py:150
  62.6 12.9 %shard_map.106 = (bf16[256,512]{1,0:T(8,128)(2,1)S(1)}, bf16[256,512]{1,0:T(8,128)(2,1)S(1)}, bf16[256,512]{1,0:T(8,128)(2,1)S(1)}, bf16[256,512]{1,0:T(8,128)(2...) custom-call(s32[11]{0:T(128)S(1)} %pad_add_fusion.info_ref.info, ...), custom_call_target="tpu_custom_call" | custom-call | flops 4026531840 | bytes 5242880 | tf_op jit(solution)/shard_map/pallas_call | solution.py:150
  76.4 1.8 %collective-permute-start.16 = (bf16[2,4,256,128]{3,2,1,0:T(8,128)(2,1)S(1)}, bf16[2,4,256,128]{3,2,1,0:T(8,128)(2,1)S(1)}, u32[]{:S(2)}, u32[]{:S(2)}) collective-permute-start(bf16[2,4,256,128]{3,2,1,0:T(8,128)(2,1)S(1)} %get-tuple-element.94), channel_id=1, source_target_pairs={{8,0},{10,2},{12,4},{14,6},{16,8},{18,10},{20,12},{22,14},{24,16},... | collective-permute-start | bytes 1572872 | tf_op jit(solution)/shard_map/ppermute | solution.py:23
  78.2 2.9 %shard_map.109.refs_2_ = f32[2688,256]{1,0:T(8,128)S(1)} custom-call(bf16[256,2688]{1,0:T(8,128)(2,1)S(1)} %copy-done.2, bf16[384,2688]{1,0:T(8,128)(2,1)S(1)} %shard_map.108.refs_1_, bf16[1024,256]{1,0:T(8,128)(2,1)S(1)} %get-tuple-element.91.refs_3_.refs_2_.refs_1_), custom_call_target="tpu_custom_call" | custom-call | flops 880803840 | bytes 8257536 | tf_op jit(solution)/shard_map/pallas_call | solution.py:293
  81.2 3.1 %shard_map.110 = (bf16[672,256]{1,0:T(8,128)(2,1)S(1)}, bf16[672,256]{1,0:T(8,128)(2,1)S(1)}, bf16[2,672,256]{2,1,0:T(8,128)(2,1)S(1)}) custom-call(s32[11]{0:T(128)S(1)} %pad_add_fusion.info_ref.info, bf16[384,2688]{1,0:T(8,128)(2,1)S(1)} %collective-permute-done.15.refs_0_.refs_2_, bf16[1024,256]{1,0:T(8,128)(2,1)S(1)} %get-tuple-element.91.refs_3_.refs_2_.refs_1_, ...), custom_call_target="tpu_custom_call" | custom-call | flops 1409286144 | bytes 6881280 | tf_op jit(solution)/shard_map/pallas_call | solution.py:344
  84.3 4.7 %collective-permute-start.21 = (bf16[2,672,256]{2,1,0:T(8,128)(2,1)S(1)}, bf16[2,672,256]{2,1,0:T(8,128)(2,1)S(1)}, u32[]{:S(2)}, u32[]{:S(2)}) collective-permute-start(bf16[2,672,256]{2,1,0:T(8,128)(2,1)S(1)} %get-tuple-element.106), channel_id=1, source_target_pairs={{0,16},{2,18},{4,20},{6,22},{8,24},{10,26},{12,28},{14,30},{16,0},... | collective-permute-start | bytes 2064392 | tf_op jit(solution)/shard_map/ppermute | solution.py:27
  93.8 4.5 %shard_map.111 = (bf16[672,256]{1,0:T(8,128)(2,1)S(1)}, bf16[672,256]{1,0:T(8,128)(2,1)S(1)}, bf16[2,672,256]{2,1,0:T(8,128)(2,1)S(1)}) custom-call(s32[11]{0:T(128)S(1)} %pad_add_fusion.info_ref.info, bf16[256,2688]{1,0:T(8,128)(2,1)S(1)} %copy-done.2, bf16[384,2688]{1,0:T(8,128)(2,1)S(1)} %shard_map.108.refs_1_, ...), custom_call_target="tpu_custom_call" | custom-call | flops 1409286144 | bytes 6881280 | tf_op jit(solution)/shard_map/pallas_call | solution.py:344
  98.3 2.2 %collective-permute-start.26 = (bf16[2,672,256]{2,1,0:T(8,128)(2,1)S(1)}, bf16[2,672,256]{2,1,0:T(8,128)(2,1)S(1)}, u32[]{:S(2)}, u32[]{:S(2)}) collective-permute-start(bf16[2,672,256]{2,1,0:T(8,128)(2,1)S(1)} %get-tuple-element.116), channel_id=1, source_target_pairs={{0,8},{2,10},{4,12},{6,14},{8,0},{10,2},{12,4},{14,6},{16,24},{18,... | collective-permute-start | bytes 2064392 | tf_op jit(solution)/shard_map/ppermute | solution.py:27
  101.8 2.6 %collective-permute-start.19 = (bf16[256,512]{1,0:T(8,128)(2,1)S(1)}, bf16[256,512]{1,0:T(8,128)(2,1)S(1)}, u32[]{:S(2)}, u32[]{:S(2)}) collective-permute-start(bf16[256,512]{1,0:T(8,128)(2,1)S(1)} %get-tuple-element.101), channel_id=1, source_target_pairs={{0,4},{2,6},{4,0},{6,2},{8,12},{10,14},{12,8},{14,10},{16,20},{18,... | collective-permute-start | bytes 786440 | tf_op jit(solution)/shard_map/ppermute | solution.py:27
  106.3 7.5 %shard_map.113 = (f32[1344,256]{1,0:T(8,128)S(1)}, bf16[1344,256]{1,0:T(8,128)(2,1)S(1)}) custom-call(s32[11]{0:T(128)S(1)} %pad_add_fusion.info_ref.info, bf16[256,2048]{1,0:T(8,128)(2,1)S(1)} %shard_map.112.attn_ref, bf16[2048,2688]{1,0:T(8,128)(2,1)S(1)} %bitcast.6), custom_call_target="tpu_custom_call" | custom-call | flops 2818572288 | bytes 11010048 | tf_op jit(solution)/shard_map/pallas_call | solution.py:410
  113.9 10.6 %collective-permute-done.21.refs_2_ = bf16[2,672,256]{2,1,0:T(8,128)(2,1)S(1)} collective-permute-done((bf16[2,672,256]{2,1,0:T(8,128)(2,1)S(1)}, bf16[2,672,256]{2,1,0:T(8,128)(2,1)S(1)}, u32[]{:S(2)}, u32[]{:S(2)}) %collective-permute-start.21) | collective-permute-done | bytes 688160 | tf_op jit(solution)/shard_map/ppermute | solution.py:27
  127.3 1.9 %collective-permute-done.26.refs_2_ = bf16[2,672,256]{2,1,0:T(8,128)(2,1)S(1)} collective-permute-done((bf16[2,672,256]{2,1,0:T(8,128)(2,1)S(1)}, bf16[2,672,256]{2,1,0:T(8,128)(2,1)S(1)}, u32[]{:S(2)}, u32[]{:S(2)}) %collective-permute-start.26) | collective-permute-done | bytes 688160 | tf_op jit(solution)/shard_map/ppermute | solution.py:27
  129.9 1.5 collective-permute-start.27
  131.3 2.5 %collective-permute-start.25 = (bf16[672,256]{1,0:T(8,128)(2,1)S(1)}, bf16[672,256]{1,0:T(8,128)(2,1)S(1)}, u32[]{:S(2)}, u32[]{:S(2)}) collective-permute-start(bf16[672,256]{1,0:T(8,128)(2,1)S(1)} %get-tuple-element.107.refs_7_.refs_3_), channel_id=1, source_target_pairs={{0,8},{2,10},{4,12},{6,14},{8,0},{10,2},{12,4},{14,6},{16,24},{18,... | collective-permute-start | bytes 1032200 | tf_op jit(solution)/shard_map/ppermute | solution.py:27
  133.8 1.5 collective-permute-start.23
  136.5 9.2 %collective-permute-done.23.refs_2_.refs_5_ = bf16[256,512]{1,0:T(8,128)(2,1)S(1)} collective-permute-done((bf16[256,512]{1,0:T(8,128)(2,1)S(1)}, bf16[256,512]{1,0:T(8,128)(2,1)S(1)}, u32[]{:S(2)}, u32[]{:S(2)}) %collective-permute-start.23) | collective-permute-done | bytes 262176 | tf_op jit(solution)/shard_map/ppermute | solution.py:27
  151.5 1.6 shard_map.117
  153.1 1.5 shard_map.114
  154.6 1.6 %shard_map.118 = (bf16[256,1024]{1,0:T(8,128)(2,1)}, bf16[256,1024]{1,0:T(8,128)(2,1)}) custom-call(s32[11]{0:T(128)S(1)} %pad_add_fusion.info_ref.info, bf16[256,512]{1,0:T(8,128)(2,1)S(1)} %get-tuple-element.108.refs_4_.refs_0_, bf16[256,512]{1,0:T(8,128)(2,1)S(1)} %collective-permute-done.22.refs_1_.refs_4_, ...), custom_call_target="tpu_custom_call" | custom-call | bytes 2097152 | tf_op jit(solution)/shard_map/pallas_call | solution.py:187
  156.2 2.1 %collective-permute-done.29.refs_2_ = bf16[168,512]{1,0:T(8,128)(2,1)S(1)} collective-permute-done((bf16[168,512]{1,0:T(8,128)(2,1)S(1)}, bf16[168,512]{1,0:T(8,128)(2,1)S(1)}, u32[]{:S(2)}, u32[]{:S(2)}) %collective-permute-start.29) | collective-permute-done | bytes 172064 | tf_op jit(solution)/shard_map/ppermute | solution.py:27
  158.4 1.7 %shard_map.121 = f32[168,2048]{1,0:T(8,128)} custom-call(s32[11]{0:T(128)S(1)} %pad_add_fusion.info_ref.info, bf16[168,512]{1,0:T(8,128)(2,1)S(1)} %get-tuple-element.119.refs_0_, bf16[168,512]{1,0:T(8,128)(2,1)S(1)} %collective-permute-done.28.refs_1_, bf16[168,512]{1,0:T(8,128)(2,1)S(1)} %collective-permute-done.29.refs_2_, ...), custom_call_target="tpu_custom_call" | custom-call | bytes 2064384 | tf_op jit(solution)/shard_map/pallas_call | solution.py:187
  (72 shorter events, 29.2 us)
Async XLA Ops:
  3.0 19.6 %collective-permute-start.3 = (bf16[256,512]{1,0:T(8,128)(2,1)S(1)}, bf16[256,512]{1,0:T(8,128)(2,1)S(1)}, u32[]{:S(2)}, u32[]{:S(2)}) collective-permute-start(bf16[256,512]{1,0:T(8,128)(2,1)S(1)} %get-tuple-element.73), channel_id=1, source_target_pairs={{0,2},{2,0},{4,6},{6,4},{8,10},{10,8},{12,14},{14,12},{16,18},{18,... | collective-permute-start | bytes 786440 | tf_op jit(solution)/shard_map/ppermute | solution.py:27
  6.0 16.6 %collective-permute-start.4 = (bf16[256,512]{1,0:T(8,128)(2,1)S(1)}, bf16[256,512]{1,0:T(8,128)(2,1)S(1)}, u32[]{:S(2)}, u32[]{:S(2)}) collective-permute-start(bf16[256,512]{1,0:T(8,128)(2,1)S(1)} %get-tuple-element.74), channel_id=1, source_target_pairs={{0,4},{2,6},{4,0},{6,2},{8,12},{10,14},{12,8},{14,10},{16,20},{18,... | collective-permute-start | bytes 786440 | tf_op jit(solution)/shard_map/ppermute | solution.py:27
  7.5 15.1 %collective-permute-start.5 = (bf16[256,512]{1,0:T(8,128)(2,1)S(1)}, bf16[256,512]{1,0:T(8,128)(2,1)S(1)}, u32[]{:S(2)}, u32[]{:S(2)}) collective-permute-start(bf16[256,512]{1,0:T(8,128)(2,1)S(1)} %get-tuple-element.75), channel_id=1, source_target_pairs={{0,6},{2,4},{4,2},{6,0},{8,14},{10,12},{12,10},{14,8},{16,22},{18,... | collective-permute-start | bytes 786440 | tf_op jit(solution)/shard_map/ppermute | solution.py:27
  19.0 14.9 %collective-permute-start = (bf16[256,1024]{1,0:T(8,128)(2,1)S(1)}, bf16[256,1024]{1,0:T(8,128)(2,1)S(1)}, u32[]{:S(2)}, u32[]{:S(2)}) collective-permute-start(bf16[256,1024]{1,0:T(8,128)(2,1)S(1)} %get-tuple-element.69.refs_5_), channel_id=1, source_target_pairs={{0,2},{2,0},{4,6},{6,4},{8,10},{10,8},{12,14},{14,12},{16,18},{18,... | collective-permute-start | bytes 1572872 | tf_op jit(solution)/shard_map/ppermute | solution.py:27
  21.0 23.8 %collective-permute-start.1 = (bf16[256,1024]{1,0:T(8,128)(2,1)S(1)}, bf16[256,1024]{1,0:T(8,128)(2,1)S(1)}, u32[]{:S(2)}, u32[]{:S(2)}) collective-permute-start(bf16[256,1024]{1,0:T(8,128)(2,1)S(1)} %get-tuple-element.70.refs_6_), channel_id=1, source_target_pairs={{0,4},{2,6},{4,0},{6,2},{8,12},{10,14},{12,8},{14,10},{16,20},{18,... | collective-permute-start | bytes 1572872 | tf_op jit(solution)/shard_map/ppermute | solution.py:27
  22.5 22.3 %collective-permute-start.2 = (bf16[256,1024]{1,0:T(8,128)(2,1)S(1)}, bf16[256,1024]{1,0:T(8,128)(2,1)S(1)}, u32[]{:S(2)}, u32[]{:S(2)}) collective-permute-start(bf16[256,1024]{1,0:T(8,128)(2,1)S(1)} %get-tuple-element.71.refs_7_), channel_id=1, source_target_pairs={{0,6},{2,4},{4,2},{6,0},{8,14},{10,12},{12,10},{14,8},{16,22},{18,... | collective-permute-start | bytes 1572872 | tf_op jit(solution)/shard_map/ppermute | solution.py:27
  23.3 25.0 %collective-permute-start.7 = (bf16[4,256,256]{2,1,0:T(8,128)(2,1)S(1)}, bf16[4,256,256]{2,1,0:T(8,128)(2,1)S(1)}, u32[]{:S(2)}, u32[]{:S(2)}) collective-permute-start(bf16[4,256,256]{2,1,0:T(8,128)(2,1)S(1)} %get-tuple-element.77.refs_8_.refs_9_), channel_id=1, source_target_pairs={{0,8},{2,10},{4,12},{6,14},{8,16},{10,18},{12,20},{14,22},{16,24},... | collective-permute-start | bytes 1572872 | tf_op jit(solution)/shard_map/ppermute | solution.py:23
  27.9 34.7 %collective-permute-start.6 = (bf16[4,256,256]{2,1,0:T(8,128)(2,1)S(1)}, bf16[4,256,256]{2,1,0:T(8,128)(2,1)S(1)}, u32[]{:S(2)}, u32[]{:S(2)}) collective-permute-start(bf16[4,256,256]{2,1,0:T(8,128)(2,1)S(1)} %get-tuple-element.76.refs_8_.refs_9_), channel_id=1, source_target_pairs={{0,8},{2,10},{4,12},{6,14},{8,16},{10,18},{12,20},{14,22},{16,24},... | collective-permute-start | bytes 1572872 | tf_op jit(solution)/shard_map/ppermute | solution.py:23
  44.8 30.8 %collective-permute-start.13 = (bf16[128,2688]{1,0:T(8,128)(2,1)S(1)}, bf16[128,2688]{1,0:T(8,128)(2,1)S(1)}, u32[]{:S(2)}, u32[]{:S(2)}) collective-permute-start(bf16[128,2688]{1,0:T(8,128)(2,1)S(1)} %shard_map.107), channel_id=1, source_target_pairs={{0,6},{2,4},{4,2},{6,0},{8,14},{10,12},{12,10},{14,8},{16,22},{18,... | collective-permute-start | bytes 2064392 | tf_op jit(solution)/shard_map/ppermute | solution.py:27
  46.3 29.3 %collective-permute-start.12 = (bf16[128,2688]{1,0:T(8,128)(2,1)S(1)}, bf16[128,2688]{1,0:T(8,128)(2,1)S(1)}, u32[]{:S(2)}, u32[]{:S(2)}) collective-permute-start(bf16[128,2688]{1,0:T(8,128)(2,1)S(1)} %shard_map.107), channel_id=1, source_target_pairs={{0,4},{2,6},{4,0},{6,2},{8,12},{10,14},{12,8},{14,10},{16,20},{18,... | collective-permute-start | bytes 2064392 | tf_op jit(solution)/shard_map/ppermute | solution.py:27
  47.5 28.2 %collective-permute-start.11 = (bf16[128,2688]{1,0:T(8,128)(2,1)S(1)}, bf16[128,2688]{1,0:T(8,128)(2,1)S(1)}, u32[]{:S(2)}, u32[]{:S(2)}) collective-permute-start(bf16[128,2688]{1,0:T(8,128)(2,1)S(1)} %shard_map.107), channel_id=1, source_target_pairs={{0,2},{2,0},{4,6},{6,4},{8,10},{10,8},{12,14},{14,12},{16,18},{18,... | collective-permute-start | bytes 2064392 | tf_op jit(solution)/shard_map/ppermute | solution.py:27
  61.1 14.5 %collective-permute-start.14 = (bf16[2,4,256,128]{3,2,1,0:T(8,128)(2,1)S(1)}, bf16[2,4,256,128]{3,2,1,0:T(8,128)(2,1)S(1)}, u32[]{:S(2)}, u32[]{:S(2)}) collective-permute-start(bf16[2,4,256,128]{3,2,1,0:T(8,128)(2,1)S(1)} %get-tuple-element.93), channel_id=1, source_target_pairs={{8,0},{10,2},{12,4},{14,6},{16,8},{18,10},{20,12},{22,14},{24,16},... | collective-permute-start | bytes 1572872 | tf_op jit(solution)/shard_map/ppermute | solution.py:23
  75.6 30.7 %slice-start = ((s8[11010048]{0:T(1024)(128)(4,1)}), s8[4194304]{0:T(1024)(128)(4,1)S(1)}, s32[]{:S(2)}) async-start(s8[11010048]{0:T(1024)(128)(4,1)} %bitcast.5), calls=%async_computation | async-start | bytes 8388608
  76.3 4.8 %collective-permute-start.15 = (bf16[384,2688]{1,0:T(8,128)(2,1)S(1)}, bf16[384,2688]{1,0:T(8,128)(2,1)S(1)}, u32[]{:S(2)}, u32[]{:S(2)}) collective-permute-start(bf16[384,2688]{1,0:T(8,128)(2,1)S(1)} %shard_map.108.refs_1_), channel_id=1, source_target_pairs={{0,1},{1,0},{2,3},{3,2},{4,5},{5,4},{6,7},{7,6},{8,9},{9,8},{10,11... | collective-permute-start | bytes 6193160 | tf_op jit(solution)/shard_map/ppermute | solution.py:27
  76.4 17.3 %collective-permute-start.16 = (bf16[2,4,256,128]{3,2,1,0:T(8,128)(2,1)S(1)}, bf16[2,4,256,128]{3,2,1,0:T(8,128)(2,1)S(1)}, u32[]{:S(2)}, u32[]{:S(2)}) collective-permute-start(bf16[2,4,256,128]{3,2,1,0:T(8,128)(2,1)S(1)} %get-tuple-element.94), channel_id=1, source_target_pairs={{8,0},{10,2},{12,4},{14,6},{16,8},{18,10},{20,12},{22,14},{24,16},... | collective-permute-start | bytes 1572872 | tf_op jit(solution)/shard_map/ppermute | solution.py:23
  84.3 40.2 %collective-permute-start.21 = (bf16[2,672,256]{2,1,0:T(8,128)(2,1)S(1)}, bf16[2,672,256]{2,1,0:T(8,128)(2,1)S(1)}, u32[]{:S(2)}, u32[]{:S(2)}) collective-permute-start(bf16[2,672,256]{2,1,0:T(8,128)(2,1)S(1)} %get-tuple-element.106), channel_id=1, source_target_pairs={{0,16},{2,18},{4,20},{6,22},{8,24},{10,26},{12,28},{14,30},{16,0},... | collective-permute-start | bytes 2064392 | tf_op jit(solution)/shard_map/ppermute | solution.py:27
  89.0 11.5 %collective-permute-start.8 = (bf16[256,512]{1,0:T(8,128)(2,1)S(1)}, bf16[256,512]{1,0:T(8,128)(2,1)S(1)}, u32[]{:S(2)}, u32[]{:S(2)}) collective-permute-start(bf16[256,512]{1,0:T(8,128)(2,1)S(1)} %get-tuple-element.87), channel_id=1, source_target_pairs={{0,2},{2,0},{4,6},{6,4},{8,10},{10,8},{12,14},{14,12},{16,18},{18,... | collective-permute-start | bytes 786440 | tf_op jit(solution)/shard_map/ppermute | solution.py:27
  90.3 11.5 %collective-permute-start.9 = (bf16[256,512]{1,0:T(8,128)(2,1)S(1)}, bf16[256,512]{1,0:T(8,128)(2,1)S(1)}, u32[]{:S(2)}, u32[]{:S(2)}) collective-permute-start(bf16[256,512]{1,0:T(8,128)(2,1)S(1)} %get-tuple-element.88), channel_id=1, source_target_pairs={{0,4},{2,6},{4,0},{6,2},{8,12},{10,14},{12,8},{14,10},{16,20},{18,... | collective-permute-start | bytes 786440 | tf_op jit(solution)/shard_map/ppermute | solution.py:27
  91.1 13.2 %collective-permute-start.10 = (bf16[256,512]{1,0:T(8,128)(2,1)S(1)}, bf16[256,512]{1,0:T(8,128)(2,1)S(1)}, u32[]{:S(2)}, u32[]{:S(2)}) collective-permute-start(bf16[256,512]{1,0:T(8,128)(2,1)S(1)} %get-tuple-element.89), channel_id=1, source_target_pairs={{0,6},{2,4},{4,2},{6,0},{8,14},{10,12},{12,10},{14,8},{16,22},{18,... | collective-permute-start | bytes 786440 | tf_op jit(solution)/shard_map/ppermute | solution.py:27
  98.3 30.9 %collective-permute-start.26 = (bf16[2,672,256]{2,1,0:T(8,128)(2,1)S(1)}, bf16[2,672,256]{2,1,0:T(8,128)(2,1)S(1)}, u32[]{:S(2)}, u32[]{:S(2)}) collective-permute-start(bf16[2,672,256]{2,1,0:T(8,128)(2,1)S(1)} %get-tuple-element.116), channel_id=1, source_target_pairs={{0,8},{2,10},{4,12},{6,14},{8,0},{10,2},{12,4},{14,6},{16,24},{18,... | collective-permute-start | bytes 2064392 | tf_op jit(solution)/shard_map/ppermute | solution.py:27
  100.5 24.7 %collective-permute-start.18 = (bf16[256,512]{1,0:T(8,128)(2,1)S(1)}, bf16[256,512]{1,0:T(8,128)(2,1)S(1)}, u32[]{:S(2)}, u32[]{:S(2)}) collective-permute-start(bf16[256,512]{1,0:T(8,128)(2,1)S(1)} %get-tuple-element.100), channel_id=1, source_target_pairs={{0,2},{2,0},{4,6},{6,4},{8,10},{10,8},{12,14},{14,12},{16,18},{18,... | collective-permute-start | bytes 786440 | tf_op jit(solution)/shard_map/ppermute | solution.py:27
  101.8 23.5 %collective-permute-start.19 = (bf16[256,512]{1,0:T(8,128)(2,1)S(1)}, bf16[256,512]{1,0:T(8,128)(2,1)S(1)}, u32[]{:S(2)}, u32[]{:S(2)}) collective-permute-start(bf16[256,512]{1,0:T(8,128)(2,1)S(1)} %get-tuple-element.101), channel_id=1, source_target_pairs={{0,4},{2,6},{4,0},{6,2},{8,12},{10,14},{12,8},{14,10},{16,20},{18,... | collective-permute-start | bytes 786440 | tf_op jit(solution)/shard_map/ppermute | solution.py:27
  104.3 20.9 %collective-permute-start.20 = (bf16[256,512]{1,0:T(8,128)(2,1)S(1)}, bf16[256,512]{1,0:T(8,128)(2,1)S(1)}, u32[]{:S(2)}, u32[]{:S(2)}) collective-permute-start(bf16[256,512]{1,0:T(8,128)(2,1)S(1)} %get-tuple-element.102), channel_id=1, source_target_pairs={{0,6},{2,4},{4,2},{6,0},{8,14},{10,12},{12,10},{14,8},{16,22},{18,... | collective-permute-start | bytes 786440 | tf_op jit(solution)/shard_map/ppermute | solution.py:27
  126.0 9.3 %collective-permute-start.22 = (bf16[256,512]{1,0:T(8,128)(2,1)S(1)}, bf16[256,512]{1,0:T(8,128)(2,1)S(1)}, u32[]{:S(2)}, u32[]{:S(2)}) collective-permute-start(bf16[256,512]{1,0:T(8,128)(2,1)S(1)} %get-tuple-element.109.refs_5_), channel_id=1, source_target_pairs={{0,2},{2,0},{4,6},{6,4},{8,10},{10,8},{12,14},{14,12},{16,18},{18,... | collective-permute-start | bytes 786440 | tf_op jit(solution)/shard_map/ppermute | solution.py:27
  127.3 25.8 %collective-permute-start.17 = (bf16[1344,256]{1,0:T(8,128)(2,1)S(1)}, bf16[1344,256]{1,0:T(8,128)(2,1)S(1)}, u32[]{:S(2)}, u32[]{:S(2)}) collective-permute-start(bf16[1344,256]{1,0:T(8,128)(2,1)S(1)} %get-tuple-element.98.refs_3_), channel_id=1, source_target_pairs={{0,1},{1,0},{2,3},{3,2},{4,5},{5,4},{6,7},{7,6},{8,9},{9,8},{10,11... | collective-permute-start | bytes 2064392 | tf_op jit(solution)/shard_map/ppermute | solution.py:27
  129.9 17.2 %collective-permute-start.27 = (bf16[672,256]{1,0:T(8,128)(2,1)S(1)}, bf16[672,256]{1,0:T(8,128)(2,1)S(1)}, u32[]{:S(2)}, u32[]{:S(2)}) collective-permute-start(bf16[672,256]{1,0:T(8,128)(2,1)S(1)} %get-tuple-element.118), channel_id=1, source_target_pairs={{0,16},{2,18},{4,20},{6,22},{8,24},{10,26},{12,28},{14,30},{16,0},... | collective-permute-start | bytes 1032200 | tf_op jit(solution)/shard_map/ppermute | solution.py:27
  131.3 15.8 %collective-permute-start.25 = (bf16[672,256]{1,0:T(8,128)(2,1)S(1)}, bf16[672,256]{1,0:T(8,128)(2,1)S(1)}, u32[]{:S(2)}, u32[]{:S(2)}) collective-permute-start(bf16[672,256]{1,0:T(8,128)(2,1)S(1)} %get-tuple-element.107.refs_7_.refs_3_), channel_id=1, source_target_pairs={{0,8},{2,10},{4,12},{6,14},{8,0},{10,2},{12,4},{14,6},{16,24},{18,... | collective-permute-start | bytes 1032200 | tf_op jit(solution)/shard_map/ppermute | solution.py:27
  133.8 11.9 %collective-permute-start.23 = (bf16[256,512]{1,0:T(8,128)(2,1)S(1)}, bf16[256,512]{1,0:T(8,128)(2,1)S(1)}, u32[]{:S(2)}, u32[]{:S(2)}) collective-permute-start(bf16[256,512]{1,0:T(8,128)(2,1)S(1)} %get-tuple-element.110.refs_6_), channel_id=1, source_target_pairs={{0,4},{2,6},{4,0},{6,2},{8,12},{10,14},{12,8},{14,10},{16,20},{18,... | collective-permute-start | bytes 786440 | tf_op jit(solution)/shard_map/ppermute | solution.py:27
  135.4 10.4 %collective-permute-start.24 = (bf16[256,512]{1,0:T(8,128)(2,1)S(1)}, bf16[256,512]{1,0:T(8,128)(2,1)S(1)}, u32[]{:S(2)}, u32[]{:S(2)}) collective-permute-start(bf16[256,512]{1,0:T(8,128)(2,1)S(1)} %get-tuple-element.111.refs_7_), channel_id=1, source_target_pairs={{0,6},{2,4},{4,2},{6,0},{8,14},{10,12},{12,10},{14,8},{16,22},{18,... | collective-permute-start | bytes 786440 | tf_op jit(solution)/shard_map/ppermute | solution.py:27
  147.9 8.3 %collective-permute-start.28 = (bf16[168,512]{1,0:T(8,128)(2,1)S(1)}, bf16[168,512]{1,0:T(8,128)(2,1)S(1)}, u32[]{:S(2)}, u32[]{:S(2)}) collective-permute-start(bf16[168,512]{1,0:T(8,128)(2,1)S(1)} %get-tuple-element.120), channel_id=1, source_target_pairs={{0,2},{2,0},{4,6},{6,4},{8,10},{10,8},{12,14},{14,12},{16,18},{18,... | collective-permute-start | bytes 516104 | tf_op jit(solution)/shard_map/ppermute | solution.py:27
  149.3 9.1 %collective-permute-start.29 = (bf16[168,512]{1,0:T(8,128)(2,1)S(1)}, bf16[168,512]{1,0:T(8,128)(2,1)S(1)}, u32[]{:S(2)}, u32[]{:S(2)}) collective-permute-start(bf16[168,512]{1,0:T(8,128)(2,1)S(1)} %get-tuple-element.121), channel_id=1, source_target_pairs={{0,4},{2,6},{4,0},{6,2},{8,12},{10,14},{12,8},{14,10},{16,20},{18,... | collective-permute-start | bytes 516104 | tf_op jit(solution)/shard_map/ppermute | solution.py:27
  150.2 8.2 %collective-permute-start.30 = (bf16[168,512]{1,0:T(8,128)(2,1)S(1)}, bf16[168,512]{1,0:T(8,128)(2,1)S(1)}, u32[]{:S(2)}, u32[]{:S(2)}) collective-permute-start(bf16[168,512]{1,0:T(8,128)(2,1)S(1)} %get-tuple-element.122), channel_id=1, source_target_pairs={{0,6},{2,4},{4,2},{6,0},{8,14},{10,12},{12,10},{14,8},{16,22},{18,... | collective-permute-start | bytes 516104 | tf_op jit(solution)/shard_map/ppermute | solution.py:27
  (8 other events, 62.8 us)

commit v7 on v5

--- a/solution.py
+++ b/solution.py
@@ -429,7 +429,8 @@
     def pack_half(info_ref, ins, outs):
         outs[0][...] = ins[0][pl.ds(pl.multiple_of(info_ref[1] * (rows // 2), 16), rows // 2), :]
 
-    half = moved(pack_half, info, [out_grad], [shape(rows // 2, d_out)], q_and_d[1:])[0]
+    half = moved(pack_half, info, [out_grad], [shape(rows // 2, d_out)])[0]
+    half, *_ = lax.optimization_barrier((half, *q_and_d[1:]))
     near = traded([half] * GROUP)[1:]
 
     def pack_near(info_ref, ins, outs):

time: 161 us -> 161 us (level)
  no operation moved by 1% of the time
where the time goes in v7:
time: 161 us; the launch traced here: 160 us
  Pallas kernels  59.7 us (37%)
  waiting for transfers between devices  46.4 us (29%)
  starting transfers between devices  44.7 us (28%)
  local copies, waits for them, and re-layouts  8.3 us (5%)
    ppermute x27, waiting for transfers between devices, swapped(): lax.ppermute(shard, axis, [(i, i ^ by) for i in range(lax.axis_size(axis))])  43.6 us
    ppermute x27, starting transfers between devices, swapped(): lax.ppermute(shard, axis, [(i, i ^ by) for i in range(lax.axis_size(axis))])  34 us
    pallas_call x2, Pallas kernels, attention(): pl.pallas_call(functools.partial(attention_kernel, rows, len(held)), grid...  25.8 us
    pallas_call x12, Pallas kernels, moved(): pl.pallas_call(kernel, grid=(1,), in_specs=[SMEM] + [entire(a) for a in a...  11.9 us
    ppermute x4, starting transfers between devices, shifted(): return lax.ppermute(shard, axis, pairs)  10.7 us
    pallas_call x2, Pallas kernels, weight_terms(): pl.pallas_call(kernel, grid=(steps,), in_specs=[SMEM] + [pl.BlockSpec((p....  9.04 us
    unnamed x18, local copies, waits for them, and re-layouts  7.57 us
    pallas_call x1, Pallas kernels, project(): pl.pallas_call(kernel, grid=(steps,), in_specs=[SMEM, entire(attn), pl.Bl...  7.54 us
  transfers between devices with their start and end apart: 31, of which 11 were waited for; matrix products, arithmetic and copies ran while one was open for 1% of the time, Pallas kernels for 36%

profile of v7, /device:TPU:0, one launch (start us, length us, event | category | flops | bytes accessed | tf_op | source)
XLA Modules:
  0.0 160.2 jit_solution(14019721208053520298)
XLA Ops:
  3.0 3.0 %collective-permute-start.3 = (bf16[256,512]{1,0:T(8,128)(2,1)S(1)}, bf16[256,512]{1,0:T(8,128)(2,1)S(1)}, u32[]{:S(2)}, u32[]{:S(2)}) collective-permute-start(bf16[256,512]{1,0:T(8,128)(2,1)S(1)} %get-tuple-element.73), channel_id=1, source_target_pairs={{0,2},{2,0},{4,6},{6,4},{8,10},{10,8},{12,14},{14,12},{16,18},{18,... | collective-permute-start | bytes 786440 | tf_op jit(solution)/shard_map/ppermute | solution.py:27
  6.0 1.5 collective-permute-start.4
  8.3 4.1 %copy-done = bf16[2048,2688]{1,0:T(8,128)(2,1)S(1)} copy-done((bf16[2048,2688]{1,0:T(8,128)(2,1)S(1)}, bf16[2048,2688]{1,0:T(8,128)(2,1)}, u32[]{:S(2)}) %copy-start) | copy-done | bytes 11010072
  13.8 4.5 %shard_map.101 = (bf16[256,512]{1,0:T(8,128)(2,1)S(1)}, bf16[256,512]{1,0:T(8,128)(2,1)S(1)}, bf16[256,512]{1,0:T(8,128)(2,1)S(1)}, bf16[256,512]{1,0:T(8,128)(2,1)S(1)}) custom-call(s32[11]{0:T(128)S(1)} %pad_add_fusion.info_ref.info, bf16[256,2688]{1,0:T(8,128)(2,1)S(1)} %copy-done.1, bf16[2048,2688]{1,0:T(8,128)(2,1)S(1)} %copy-done), custom_call_target="tpu_custom_call" | custom-call | flops 2818572288 | bytes 11010048 | tf_op jit(solution)/shard_map/pallas_call | solution.py:257
  19.0 2.0 %collective-permute-start = (bf16[256,1024]{1,0:T(8,128)(2,1)S(1)}, bf16[256,1024]{1,0:T(8,128)(2,1)S(1)}, u32[]{:S(2)}, u32[]{:S(2)}) collective-permute-start(bf16[256,1024]{1,0:T(8,128)(2,1)S(1)} %get-tuple-element.69.refs_5_), channel_id=1, source_target_pairs={{0,2},{2,0},{4,6},{6,4},{8,10},{10,8},{12,14},{14,12},{16,18},{18,... | collective-permute-start | bytes 1572872 | tf_op jit(solution)/shard_map/ppermute | solution.py:27
  21.0 1.5 collective-permute-start.1
  23.3 4.0 %collective-permute-start.7 = (bf16[4,256,256]{2,1,0:T(8,128)(2,1)S(1)}, bf16[4,256,256]{2,1,0:T(8,128)(2,1)S(1)}, u32[]{:S(2)}, u32[]{:S(2)}) collective-permute-start(bf16[4,256,256]{2,1,0:T(8,128)(2,1)S(1)} %get-tuple-element.77.refs_8_.refs_9_), channel_id=1, source_target_pairs={{0,8},{2,10},{4,12},{6,14},{8,16},{10,18},{12,20},{14,22},{16,24},... | collective-permute-start | bytes 1572872 | tf_op jit(solution)/shard_map/ppermute | solution.py:23
  27.9 3.5 %collective-permute-start.6 = (bf16[4,256,256]{2,1,0:T(8,128)(2,1)S(1)}, bf16[4,256,256]{2,1,0:T(8,128)(2,1)S(1)}, u32[]{:S(2)}, u32[]{:S(2)}) collective-permute-start(bf16[4,256,256]{2,1,0:T(8,128)(2,1)S(1)} %get-tuple-element.76.refs_8_.refs_9_), channel_id=1, source_target_pairs={{0,8},{2,10},{4,12},{6,14},{8,16},{10,18},{12,20},{14,22},{16,24},... | collective-permute-start | bytes 1572872 | tf_op jit(solution)/shard_map/ppermute | solution.py:23
  31.4 2.6 %collective-permute-done.refs_1_.refs_5_ = bf16[256,1024]{1,0:T(8,128)(2,1)S(1)} collective-permute-done((bf16[256,1024]{1,0:T(8,128)(2,1)S(1)}, bf16[256,1024]{1,0:T(8,128)(2,1)S(1)}, u32[]{:S(2)}, u32[]{:S(2)}) %collective-permute-start) | collective-permute-done | bytes 524320 | tf_op jit(solution)/shard_map/ppermute | solution.py:27
  33.9 10.9 %collective-permute-done.1.refs_2_.refs_6_ = bf16[256,1024]{1,0:T(8,128)(2,1)S(1)} collective-permute-done((bf16[256,1024]{1,0:T(8,128)(2,1)S(1)}, bf16[256,1024]{1,0:T(8,128)(2,1)S(1)}, u32[]{:S(2)}, u32[]{:S(2)}) %collective-permute-start.1) | collective-permute-done | bytes 524320 | tf_op jit(solution)/shard_map/ppermute | solution.py:27
  44.8 1.5 collective-permute-start.13
  48.3 12.8 %shard_map.105 = (bf16[256,256]{1,0:T(8,128)(2,1)S(1)}, bf16[256,256]{1,0:T(8,128)(2,1)S(1)}, bf16[256,256]{1,0:T(8,128)(2,1)S(1)}, bf16[256,256]{1,0:T(8,128)(2...) custom-call(s32[11]{0:T(128)S(1)} %pad_add_fusion.info_ref.info, ...), custom_call_target="tpu_custom_call" | custom-call | flops 4026531840 | bytes 5242880 | tf_op jit(solution)/shard_map/pallas_call | solution.py:150
  61.1 1.5 collective-permute-start.14
  62.6 13.0 %shard_map.106 = (bf16[256,512]{1,0:T(8,128)(2,1)S(1)}, bf16[256,512]{1,0:T(8,128)(2,1)S(1)}, bf16[256,512]{1,0:T(8,128)(2,1)S(1)}, bf16[256,512]{1,0:T(8,128)(2...) custom-call(s32[11]{0:T(128)S(1)} %pad_add_fusion.info_ref.info, ...), custom_call_target="tpu_custom_call" | custom-call | flops 4026531840 | bytes 5242880 | tf_op jit(solution)/shard_map/pallas_call | solution.py:150
  76.4 1.8 %collective-permute-start.16 = (bf16[2,4,256,128]{3,2,1,0:T(8,128)(2,1)S(1)}, bf16[2,4,256,128]{3,2,1,0:T(8,128)(2,1)S(1)}, u32[]{:S(2)}, u32[]{:S(2)}) collective-permute-start(bf16[2,4,256,128]{3,2,1,0:T(8,128)(2,1)S(1)} %get-tuple-element.94), channel_id=1, source_target_pairs={{8,0},{10,2},{12,4},{14,6},{16,8},{18,10},{20,12},{22,14},{24,16},... | collective-permute-start | bytes 1572872 | tf_op jit(solution)/shard_map/ppermute | solution.py:23
  78.2 2.3 %collective-permute-done.15.refs_2_ = bf16[384,2688]{1,0:T(8,128)(2,1)S(1)} collective-permute-done((bf16[384,2688]{1,0:T(8,128)(2,1)S(1)}, bf16[384,2688]{1,0:T(8,128)(2,1)S(1)}, u32[]{:S(2)}, u32[]{:S(2)}) %collective-permute-start.15) | collective-permute-done | bytes 2064416 | tf_op jit(solution)/shard_map/ppermute | solution.py:27
  80.5 4.5 %shard_map.109 = (bf16[672,256]{1,0:T(8,128)(2,1)S(1)}, bf16[672,256]{1,0:T(8,128)(2,1)S(1)}, bf16[2,672,256]{2,1,0:T(8,128)(2,1)S(1)}) custom-call(s32[11]{0:T(128)S(1)} %pad_add_fusion.info_ref.info, bf16[256,2688]{1,0:T(8,128)(2,1)S(1)} %copy-done.2, bf16[384,2688]{1,0:T(8,128)(2,1)S(1)} %shard_map.108.refs_1_, ...), custom_call_target="tpu_custom_call" | custom-call | flops 1409286144 | bytes 6881280 | tf_op jit(solution)/shard_map/pallas_call | solution.py:308
  85.0 2.7 %collective-permute-start.21 = (bf16[2,672,256]{2,1,0:T(8,128)(2,1)S(1)}, bf16[2,672,256]{2,1,0:T(8,128)(2,1)S(1)}, u32[]{:S(2)}, u32[]{:S(2)}) collective-permute-start(bf16[2,672,256]{2,1,0:T(8,128)(2,1)S(1)} %get-tuple-element.106), channel_id=1, source_target_pairs={{0,8},{2,10},{4,12},{6,14},{8,0},{10,2},{12,4},{14,6},{16,24},{18,... | collective-permute-start | bytes 2064392 | tf_op jit(solution)/shard_map/ppermute | solution.py:27
  91.2 2.8 %collective-permute-done.16.refs_4_.refs_3_ = bf16[2,4,256,128]{3,2,1,0:T(8,128)(2,1)S(1)} collective-permute-done((bf16[2,4,256,128]{3,2,1,0:T(8,128)(2,1)S(1)}, bf16[2,4,256,128]{3,2,1,0:T(8,128)(2,1)S(1)}, u32[]{:S(2)}, u32[]{:S(2)}) %collective-permute-start.16) | collective-permute-done | bytes 524320 | tf_op jit(solution)/shard_map/ppermute | solution.py:23
  94.0 4.5 %shard_map.110 = (bf16[672,256]{1,0:T(8,128)(2,1)S(1)}, bf16[672,256]{1,0:T(8,128)(2,1)S(1)}, bf16[2,672,256]{2,1,0:T(8,128)(2,1)S(1)}) custom-call(s32[11]{0:T(128)S(1)} %pad_add_fusion.info_ref.info, bf16[256,2688]{1,0:T(8,128)(2,1)S(1)} %copy-done.2, bf16[384,2688]{1,0:T(8,128)(2,1)S(1)} %shard_map.108.refs_1_, ...), custom_call_target="tpu_custom_call" | custom-call | flops 1409286144 | bytes 6881280 | tf_op jit(solution)/shard_map/pallas_call | solution.py:308
  98.6 3.0 %collective-permute-start.26 = (bf16[2,672,256]{2,1,0:T(8,128)(2,1)S(1)}, bf16[2,672,256]{2,1,0:T(8,128)(2,1)S(1)}, u32[]{:S(2)}, u32[]{:S(2)}) collective-permute-start(bf16[2,672,256]{2,1,0:T(8,128)(2,1)S(1)} %get-tuple-element.116), channel_id=1, source_target_pairs={{0,16},{2,18},{4,20},{6,22},{8,24},{10,26},{12,28},{14,30},{16,0},... | collective-permute-start | bytes 2064392 | tf_op jit(solution)/shard_map/ppermute | solution.py:27
  105.7 7.5 %shard_map.112 = (f32[1344,256]{1,0:T(8,128)S(1)}, bf16[1344,256]{1,0:T(8,128)(2,1)S(1)}) custom-call(s32[11]{0:T(128)S(1)} %pad_add_fusion.info_ref.info, bf16[256,2048]{1,0:T(8,128)(2,1)S(1)} %shard_map.111.attn_ref, bf16[2048,2688]{1,0:T(8,128)(2,1)S(1)} %bitcast.6), custom_call_target="tpu_custom_call" | custom-call | flops 2818572288 | bytes 11010048 | tf_op jit(solution)/shard_map/pallas_call | solution.py:373
  113.2 4.3 %collective-permute-done.21.refs_2_ = bf16[2,672,256]{2,1,0:T(8,128)(2,1)S(1)} collective-permute-done((bf16[2,672,256]{2,1,0:T(8,128)(2,1)S(1)}, bf16[2,672,256]{2,1,0:T(8,128)(2,1)S(1)}, u32[]{:S(2)}, u32[]{:S(2)}) %collective-permute-start.21) | collective-permute-done | bytes 688160 | tf_op jit(solution)/shard_map/ppermute | solution.py:27
  120.3 10.9 %collective-permute-done.26.refs_2_ = bf16[2,672,256]{2,1,0:T(8,128)(2,1)S(1)} collective-permute-done((bf16[2,672,256]{2,1,0:T(8,128)(2,1)S(1)}, bf16[2,672,256]{2,1,0:T(8,128)(2,1)S(1)}, u32[]{:S(2)}, u32[]{:S(2)}) %collective-permute-start.26) | collective-permute-done | bytes 688160 | tf_op jit(solution)/shard_map/ppermute | solution.py:27
  132.0 2.1 %collective-permute-start.25 = (bf16[672,256]{1,0:T(8,128)(2,1)S(1)}, bf16[672,256]{1,0:T(8,128)(2,1)S(1)}, u32[]{:S(2)}, u32[]{:S(2)}) collective-permute-start(bf16[672,256]{1,0:T(8,128)(2,1)S(1)} %get-tuple-element.107.refs_7_.refs_3_), channel_id=1, source_target_pairs={{0,16},{2,18},{4,20},{6,22},{8,24},{10,26},{12,28},{14,30},{16,0},... | collective-permute-start | bytes 1032200 | tf_op jit(solution)/shard_map/ppermute | solution.py:27
  134.1 1.5 collective-permute-start.23
  136.8 8.9 %collective-permute-done.23.refs_2_.refs_5_ = bf16[256,512]{1,0:T(8,128)(2,1)S(1)} collective-permute-done((bf16[256,512]{1,0:T(8,128)(2,1)S(1)}, bf16[256,512]{1,0:T(8,128)(2,1)S(1)}, u32[]{:S(2)}, u32[]{:S(2)}) %collective-permute-start.23) | collective-permute-done | bytes 262176 | tf_op jit(solution)/shard_map/ppermute | solution.py:27
  146.6 2.5 %collective-permute-done.25.refs_1_ = bf16[672,256]{1,0:T(8,128)(2,1)S(1)} collective-permute-done((bf16[672,256]{1,0:T(8,128)(2,1)S(1)}, bf16[672,256]{1,0:T(8,128)(2,1)S(1)}, u32[]{:S(2)}, u32[]{:S(2)}) %collective-permute-start.25) | collective-permute-done | bytes 344096 | tf_op jit(solution)/shard_map/ppermute | solution.py:27
  153.5 1.6 shard_map.116
  155.1 1.5 shard_map.113
  156.6 1.6 %shard_map.117 = (bf16[256,1024]{1,0:T(8,128)(2,1)}, bf16[256,1024]{1,0:T(8,128)(2,1)}) custom-call(s32[11]{0:T(128)S(1)} %pad_add_fusion.info_ref.info, bf16[256,512]{1,0:T(8,128)(2,1)S(1)} %get-tuple-element.108.refs_4_.refs_0_, bf16[256,512]{1,0:T(8,128)(2,1)S(1)} %collective-permute-done.22.refs_1_.refs_4_, ...), custom_call_target="tpu_custom_call" | custom-call | bytes 2097152 | tf_op jit(solution)/shard_map/pallas_call | solution.py:187
  158.5 1.7 %shard_map.120 = f32[168,2048]{1,0:T(8,128)} custom-call(s32[11]{0:T(128)S(1)} %pad_add_fusion.info_ref.info, bf16[168,512]{1,0:T(8,128)(2,1)S(1)} %get-tuple-element.119.refs_0_, bf16[168,512]{1,0:T(8,128)(2,1)S(1)} %collective-permute-done.28.refs_1_, bf16[168,512]{1,0:T(8,128)(2,1)S(1)} %collective-permute-done.29.refs_2_, ...), custom_call_target="tpu_custom_call" | custom-call | bytes 2064384 | tf_op jit(solution)/shard_map/pallas_call | solution.py:187
  (71 shorter events, 27.1 us)
Async XLA Ops:
  3.0 19.6 %collective-permute-start.3 = (bf16[256,512]{1,0:T(8,128)(2,1)S(1)}, bf16[256,512]{1,0:T(8,128)(2,1)S(1)}, u32[]{:S(2)}, u32[]{:S(2)}) collective-permute-start(bf16[256,512]{1,0:T(8,128)(2,1)S(1)} %get-tuple-element.73), channel_id=1, source_target_pairs={{0,2},{2,0},{4,6},{6,4},{8,10},{10,8},{12,14},{14,12},{16,18},{18,... | collective-permute-start | bytes 786440 | tf_op jit(solution)/shard_map/ppermute | solution.py:27
  6.0 16.6 %collective-permute-start.4 = (bf16[256,512]{1,0:T(8,128)(2,1)S(1)}, bf16[256,512]{1,0:T(8,128)(2,1)S(1)}, u32[]{:S(2)}, u32[]{:S(2)}) collective-permute-start(bf16[256,512]{1,0:T(8,128)(2,1)S(1)} %get-tuple-element.74), channel_id=1, source_target_pairs={{0,4},{2,6},{4,0},{6,2},{8,12},{10,14},{12,8},{14,10},{16,20},{18,... | collective-permute-start | bytes 786440 | tf_op jit(solution)/shard_map/ppermute | solution.py:27
  7.5 15.1 %collective-permute-start.5 = (bf16[256,512]{1,0:T(8,128)(2,1)S(1)}, bf16[256,512]{1,0:T(8,128)(2,1)S(1)}, u32[]{:S(2)}, u32[]{:S(2)}) collective-permute-start(bf16[256,512]{1,0:T(8,128)(2,1)S(1)} %get-tuple-element.75), channel_id=1, source_target_pairs={{0,6},{2,4},{4,2},{6,0},{8,14},{10,12},{12,10},{14,8},{16,22},{18,... | collective-permute-start | bytes 786440 | tf_op jit(solution)/shard_map/ppermute | solution.py:27
  19.0 14.9 %collective-permute-start = (bf16[256,1024]{1,0:T(8,128)(2,1)S(1)}, bf16[256,1024]{1,0:T(8,128)(2,1)S(1)}, u32[]{:S(2)}, u32[]{:S(2)}) collective-permute-start(bf16[256,1024]{1,0:T(8,128)(2,1)S(1)} %get-tuple-element.69.refs_5_), channel_id=1, source_target_pairs={{0,2},{2,0},{4,6},{6,4},{8,10},{10,8},{12,14},{14,12},{16,18},{18,... | collective-permute-start | bytes 1572872 | tf_op jit(solution)/shard_map/ppermute | solution.py:27
  21.0 23.8 %collective-permute-start.1 = (bf16[256,1024]{1,0:T(8,128)(2,1)S(1)}, bf16[256,1024]{1,0:T(8,128)(2,1)S(1)}, u32[]{:S(2)}, u32[]{:S(2)}) collective-permute-start(bf16[256,1024]{1,0:T(8,128)(2,1)S(1)} %get-tuple-element.70.refs_6_), channel_id=1, source_target_pairs={{0,4},{2,6},{4,0},{6,2},{8,12},{10,14},{12,8},{14,10},{16,20},{18,... | collective-permute-start | bytes 1572872 | tf_op jit(solution)/shard_map/ppermute | solution.py:27
  22.5 22.3 %collective-permute-start.2 = (bf16[256,1024]{1,0:T(8,128)(2,1)S(1)}, bf16[256,1024]{1,0:T(8,128)(2,1)S(1)}, u32[]{:S(2)}, u32[]{:S(2)}) collective-permute-start(bf16[256,1024]{1,0:T(8,128)(2,1)S(1)} %get-tuple-element.71.refs_7_), channel_id=1, source_target_pairs={{0,6},{2,4},{4,2},{6,0},{8,14},{10,12},{12,10},{14,8},{16,22},{18,... | collective-permute-start | bytes 1572872 | tf_op jit(solution)/shard_map/ppermute | solution.py:27
  23.3 25.0 %collective-permute-start.7 = (bf16[4,256,256]{2,1,0:T(8,128)(2,1)S(1)}, bf16[4,256,256]{2,1,0:T(8,128)(2,1)S(1)}, u32[]{:S(2)}, u32[]{:S(2)}) collective-permute-start(bf16[4,256,256]{2,1,0:T(8,128)(2,1)S(1)} %get-tuple-element.77.refs_8_.refs_9_), channel_id=1, source_target_pairs={{0,8},{2,10},{4,12},{6,14},{8,16},{10,18},{12,20},{14,22},{16,24},... | collective-permute-start | bytes 1572872 | tf_op jit(solution)/shard_map/ppermute | solution.py:23
  27.9 34.7 %collective-permute-start.6 = (bf16[4,256,256]{2,1,0:T(8,128)(2,1)S(1)}, bf16[4,256,256]{2,1,0:T(8,128)(2,1)S(1)}, u32[]{:S(2)}, u32[]{:S(2)}) collective-permute-start(bf16[4,256,256]{2,1,0:T(8,128)(2,1)S(1)} %get-tuple-element.76.refs_8_.refs_9_), channel_id=1, source_target_pairs={{0,8},{2,10},{4,12},{6,14},{8,16},{10,18},{12,20},{14,22},{16,24},... | collective-permute-start | bytes 1572872 | tf_op jit(solution)/shard_map/ppermute | solution.py:23
  44.8 30.8 %collective-permute-start.13 = (bf16[128,2688]{1,0:T(8,128)(2,1)S(1)}, bf16[128,2688]{1,0:T(8,128)(2,1)S(1)}, u32[]{:S(2)}, u32[]{:S(2)}) collective-permute-start(bf16[128,2688]{1,0:T(8,128)(2,1)S(1)} %shard_map.107), channel_id=1, source_target_pairs={{0,6},{2,4},{4,2},{6,0},{8,14},{10,12},{12,10},{14,8},{16,22},{18,... | collective-permute-start | bytes 2064392 | tf_op jit(solution)/shard_map/ppermute | solution.py:27
  46.3 29.3 %collective-permute-start.12 = (bf16[128,2688]{1,0:T(8,128)(2,1)S(1)}, bf16[128,2688]{1,0:T(8,128)(2,1)S(1)}, u32[]{:S(2)}, u32[]{:S(2)}) collective-permute-start(bf16[128,2688]{1,0:T(8,128)(2,1)S(1)} %shard_map.107), channel_id=1, source_target_pairs={{0,4},{2,6},{4,0},{6,2},{8,12},{10,14},{12,8},{14,10},{16,20},{18,... | collective-permute-start | bytes 2064392 | tf_op jit(solution)/shard_map/ppermute | solution.py:27
  47.5 28.2 %collective-permute-start.11 = (bf16[128,2688]{1,0:T(8,128)(2,1)S(1)}, bf16[128,2688]{1,0:T(8,128)(2,1)S(1)}, u32[]{:S(2)}, u32[]{:S(2)}) collective-permute-start(bf16[128,2688]{1,0:T(8,128)(2,1)S(1)} %shard_map.107), channel_id=1, source_target_pairs={{0,2},{2,0},{4,6},{6,4},{8,10},{10,8},{12,14},{14,12},{16,18},{18,... | collective-permute-start | bytes 2064392 | tf_op jit(solution)/shard_map/ppermute | solution.py:27
  61.1 14.5 %collective-permute-start.14 = (bf16[2,4,256,128]{3,2,1,0:T(8,128)(2,1)S(1)}, bf16[2,4,256,128]{3,2,1,0:T(8,128)(2,1)S(1)}, u32[]{:S(2)}, u32[]{:S(2)}) collective-permute-start(bf16[2,4,256,128]{3,2,1,0:T(8,128)(2,1)S(1)} %get-tuple-element.93), channel_id=1, source_target_pairs={{8,0},{10,2},{12,4},{14,6},{16,8},{18,10},{20,12},{22,14},{24,16},... | collective-permute-start | bytes 1572872 | tf_op jit(solution)/shard_map/ppermute | solution.py:23
  75.6 30.0 %slice-start = ((s8[11010048]{0:T(1024)(128)(4,1)}), s8[4194304]{0:T(1024)(128)(4,1)S(1)}, s32[]{:S(2)}) async-start(s8[11010048]{0:T(1024)(128)(4,1)} %bitcast.5), calls=%async_computation | async-start | bytes 8388608
  76.3 4.2 %collective-permute-start.15 = (bf16[384,2688]{1,0:T(8,128)(2,1)S(1)}, bf16[384,2688]{1,0:T(8,128)(2,1)S(1)}, u32[]{:S(2)}, u32[]{:S(2)}) collective-permute-start(bf16[384,2688]{1,0:T(8,128)(2,1)S(1)} %shard_map.108.refs_1_), channel_id=1, source_target_pairs={{0,1},{1,0},{2,3},{3,2},{4,5},{5,4},{6,7},{7,6},{8,9},{9,8},{10,11... | collective-permute-start | bytes 6193160 | tf_op jit(solution)/shard_map/ppermute | solution.py:27
  76.4 17.6 %collective-permute-start.16 = (bf16[2,4,256,128]{3,2,1,0:T(8,128)(2,1)S(1)}, bf16[2,4,256,128]{3,2,1,0:T(8,128)(2,1)S(1)}, u32[]{:S(2)}, u32[]{:S(2)}) collective-permute-start(bf16[2,4,256,128]{3,2,1,0:T(8,128)(2,1)S(1)} %get-tuple-element.94), channel_id=1, source_target_pairs={{8,0},{10,2},{12,4},{14,6},{16,8},{18,10},{20,12},{22,14},{24,16},... | collective-permute-start | bytes 1572872 | tf_op jit(solution)/shard_map/ppermute | solution.py:23
  85.0 32.5 %collective-permute-start.21 = (bf16[2,672,256]{2,1,0:T(8,128)(2,1)S(1)}, bf16[2,672,256]{2,1,0:T(8,128)(2,1)S(1)}, u32[]{:S(2)}, u32[]{:S(2)}) collective-permute-start(bf16[2,672,256]{2,1,0:T(8,128)(2,1)S(1)} %get-tuple-element.106), channel_id=1, source_target_pairs={{0,8},{2,10},{4,12},{6,14},{8,0},{10,2},{12,4},{14,6},{16,24},{18,... | collective-permute-start | bytes 2064392 | tf_op jit(solution)/shard_map/ppermute | solution.py:27
  87.7 13.8 %collective-permute-start.8 = (bf16[256,512]{1,0:T(8,128)(2,1)S(1)}, bf16[256,512]{1,0:T(8,128)(2,1)S(1)}, u32[]{:S(2)}, u32[]{:S(2)}) collective-permute-start(bf16[256,512]{1,0:T(8,128)(2,1)S(1)} %get-tuple-element.87), channel_id=1, source_target_pairs={{0,2},{2,0},{4,6},{6,4},{8,10},{10,8},{12,14},{14,12},{16,18},{18,... | collective-permute-start | bytes 786440 | tf_op jit(solution)/shard_map/ppermute | solution.py:27
  89.0 13.8 %collective-permute-start.9 = (bf16[256,512]{1,0:T(8,128)(2,1)S(1)}, bf16[256,512]{1,0:T(8,128)(2,1)S(1)}, u32[]{:S(2)}, u32[]{:S(2)}) collective-permute-start(bf16[256,512]{1,0:T(8,128)(2,1)S(1)} %get-tuple-element.88), channel_id=1, source_target_pairs={{0,4},{2,6},{4,0},{6,2},{8,12},{10,14},{12,8},{14,10},{16,20},{18,... | collective-permute-start | bytes 786440 | tf_op jit(solution)/shard_map/ppermute | solution.py:27
  89.8 13.8 %collective-permute-start.10 = (bf16[256,512]{1,0:T(8,128)(2,1)S(1)}, bf16[256,512]{1,0:T(8,128)(2,1)S(1)}, u32[]{:S(2)}, u32[]{:S(2)}) collective-permute-start(bf16[256,512]{1,0:T(8,128)(2,1)S(1)} %get-tuple-element.89), channel_id=1, source_target_pairs={{0,6},{2,4},{4,2},{6,0},{8,14},{10,12},{12,10},{14,8},{16,22},{18,... | collective-permute-start | bytes 786440 | tf_op jit(solution)/shard_map/ppermute | solution.py:27
  98.6 32.7 %collective-permute-start.26 = (bf16[2,672,256]{2,1,0:T(8,128)(2,1)S(1)}, bf16[2,672,256]{2,1,0:T(8,128)(2,1)S(1)}, u32[]{:S(2)}, u32[]{:S(2)}) collective-permute-start(bf16[2,672,256]{2,1,0:T(8,128)(2,1)S(1)} %get-tuple-element.116), channel_id=1, source_target_pairs={{0,16},{2,18},{4,20},{6,22},{8,24},{10,26},{12,28},{14,30},{16,0},... | collective-permute-start | bytes 2064392 | tf_op jit(solution)/shard_map/ppermute | solution.py:27
  101.5 16.7 %collective-permute-start.18 = (bf16[256,512]{1,0:T(8,128)(2,1)S(1)}, bf16[256,512]{1,0:T(8,128)(2,1)S(1)}, u32[]{:S(2)}, u32[]{:S(2)}) collective-permute-start(bf16[256,512]{1,0:T(8,128)(2,1)S(1)} %get-tuple-element.100), channel_id=1, source_target_pairs={{0,2},{2,0},{4,6},{6,4},{8,10},{10,8},{12,14},{14,12},{16,18},{18,... | collective-permute-start | bytes 786440 | tf_op jit(solution)/shard_map/ppermute | solution.py:27
  102.8 15.5 %collective-permute-start.19 = (bf16[256,512]{1,0:T(8,128)(2,1)S(1)}, bf16[256,512]{1,0:T(8,128)(2,1)S(1)}, u32[]{:S(2)}, u32[]{:S(2)}) collective-permute-start(bf16[256,512]{1,0:T(8,128)(2,1)S(1)} %get-tuple-element.101), channel_id=1, source_target_pairs={{0,4},{2,6},{4,0},{6,2},{8,12},{10,14},{12,8},{14,10},{16,20},{18,... | collective-permute-start | bytes 786440 | tf_op jit(solution)/shard_map/ppermute | solution.py:27
  103.6 14.7 %collective-permute-start.20 = (bf16[256,512]{1,0:T(8,128)(2,1)S(1)}, bf16[256,512]{1,0:T(8,128)(2,1)S(1)}, u32[]{:S(2)}, u32[]{:S(2)}) collective-permute-start(bf16[256,512]{1,0:T(8,128)(2,1)S(1)} %get-tuple-element.102), channel_id=1, source_target_pairs={{0,6},{2,4},{4,2},{6,0},{8,14},{10,12},{12,10},{14,8},{16,22},{18,... | collective-permute-start | bytes 786440 | tf_op jit(solution)/shard_map/ppermute | solution.py:27
  119.0 16.6 %collective-permute-start.22 = (bf16[256,512]{1,0:T(8,128)(2,1)S(1)}, bf16[256,512]{1,0:T(8,128)(2,1)S(1)}, u32[]{:S(2)}, u32[]{:S(2)}) collective-permute-start(bf16[256,512]{1,0:T(8,128)(2,1)S(1)} %get-tuple-element.109.refs_5_), channel_id=1, source_target_pairs={{0,2},{2,0},{4,6},{6,4},{8,10},{10,8},{12,14},{14,12},{16,18},{18,... | collective-permute-start | bytes 786440 | tf_op jit(solution)/shard_map/ppermute | solution.py:27
  120.3 34.7 %collective-permute-start.17 = (bf16[1344,256]{1,0:T(8,128)(2,1)S(1)}, bf16[1344,256]{1,0:T(8,128)(2,1)S(1)}, u32[]{:S(2)}, u32[]{:S(2)}) collective-permute-start(bf16[1344,256]{1,0:T(8,128)(2,1)S(1)} %get-tuple-element.98.refs_3_), channel_id=1, source_target_pairs={{0,1},{1,0},{2,3},{3,2},{4,5},{5,4},{6,7},{7,6},{8,9},{9,8},{10,11... | collective-permute-start | bytes 2064392 | tf_op jit(solution)/shard_map/ppermute | solution.py:27
  132.0 14.7 %collective-permute-start.27 = (bf16[672,256]{1,0:T(8,128)(2,1)S(1)}, bf16[672,256]{1,0:T(8,128)(2,1)S(1)}, u32[]{:S(2)}, u32[]{:S(2)}) collective-permute-start(bf16[672,256]{1,0:T(8,128)(2,1)S(1)} %get-tuple-element.118), channel_id=1, source_target_pairs={{0,8},{2,10},{4,12},{6,14},{8,0},{10,2},{12,4},{14,6},{16,24},{18,... | collective-permute-start | bytes 1032200 | tf_op jit(solution)/shard_map/ppermute | solution.py:27
  132.0 17.1 %collective-permute-start.25 = (bf16[672,256]{1,0:T(8,128)(2,1)S(1)}, bf16[672,256]{1,0:T(8,128)(2,1)S(1)}, u32[]{:S(2)}, u32[]{:S(2)}) collective-permute-start(bf16[672,256]{1,0:T(8,128)(2,1)S(1)} %get-tuple-element.107.refs_7_.refs_3_), channel_id=1, source_target_pairs={{0,16},{2,18},{4,20},{6,22},{8,24},{10,26},{12,28},{14,30},{16,0},... | collective-permute-start | bytes 1032200 | tf_op jit(solution)/shard_map/ppermute | solution.py:27
  134.1 11.7 %collective-permute-start.23 = (bf16[256,512]{1,0:T(8,128)(2,1)S(1)}, bf16[256,512]{1,0:T(8,128)(2,1)S(1)}, u32[]{:S(2)}, u32[]{:S(2)}) collective-permute-start(bf16[256,512]{1,0:T(8,128)(2,1)S(1)} %get-tuple-element.110.refs_6_), channel_id=1, source_target_pairs={{0,4},{2,6},{4,0},{6,2},{8,12},{10,14},{12,8},{14,10},{16,20},{18,... | collective-permute-start | bytes 786440 | tf_op jit(solution)/shard_map/ppermute | solution.py:27
  135.6 10.1 %collective-permute-start.24 = (bf16[256,512]{1,0:T(8,128)(2,1)S(1)}, bf16[256,512]{1,0:T(8,128)(2,1)S(1)}, u32[]{:S(2)}, u32[]{:S(2)}) collective-permute-start(bf16[256,512]{1,0:T(8,128)(2,1)S(1)} %get-tuple-element.111.refs_7_), channel_id=1, source_target_pairs={{0,6},{2,4},{4,2},{6,0},{8,14},{10,12},{12,10},{14,8},{16,22},{18,... | collective-permute-start | bytes 786440 | tf_op jit(solution)/shard_map/ppermute | solution.py:27
  149.9 8.3 %collective-permute-start.28 = (bf16[168,512]{1,0:T(8,128)(2,1)S(1)}, bf16[168,512]{1,0:T(8,128)(2,1)S(1)}, u32[]{:S(2)}, u32[]{:S(2)}) collective-permute-start(bf16[168,512]{1,0:T(8,128)(2,1)S(1)} %get-tuple-element.120), channel_id=1, source_target_pairs={{0,2},{2,0},{4,6},{6,4},{8,10},{10,8},{12,14},{14,12},{16,18},{18,... | collective-permute-start | bytes 516104 | tf_op jit(solution)/shard_map/ppermute | solution.py:27
  151.2 7.2 %collective-permute-start.29 = (bf16[168,512]{1,0:T(8,128)(2,1)S(1)}, bf16[168,512]{1,0:T(8,128)(2,1)S(1)}, u32[]{:S(2)}, u32[]{:S(2)}) collective-permute-start(bf16[168,512]{1,0:T(8,128)(2,1)S(1)} %get-tuple-element.121), channel_id=1, source_target_pairs={{0,4},{2,6},{4,0},{6,2},{8,12},{10,14},{12,8},{14,10},{16,20},{18,... | collective-permute-start | bytes 516104 | tf_op jit(solution)/shard_map/ppermute | solution.py:27
  152.0 6.4 %collective-permute-start.30 = (bf16[168,512]{1,0:T(8,128)(2,1)S(1)}, bf16[168,512]{1,0:T(8,128)(2,1)S(1)}, u32[]{:S(2)}, u32[]{:S(2)}) collective-permute-start(bf16[168,512]{1,0:T(8,128)(2,1)S(1)} %get-tuple-element.122), channel_id=1, source_target_pairs={{0,6},{2,4},{4,2},{6,0},{8,14},{10,12},{12,10},{14,8},{16,22},{18,... | collective-permute-start | bytes 516104 | tf_op jit(solution)/shard_map/ppermute | solution.py:27
  (8 other events, 61.2 us)
